TPU v7x, 128 devices: a whole 4x4x4 slice. The times are simulated.
128 devices in a mesh: lat: 16 (over x, y), wave: 8 (over z, core).
Axes of the slice: x: 4, y: 4, z: 4, core: 2. Of those that a mesh axis runs over, the one named last changes fastest.
Arguments:
- fields: bfloat16 [24, 128, 5120], P(None, 'lat', 'wave'), may hold values from -6 to 6
- row_length: int32 [128], P('lat'), may hold values from 2560 to 5120, as said below
- wave_order: int32 [1280], replicated, may hold values from 0 to 1279, each once
- depart_row: int32 [128, 5120], P('lat', 'wave'), may hold values from -7 to 6
- depart_col: int32 [128, 5120], P('lat', 'wave'), may hold values from -7 to 6
- frac_row: float32 [128, 5120], P('lat', 'wave'), may hold values from 0 to 1
- frac_col: float32 [128, 5120], P('lat', 'wave'), may hold values from 0 to 1
- legendre: bfloat16 [1280, 128, 1280], P(('lat', 'wave')), may hold values from -0.5 to 0.5
Outputs:
- spectral: float32 [1280, 48, 1280], P(('lat', 'wave'))
Inputs may be any that keep to these rules, and one draw needn't show every extreme that they name: `row_length`: every row length lies between 2560 and 5120; at least one row has 5120 points. `wave_order`: each wavenumber stands in exactly one slot.
All inputs are finite; a program needn't handle non-finite values.
Results may differ from a plain program's by a relative error of at most 0.009.
Values may be sent and summed in bfloat16 or wider, within the bound.
No kernel may reach another device: no remote copies, remote signals or barrier semaphores. Data moves between devices by JAX's collectives and lax.ppermute only.
A program may use at most 128 MiB of HBM per device.

v0:
```python
import math

import jax
import jax.numpy as jnp
from jax import lax
from jax.experimental import pallas as pl
from jax.experimental.pallas import tpu as pltpu
from jax.sharding import PartitionSpec as P

F32 = jnp.float32
BF16 = jnp.bfloat16
VMEM = pl.BlockSpec(memory_space=pltpu.VMEM)
SMEM = pl.BlockSpec(memory_space=pltpu.SMEM)
LIMIT = 48 * 1024 * 1024

SLICES = 24
BAND = 8
WIDE = 640
BLOCKS = 5
SLOTS = 10
DEVICES = 128
ROWS = 4
STACK = 128


def cubic_weights(fraction):
    return (
        -fraction * (fraction - 1.0) * (fraction - 2.0) / 6.0,
        (fraction + 1.0) * (fraction - 1.0) * (fraction - 2.0) / 2.0,
        -(fraction + 1.0) * fraction * (fraction - 2.0) / 2.0,
        (fraction + 1.0) * fraction * (fraction - 1.0) / 6.0,
    )


def picked_weight(distance, weights):
    chosen = jnp.where(distance == 3, weights[3], 0.0)
    for step in (2, 1, 0):
        chosen = jnp.where(distance == step, weights[step], chosen)
    return chosen


def interpolate_kernel(
    place, live, own, above, below, depart_row, depart_col, frac_row, frac_col, keep, send,
    main, edge, columns, row_table, points, stack,
):
    lane = lax.broadcasted_iota(jnp.int32, (1, WIDE), 1) % 128
    for base, first, fraction in (
        (0, depart_col[...] + lane - 1, frac_col),
        (8, depart_row[...] + (BAND - 1), frac_row),
    ):
        for step, value in enumerate((first.astype(F32),) + cubic_weights(fraction[...])):
            for row in range(BAND):
                points[row, base + step : base + step + 1, :] = value[row : row + 1, :]
    count = BAND * SLICES
    for part, ref in enumerate((above, own, below)):
        rows = pl.ds(part * count, count)
        main[rows, :] = ref[:, :WIDE]
        for block in range(BLOCKS):
            right = block + 1
            left = block - 1 if block else BLOCKS
            edge[rows, 128 * block : 128 * block + 128] = jnp.concatenate(
                [ref[:, 128 * right : 128 * right + 64], ref[:, 128 * left + 64 : 128 * left + 128]],
                axis=1,
            )
    columns[...] = jnp.zeros_like(columns)
    stack[...] = jnp.zeros_like(stack)
    core = place[0]

    def one_pair(step, carry):
        pair = step ^ (2 * core)
        window = pl.ds(pl.multiple_of(pair * (2 * SLICES), 2 * SLICES), 18 * SLICES)

        def row_of(item, block):
            return jnp.concatenate(
                [
                    points[2 * pair + half, item : item + 1, 128 * block : 128 * block + 128]
                    for half in range(2)
                ],
                axis=1,
            )

        for block in range(BLOCKS):
            start = row_of(0, block)
            weights = [row_of(1 + k, block) for k in range(4)]
            source = lax.broadcasted_iota(jnp.int32, (144, 256), 0).astype(F32)
            columns[0:144, :] = picked_weight(source - start, weights).astype(BF16)
            source = lax.broadcasted_iota(jnp.int32, (16, 256), 0).astype(F32) - 16.0
            columns[240:256, :] = picked_weight(source - start, weights).astype(BF16)
            half = (lax.broadcasted_iota(jnp.int32, (1, 256), 1) >= 128).astype(F32)
            start = row_of(8, block) + half
            weights = [row_of(9 + k, block) for k in range(4)]
            source = lax.broadcasted_iota(jnp.int32, (24, 256), 0).astype(F32)
            row_table[...] = picked_weight(source - start, weights)
            lanes = slice(128 * block, 128 * block + 128)
            left = jnp.concatenate([main[window, lanes], edge[window, lanes]], axis=1)
            spread = jnp.dot(left, columns[...], preferred_element_type=F32)
            for half in range(2):
                side = slice(128 * half, 128 * half + 128)
                total = jnp.zeros((SLICES, 128), F32)
                for row in range(half, half + 17):
                    total = total + row_table[row : row + 1, side] * spread[
                        SLICES * row : SLICES * row + SLICES, side
                    ]
                position = lax.broadcasted_iota(jnp.int32, (SLICES, 128), 1) + 128 * block
                total = jnp.where(position < live[2 * pair + half], total, 0.0)
                stack[2 * step + half, SLICES * block : SLICES * block + SLICES, :] = total
        return carry

    lax.fori_loop(0, BAND // 2, one_pair, 0)
    keep[...] = stack[0:ROWS].astype(BF16)
    send[...] = stack[ROWS:].astype(BF16)


def turn(count, length, inverse):
    whole = jnp.floor(count * inverse + 0.5)
    angle = (count - whole * length) * (inverse * math.pi)
    square = angle * angle
    sine = angle * (
        1.0
        + square
        * (
            -1.0 / 6
            + square
            * (1.0 / 120 + square * (-1.0 / 5040 + square * (1.0 / 362880 - square / 39916800)))
        )
    )
    cosine = 1.0 + square * (
        -0.5
        + square
        * (
            1.0 / 24
            + square
            * (-1.0 / 720 + square * (1.0 / 40320 + square * (-1.0 / 3628800 + square / 479001600)))
        )
    )
    return 1.0 - 2.0 * sine * sine, 2.0 * sine * cosine


def twiddle_kernel(place, lengths, waves, inner, outer):
    wave_place = place[1]
    step = lax.broadcasted_iota(jnp.int32, (16, 128), 0)
    tile = jnp.where(step < 8, wave_place, wave_place ^ 1)
    offset = (tile * WIDE + (step % 8) * 128).astype(F32)
    coarse = (8 * step).astype(F32)
    fine = lax.broadcasted_iota(jnp.int32, (8, 128), 0).astype(F32)

    def one(index, carry):
        row = index // SLOTS
        slot = index % SLOTS
        length = jnp.full((1, 128), lengths[row], jnp.int32).astype(F32)
        inverse = 1.0 / length
        wave = waves[pl.ds(slot, 1), :]
        lanes = pl.ds(pl.multiple_of(slot * 256, 256), 128)
        lanes_two = pl.ds(pl.multiple_of(slot * 256 + 128, 128), 128)
        cosine, sine = turn(offset * wave, length, inverse)
        norm = lax.rsqrt(length)
        outer[row, :, lanes] = cosine * norm
        outer[row, :, lanes_two] = sine * norm
        cos_one, sin_one = turn(coarse * wave, length, inverse)
        cos_two, sin_two = turn(fine * wave, length, inverse)
        for pair in range(8):
            real = []
            imag = []
            for part in (2 * pair, 2 * pair + 1):
                c, s = cos_one[part : part + 1], sin_one[part : part + 1]
                real.append(c * cos_two - s * sin_two)
                imag.append(s * cos_two + c * sin_two)
            rows = slice(16 * pair, 16 * pair + 16)
            inner[row, rows, lanes] = jnp.concatenate(real, axis=0).astype(BF16)
            inner[row, rows, lanes_two] = jnp.concatenate(imag, axis=0).astype(BF16)
        return carry

    lax.fori_loop(0, ROWS * SLOTS, one, 0)


def fourier_kernel(mine, other, inner, outer, message, sums, shuffled):
    sums[...] = jnp.zeros_like(sums)

    def one(index, carry):
        row = index // SLOTS
        slot = index % SLOTS
        lanes = pl.ds(pl.multiple_of(slot * 256, 256), 256)
        table = inner[row, :, lanes]
        factors = outer[row, :, lanes]
        left = jnp.concatenate([mine[row], other[row]], axis=0)
        parts = jnp.dot(left, table, preferred_element_type=F32)
        real = jnp.zeros((SLICES, 128), F32)
        imag = jnp.zeros((SLICES, 128), F32)
        for side in range(2):
            for block in range(BLOCKS):
                first = STACK * side + SLICES * block
                cosine = parts[first : first + SLICES, :128]
                sine = parts[first : first + SLICES, 128:]
                at = 8 * side + block
                c, s = factors[at : at + 1, :128], factors[at : at + 1, 128:]
                real = real + (c * cosine - s * sine)
                imag = imag - (s * cosine + c * sine)
        base = row * 512 + slot * 48
        sums[pl.ds(base, SLICES, stride=2), :] = real
        sums[pl.ds(base + 1, SLICES, stride=2), :] = imag
        return carry

    lax.fori_loop(0, ROWS * SLOTS, one, 0)
    for part in range(16):
        shuffled[pl.ds(part, DEVICES, stride=16), :] = sums[128 * part : 128 * part + 128, :].T
    message[...] = shuffled[...].astype(BF16)


def legendre_kernel(waves, message, table, out, flat, sorted_rows, left):
    step = pl.program_id(0)

    @pl.when(step == 0)
    def _():
        for band in range(16):
            for core in range(2):
                total = message[8 * band + core].astype(F32)
                for z in range(1, 4):
                    total = total + message[8 * band + 2 * z + core].astype(F32)
                first = (2 * band + core) * 16
                flat[first : first + 16, :] = total
        for row in range(ROWS):
            for part in range(4):
                sorted_rows[pl.ds(128 * part + row, 32, stride=4), :] = flat[
                    pl.ds(4 * row + part, 32, stride=16), :
                ]
        for part in range(4):
            rows = slice(128 * part, 128 * part + 128)
            left[rows, :] = sorted_rows[rows, :].T.astype(BF16)

    rows = pl.ds(pl.multiple_of(step * 48, 16), 48)
    product = jnp.dot(left[rows, :], table[0], preferred_element_type=F32)
    degree = lax.broadcasted_iota(jnp.int32, product.shape, 1)
    out[0] = jnp.where(degree >= waves[step], product, 0.0)


def local(fields, row_length, wave_order, depart_row, depart_col, frac_row, frac_col, legendre):
    wave_place = lax.axis_index("wave")
    lat_place = lax.axis_index("lat")
    core = wave_place % 2
    column_start = wave_place * WIDE
    live = row_length - column_start
    live_mask = jnp.arange(WIDE, dtype=jnp.int32)[None, :] < live[:, None]
    masked = jnp.where(live_mask[None], fields, jnp.zeros_like(fields))
    own = masked.transpose(1, 0, 2).reshape(BAND * SLICES, WIDE)
    place = jnp.stack([core, wave_place]).astype(jnp.int32)

    ring = lax.axis_size("wave")
    from_left = lax.ppermute(
        own[:, WIDE - 128 :], "wave", [(i, (i + 1) % ring) for i in range(ring)]
    )
    from_right = lax.ppermute(own[:, :128], "wave", [((i + 1) % ring, i) for i in range(ring)])
    rim = jnp.concatenate([from_right[:, :64], from_left[:, 64:]], axis=1)
    own = jnp.concatenate([own, rim], axis=1)
    bands = lax.axis_size("lat")
    above = lax.ppermute(own, "lat", [(i, i + 1) for i in range(bands - 1)])
    below = lax.ppermute(own, "lat", [(i + 1, i) for i in range(bands - 1)])

    lengths = lax.dynamic_slice_in_dim(row_length, core * ROWS, ROWS)
    ordered = wave_order.reshape(DEVICES, SLOTS).T.astype(F32)
    inner, outer = pl.pallas_call(
        twiddle_kernel,
        out_shape=(
            jax.ShapeDtypeStruct((ROWS, 128, SLOTS * 256), BF16),
            jax.ShapeDtypeStruct((ROWS, 16, SLOTS * 256), F32),
        ),
        in_specs=[SMEM, SMEM, VMEM],
        out_specs=(VMEM, VMEM),
        compiler_params=pltpu.CompilerParams(vmem_limit_bytes=LIMIT),
        cost_estimate=pl.CostEstimate(flops=20_000_000, bytes_accessed=3_000_000, transcendentals=0),
        name="twiddle",
    )(place, lengths, ordered)

    keep, send = pl.pallas_call(
        interpolate_kernel,
        out_shape=(jax.ShapeDtypeStruct((ROWS, STACK, 128), BF16),) * 2,
        in_specs=[SMEM, SMEM] + [VMEM] * 7,
        out_specs=(VMEM, VMEM),
        scratch_shapes=[
            pltpu.VMEM((3 * BAND * SLICES, WIDE), BF16),
            pltpu.VMEM((3 * BAND * SLICES, WIDE), BF16),
            pltpu.VMEM((256, 256), BF16),
            pltpu.VMEM((24, 256), F32),
            pltpu.VMEM((BAND, 16, WIDE), F32),
            pltpu.VMEM((BAND, STACK, 128), F32),
        ],
        compiler_params=pltpu.CompilerParams(vmem_limit_bytes=LIMIT),
        name="interpolate",
    )(place, live, own, above, below, depart_row, depart_col, frac_row, frac_col)

    other = lax.ppermute(send, "wave", [(i, i ^ 1) for i in range(ring)])
    message = pl.pallas_call(
        fourier_kernel,
        out_shape=jax.ShapeDtypeStruct((DEVICES * 16, 128), BF16),
        in_specs=[VMEM] * 4,
        out_specs=VMEM,
        scratch_shapes=[
            pltpu.VMEM((ROWS * 512, 128), F32),
            pltpu.VMEM((DEVICES * 16, 128), F32),
        ],
        compiler_params=pltpu.CompilerParams(vmem_limit_bytes=LIMIT),
        name="fourier",
    )(keep, other, inner, outer)
    message = lax.all_to_all(
        message.reshape(DEVICES, 16, 128), ("lat", "wave"), split_axis=0, concat_axis=0, tiled=True
    )
    owner = lat_place * ring + wave_place
    own_waves = lax.dynamic_slice_in_dim(wave_order, owner * SLOTS, SLOTS)
    degrees = legendre.shape[2]
    return pl.pallas_call(
        legendre_kernel,
        grid=(SLOTS,),
        out_shape=jax.ShapeDtypeStruct((SLOTS, 2 * SLICES, degrees), F32),
        in_specs=[
            SMEM,
            pl.BlockSpec((DEVICES, 16, 128), lambda s: (0, 0, 0)),
            pl.BlockSpec((1, 128, degrees), lambda s: (s, 0, 0)),
        ],
        out_specs=pl.BlockSpec((1, 2 * SLICES, degrees), lambda s: (s, 0, 0)),
        scratch_shapes=[
            pltpu.VMEM((512, 128), F32),
            pltpu.VMEM((512, 128), F32),
            pltpu.VMEM((512, 128), BF16),
        ],
        compiler_params=pltpu.CompilerParams(vmem_limit_bytes=LIMIT),
        name="legendre",
    )(own_waves, message, legendre)


def solution(mesh):
    placed = (
        P(None, "lat", "wave"),
        P("lat"),
        P(),
        P("lat", "wave"),
        P("lat", "wave"),
        P("lat", "wave"),
        P("lat", "wave"),
        P(("lat", "wave"), None, None),
    )
    return jax.shard_map(
        local, mesh=mesh, in_specs=placed, out_specs=P(("lat", "wave"), None, None), check_vma=False
    )
```

profile of v0, /device:TPU:1, one launch (start us, length us, event | category | flops | bytes accessed | tf_op | source)
XLA Modules:
  0.0 72.6 jit_solution(11280912411282755096)
XLA Ops:
  0.0 0.7 %broadcast_subtract_fusion.live = s32[8]{0:T(128)S(1)} fusion(s32[8]{0:T(128)} %param.9, s32[]{:T(128)S(6)} %mul.14), kind=kLoop, calls=%fused_computation.4 | loop fusion | flops 8 | bytes 68 | tf_op jit(solution)/shard_map/sub | solution.py:241
  0.8 1.0 %select_bitcast_fusion = bf16[8,24,640]{2,0,1:T(8,128)(2,1)S(1)} fusion(bf16[24,8,640]{2,1,0:T(8,128)(2,1)} %param.8, pred[8,640]{1,0:T(8,128)(4,1)S(1)} %iota_compare_fusion), kind=kLoop, calls=%fused_computation.1 | loop fusion | flops 122880 | bytes 496640 | tf_op jit(solution)/shard_map/transpose | solution.py:244
  1.8 3.0 %collective-permute-start.1 = (bf16[192,128]{1,0:T(8,128)(2,1)S(1)}, bf16[192,128]{1,0:T(8,128)(2,1)S(1)}, u32[]{:S(2)}, u32[]{:S(2)}) collective-permute-start(bf16[192,128]{1,0:T(8,128)(2,1)S(1)} %get-tuple-element.14), channel_id=1, source_target_pairs={{0,1},{1,2},{2,3},{3,4},{4,5},{5,6},{6,7},{7,0},{8,9},{9,10},{10,1... | collective-permute-start | bytes 147464 | tf_op jit(solution)/shard_map/ppermute | solution.py:248
  4.9 1.2 %collective-permute-done.1 = bf16[192,128]{1,0:T(8,128)(2,1)S(1)} collective-permute-done((bf16[192,128]{1,0:T(8,128)(2,1)S(1)}, bf16[192,128]{1,0:T(8,128)(2,1)S(1)}, u32[]{:S(2)}, u32[]{:S(2)}) %collective-permute-start.1) | collective-permute-done | bytes 49184 | tf_op jit(solution)/shard_map/ppermute | solution.py:248
  6.1 2.3 %collective-permute-done = bf16[192,128]{1,0:T(8,128)(2,1)S(1)} collective-permute-done((bf16[192,128]{1,0:T(8,128)(2,1)S(1)}, bf16[192,128]{1,0:T(8,128)(2,1)S(1)}, u32[]{:S(2)}, u32[]{:S(2)}) %collective-permute-start) | collective-permute-done | bytes 49184 | tf_op jit(solution)/shard_map/ppermute | solution.py:251
  8.4 0.1 pad_maximum_fusion.own
  8.5 1.3 %collective-permute-start.3 = (bf16[192,768]{1,0:T(8,128)(2,1)S(1)}, bf16[192,768]{1,0:T(8,128)(2,1)S(1)}, u32[]{:S(2)}, u32[]{:S(2)}) collective-permute-start(bf16[192,768]{1,0:T(8,128)(2,1)S(1)} %pad_maximum_fusion.own), channel_id=1, source_target_pairs={{8,0},{16,8},{24,16},{32,24},{40,32},{48,40},{56,48},{64,56},{72,6... | collective-permute-start | bytes 884744 | tf_op jit(solution)/shard_map/ppermute | solution.py:256
  9.8 4.0 %collective-permute-start.2 = (bf16[192,768]{1,0:T(8,128)(2,1)S(1)}, bf16[192,768]{1,0:T(8,128)(2,1)S(1)}, u32[]{:S(2)}, u32[]{:S(2)}) collective-permute-start(bf16[192,768]{1,0:T(8,128)(2,1)S(1)} %pad_maximum_fusion.own), channel_id=1, source_target_pairs={{0,8},{8,16},{16,24},{24,32},{32,40},{40,48},{48,56},{56,64},{64,7... | collective-permute-start | bytes 884744 | tf_op jit(solution)/shard_map/ppermute | solution.py:255
  13.9 4.8 %collective-permute-done.3.below = bf16[192,768]{1,0:T(8,128)(2,1)S(1)} collective-permute-done((bf16[192,768]{1,0:T(8,128)(2,1)S(1)}, bf16[192,768]{1,0:T(8,128)(2,1)S(1)}, u32[]{:S(2)}, u32[]{:S(2)}) %collective-permute-start.3) | collective-permute-done | bytes 294944 | tf_op jit(solution)/shard_map/ppermute | solution.py:256
  18.7 0.9 %collective-permute-done.2.above = bf16[192,768]{1,0:T(8,128)(2,1)S(1)} collective-permute-done((bf16[192,768]{1,0:T(8,128)(2,1)S(1)}, bf16[192,768]{1,0:T(8,128)(2,1)S(1)}, u32[]{:S(2)}, u32[]{:S(2)}) %collective-permute-start.2) | collective-permute-done | bytes 294944 | tf_op jit(solution)/shard_map/ppermute | solution.py:255
  19.5 0.7 copy-done.2
  20.3 0.7 copy-done.3
  21.0 0.7 copy-done.4
  21.7 0.7 copy-done.5
  22.4 4.1 %interpolate.1 = (bf16[4,128,128]{2,1,0:T(8,128)(2,1)S(1)}, bf16[4,128,128]{2,1,0:T(8,128)(2,1)}) custom-call(s32[2]{0:T(128)S(1)} %pad_add_fusion.place, s32[8]{0:T(128)S(1)} %broadcast_subtract_fusion.live, bf16[192,768]{1,0:T(8,128)(2,1)S(1)} %pad_maximum_fusion.own, bf16[192,768]{1,0:T(8,128)(2,1)S(1)} %collective-permute-done.2.above, ...), custom_call_target="tpu_custom_call" | custom-call | tf_op jit(solution)/shard_map/interpolate/pallas_call | solution.py:273
  26.5 1.5 %collective-permute-start.4 = (bf16[4,128,128]{2,1,0:T(8,128)(2,1)}, bf16[4,128,128]{2,1,0:T(8,128)(2,1)S(1)}, u32[]{:S(2)}, u32[]{:S(2)}) collective-permute-start(bf16[4,128,128]{2,1,0:T(8,128)(2,1)} %get-tuple-element.10), channel_id=1, source_target_pairs={{0,1},{1,0},{2,3},{3,2},{4,5},{5,4},{6,7},{7,6},{8,9},{9,8},{10,11... | collective-permute-start | bytes 393224 | tf_op jit(solution)/shard_map/ppermute | solution.py:290
  28.0 0.1 convert_element_type.8
  28.2 3.6 %twiddle.1 = (bf16[4,128,2560]{2,1,0:T(8,128)(2,1)S(1)}, f32[4,16,2560]{2,1,0:T(8,128)S(1)}) custom-call(s32[2]{0:T(128)S(1)} %pad_add_fusion.place, s32[4]{0:T(128)S(1)} %dynamic_slice.7.lengths, f32[10,128]{1,0:T(8,128)S(1)} %bitcast.9), custom_call_target="tpu_custom_call" | custom-call | flops 20000000 | bytes 3000000 | tf_op jit(solution)/shard_map/twiddle/pallas_call | solution.py:260
  31.8 8.1 %fourier.1 = bf16[2048,128]{1,0:T(8,128)(2,1)S(1)} custom-call(bf16[4,128,128]{2,1,0:T(8,128)(2,1)S(1)} %get-tuple-element.9.mine, bf16[4,128,128]{2,1,0:T(8,128)(2,1)S(1)} %collective-permute-done.4.other, bf16[4,128,2560]{2,1,0:T(8,128)(2,1)S(1)} %get-tuple-element.11.inner, f32[4,16,2560]{2,1,0:T(8,128)S(1)} %get-tuple-element.12.outer), custom_call_target="tpu_custom_call" | custom-call | tf_op jit(solution)/shard_map/fourier/pallas_call | solution.py:291
  40.0 0.8 %copy-done.1 = bf16[2048,128]{1,0:T(8,128)(2,1)} copy-done((bf16[2048,128]{1,0:T(8,128)(2,1)}, bf16[2048,128]{1,0:T(8,128)(2,1)S(1)}, u32[]{:S(2)}) %copy-start.1) | copy-done | bytes 524312
  40.8 12.6 %all-to-all-start = ((bf16[128,16,128]{2,1,0:T(8,128)(2,1)}), bf16[128,16,128]{2,1,0:T(8,128)(2,1)}, u32[]{:S(2)}, u32[]{:S(2)}) async-start(bf16[128,16,128]{2,1,0:T(8,128)(2,1)} %bitcast.8), calls=%async_computation | async-start | bytes 1048576 | tf_op jit(solution)/shard_map/all_to_all | solution.py:303
  53.3 0.8 %dynamic_slice.6.waves = s32[10]{0:T(128)S(1)} dynamic-slice(s32[1280]{0:T(1024)} %param.10, s32[]{:T(128)S(6)} %select_n.17), dynamic_slice_sizes={10} | dynamic-slice | bytes 84 | tf_op jit(solution)/shard_map/dynamic_slice | solution.py:307
  54.1 12.5 %all-to-all-done.message = bf16[128,16,128]{2,1,0:T(8,128)(2,1)} async-done(((bf16[128,16,128]{2,1,0:T(8,128)(2,1)}), bf16[128,16,128]{2,1,0:T(8,128)(2,1)}, u32[]{:S(2)}, u32[]{:S(2)}) %all-to-all-start) | async-done | bytes 524320 | tf_op jit(solution)/shard_map/all_to_all | solution.py:303
  66.7 5.9 %legendre.1 = f32[10,48,1280]{2,1,0:T(8,128)} custom-call(s32[10]{0:T(128)S(1)} %dynamic_slice.6.waves, bf16[128,16,128]{2,1,0:T(8,128)(2,1)} %all-to-all-done.message, bf16[10,128,1280]{2,1,0:T(8,128)(2,1)S(1)} %copy-done), custom_call_target="tpu_custom_call" | custom-call | tf_op jit(solution)/shard_map/legendre/pallas_call | solution.py:309
  (21 shorter events, 0.4 us)
Async XLA Ops:
  0.0 28.0 %copy-start.7 = (s32[8]{0:T(128)S(1)}, s32[8]{0:T(128)}, u32[]{:S(2)}) copy-start(s32[8]{0:T(128)} %param.9) | copy-start | bytes 100
  0.0 28.0 %copy-start.6 = (s32[1280]{0:T(1024)S(1)}, s32[1280]{0:T(1024)}, u32[]{:S(2)}) copy-start(s32[1280]{0:T(1024)} %param.10) | copy-start | bytes 15364
  1.8 4.2 %collective-permute-start.1 = (bf16[192,128]{1,0:T(8,128)(2,1)S(1)}, bf16[192,128]{1,0:T(8,128)(2,1)S(1)}, u32[]{:S(2)}, u32[]{:S(2)}) collective-permute-start(bf16[192,128]{1,0:T(8,128)(2,1)S(1)} %get-tuple-element.14), channel_id=1, source_target_pairs={{0,1},{1,2},{2,3},{3,4},{4,5},{5,6},{6,7},{7,0},{8,9},{9,10},{10,1... | collective-permute-start | bytes 147464 | tf_op jit(solution)/shard_map/ppermute | solution.py:248
  4.9 3.5 %collective-permute-start = (bf16[192,128]{1,0:T(8,128)(2,1)S(1)}, bf16[192,128]{1,0:T(8,128)(2,1)S(1)}, u32[]{:S(2)}, u32[]{:S(2)}) collective-permute-start(bf16[192,128]{1,0:T(8,128)(2,1)S(1)} %get-tuple-element.13), channel_id=1, source_target_pairs={{1,0},{2,1},{3,2},{4,3},{5,4},{6,5},{7,6},{0,7},{9,8},{10,9},{11,1... | collective-permute-start | bytes 147464 | tf_op jit(solution)/shard_map/ppermute | solution.py:251
  8.5 10.2 %collective-permute-start.3 = (bf16[192,768]{1,0:T(8,128)(2,1)S(1)}, bf16[192,768]{1,0:T(8,128)(2,1)S(1)}, u32[]{:S(2)}, u32[]{:S(2)}) collective-permute-start(bf16[192,768]{1,0:T(8,128)(2,1)S(1)} %pad_maximum_fusion.own), channel_id=1, source_target_pairs={{8,0},{16,8},{24,16},{32,24},{40,32},{48,40},{56,48},{64,56},{72,6... | collective-permute-start | bytes 884744 | tf_op jit(solution)/shard_map/ppermute | solution.py:256
  9.8 9.7 %collective-permute-start.2 = (bf16[192,768]{1,0:T(8,128)(2,1)S(1)}, bf16[192,768]{1,0:T(8,128)(2,1)S(1)}, u32[]{:S(2)}, u32[]{:S(2)}) collective-permute-start(bf16[192,768]{1,0:T(8,128)(2,1)S(1)} %pad_maximum_fusion.own), channel_id=1, source_target_pairs={{0,8},{8,16},{16,24},{24,32},{32,40},{40,48},{48,56},{56,64},{64,7... | collective-permute-start | bytes 884744 | tf_op jit(solution)/shard_map/ppermute | solution.py:255
  19.5 0.7 %copy-start.2 = (s32[8,640]{1,0:T(8,128)S(1)}, s32[8,640]{1,0:T(8,128)}, u32[]{:S(2)}) copy-start(s32[8,640]{1,0:T(8,128)} %depart_row.1) | copy-start | bytes 61444
  20.3 0.7 %copy-start.3 = (s32[8,640]{1,0:T(8,128)S(1)}, s32[8,640]{1,0:T(8,128)}, u32[]{:S(2)}) copy-start(s32[8,640]{1,0:T(8,128)} %depart_col.1) | copy-start | bytes 61444
  21.0 0.7 %copy-start.4 = (f32[8,640]{1,0:T(8,128)S(1)}, f32[8,640]{1,0:T(8,128)}, u32[]{:S(2)}) copy-start(f32[8,640]{1,0:T(8,128)} %frac_row.1) | copy-start | bytes 61444
  21.7 0.7 %copy-start.5 = (f32[8,640]{1,0:T(8,128)S(1)}, f32[8,640]{1,0:T(8,128)}, u32[]{:S(2)}) copy-start(f32[8,640]{1,0:T(8,128)} %frac_col.1) | copy-start | bytes 61444
  26.5 5.3 %collective-permute-start.4 = (bf16[4,128,128]{2,1,0:T(8,128)(2,1)}, bf16[4,128,128]{2,1,0:T(8,128)(2,1)S(1)}, u32[]{:S(2)}, u32[]{:S(2)}) collective-permute-start(bf16[4,128,128]{2,1,0:T(8,128)(2,1)} %get-tuple-element.10), channel_id=1, source_target_pairs={{0,1},{1,0},{2,3},{3,2},{4,5},{5,4},{6,7},{7,6},{8,9},{9,8},{10,11... | collective-permute-start | bytes 393224 | tf_op jit(solution)/shard_map/ppermute | solution.py:290
  28.2 38.4 %copy-start = (bf16[10,128,1280]{2,1,0:T(8,128)(2,1)S(1)}, bf16[10,128,1280]{2,1,0:T(8,128)(2,1)}, u32[]{:S(2)}) copy-start(bf16[10,128,1280]{2,1,0:T(8,128)(2,1)} %table.1) | copy-start | bytes 9830404
  40.0 0.8 %copy-start.1 = (bf16[2048,128]{1,0:T(8,128)(2,1)}, bf16[2048,128]{1,0:T(8,128)(2,1)S(1)}, u32[]{:S(2)}) copy-start(bf16[2048,128]{1,0:T(8,128)(2,1)S(1)} %fourier.1) | copy-start | bytes 1572868
  40.8 25.9 %all-to-all-start = ((bf16[128,16,128]{2,1,0:T(8,128)(2,1)}), bf16[128,16,128]{2,1,0:T(8,128)(2,1)}, u32[]{:S(2)}, u32[]{:S(2)}) async-start(bf16[128,16,128]{2,1,0:T(8,128)(2,1)} %bitcast.8), calls=%async_computation | async-start | bytes 1048576 | tf_op jit(solution)/shard_map/all_to_all | solution.py:303
where the time goes:
time: 73.2 us; the launch traced here: 72.6 us
  starting transfers between devices  22.4 us (31%)
  Pallas kernels  21.7 us (30%)
  waiting for transfers between devices  21.6 us (30%)
  local copies, waits for them, and re-layouts  4.87 us (7%)
  other arithmetic  1.94 us (3%)
    all_to_all x1, starting transfers between devices, local(): lax.all_to_all(message.reshape(DEVICES, 16, 128), ('lat', 'wave'), split_...  12.6 us
    all_to_all x1, waiting for transfers between devices, local(): lax.all_to_all(message.reshape(DEVICES, 16, 128), ('lat', 'wave'), split_...  12.5 us
    pallas_call x1, Pallas kernels, local(): pl.pallas_call(fourier_kernel, out_shape=jax.ShapeDtypeStruct((DEVICES *...  8.11 us
    pallas_call x1, Pallas kernels, local(): pl.pallas_call(legendre_kernel, grid=(SLOTS,), out_shape=jax.ShapeDtypeSt...  5.94 us
    ppermute x1, waiting for transfers between devices, local(): below = lax.ppermute(own, 'lat', [(i + 1, i) for i in range(bands - 1)])  4.78 us
    pallas_call x1, Pallas kernels, local(): pl.pallas_call(interpolate_kernel, out_shape=(jax.ShapeDtypeStruct((ROWS,...  4.06 us
    ppermute x1, starting transfers between devices, local(): above = lax.ppermute(own, 'lat', [(i, i + 1) for i in range(bands - 1)])  4 us
    unnamed x16, local copies, waits for them, and re-layouts  3.71 us
  transfers between devices with their start and end apart: 6, of which 5 were waited for; matrix products, arithmetic and copies ran while one was open for 2% of the time, Pallas kernels for 5%

commit v1 on v0

v1 whole, which is shorter than its diff:
```python
import math

import jax
import jax.numpy as jnp
from jax import lax
from jax.experimental import pallas as pl
from jax.experimental.pallas import tpu as pltpu
from jax.sharding import PartitionSpec as P

F32 = jnp.float32
BF16 = jnp.bfloat16
VMEM = pl.BlockSpec(memory_space=pltpu.VMEM)
SMEM = pl.BlockSpec(memory_space=pltpu.SMEM)
LIMIT = 24 * 1024 * 1024

SLICES = 24
BAND = 8
WIDE = 640
BLOCKS = 5
SLOTS = 10
DEVICES = 128
ROWS = 4
STACK = 128


def cubic_weights(fraction):
    return (
        -fraction * (fraction - 1.0) * (fraction - 2.0) / 6.0,
        (fraction + 1.0) * (fraction - 1.0) * (fraction - 2.0) / 2.0,
        -(fraction + 1.0) * fraction * (fraction - 2.0) / 2.0,
        (fraction + 1.0) * fraction * (fraction - 1.0) / 6.0,
    )


def picked_weight(distance, weights):
    chosen = jnp.where(distance == 3, weights[3], 0.0)
    for step in (2, 1, 0):
        chosen = jnp.where(distance == step, weights[step], chosen)
    return chosen


def interpolate_kernel(
    place, live, own, above, below, columns, rows_of, keep, send, main, edge, stack
):
    count = BAND * SLICES
    for part, ref in enumerate((above, own, below)):
        rows = pl.ds(part * count, count)
        main[rows, :] = ref[:, :WIDE]
        for block in range(BLOCKS):
            right = block + 1
            left = block - 1 if block else BLOCKS
            edge[rows, 128 * block : 128 * block + 128] = jnp.concatenate(
                [ref[:, 128 * right : 128 * right + 64], ref[:, 128 * left + 64 : 128 * left + 128]],
                axis=1,
            )
    core = place[0]

    def one_pair(step, carry):
        pair = step ^ (2 * core)
        window = pl.ds(pl.multiple_of(pair * (2 * SLICES), 2 * SLICES), 18 * SLICES)
        for block in range(BLOCKS):
            lanes = slice(128 * block, 128 * block + 128)
            left = jnp.concatenate([main[window, lanes], edge[window, lanes]], axis=1)
            spread = jnp.dot(left, columns[pair, block], preferred_element_type=F32)
            for half in range(2):
                side = slice(128 * half, 128 * half + 128)
                total = jnp.zeros((SLICES, 128), F32)
                for row in range(half, half + 17):
                    total = total + rows_of[pair, block, row : row + 1, side] * spread[
                        SLICES * row : SLICES * row + SLICES, side
                    ]
                position = lax.broadcasted_iota(jnp.int32, (SLICES, 128), 1) + 128 * block
                total = jnp.where(position < live[2 * pair + half], total, 0.0)
                stack[2 * step + half, SLICES * block : SLICES * block + SLICES, :] = total
        return carry

    for row in range(BAND):
        stack[row, BLOCKS * SLICES :, :] = jnp.zeros((STACK - BLOCKS * SLICES, 128), F32)
    lax.fori_loop(0, BAND // 2, one_pair, 0)
    keep[...] = stack[0:ROWS].astype(BF16)
    send[...] = stack[ROWS:].astype(BF16)


def turn(count, length, inverse):
    whole = jnp.floor(count * inverse + 0.5)
    angle = (count - whole * length) * (inverse * math.pi)
    square = angle * angle
    sine = angle * (
        1.0
        + square
        * (
            -1.0 / 6
            + square
            * (1.0 / 120 + square * (-1.0 / 5040 + square * (1.0 / 362880 - square / 39916800)))
        )
    )
    cosine = 1.0 + square * (
        -0.5
        + square
        * (
            1.0 / 24
            + square
            * (-1.0 / 720 + square * (1.0 / 40320 + square * (-1.0 / 3628800 + square / 479001600)))
        )
    )
    return 1.0 - 2.0 * sine * sine, 2.0 * sine * cosine


def rotated(one, two):
    return one[0] * two[0] - one[1] * two[1], one[1] * two[0] + one[0] * two[1]


def table_kernel(
    place, lengths, waves, depart_row, depart_col, frac_row, frac_col,
    inner, outer, columns, rows_of, points,
):
    wave_place = place[1]
    step = lax.broadcasted_iota(jnp.int32, (8, 128), 0)
    away = ((wave_place ^ 1) - wave_place) * WIDE
    shift = jnp.where(step == 5, away, jnp.where(step == 6, 64, 128 * step + wave_place * WIDE))
    shift = shift.astype(F32)
    fine = step.astype(F32)

    def one(index, carry):
        row = index // SLOTS
        slot = index % SLOTS
        length = jnp.full((1, 128), lengths[row], jnp.int32).astype(F32)
        inverse = 1.0 / length
        wave = waves[pl.ds(slot, 1), :]
        lanes = pl.ds(pl.multiple_of(slot * 256, 256), 128)
        lanes_two = pl.ds(pl.multiple_of(slot * 256 + 128, 128), 128)
        moved = turn(shift * wave, length, inverse)
        norm = lax.rsqrt(length)
        outer[row, :, lanes] = moved[0] * norm
        outer[row, :, lanes_two] = moved[1] * norm
        other = [part[5:6] for part in moved]
        half = [part[6:7] for part in moved]
        small = turn(fine * wave, length, inverse)
        low = turn(8.0 * fine * wave, length, inverse)
        for tile in range(2):
            if tile:
                low = rotated(low, other)
            high = rotated(low, half)
            for coarse in range(0, 16, 2):
                source = low if coarse < 8 else high
                at = coarse % 8
                pairs = [
                    rotated([part[k : k + 1] for part in source], small) for k in (at, at + 1)
                ]
                rows = slice(128 * tile + 8 * coarse, 128 * tile + 8 * coarse + 16)
                for side, to in enumerate((lanes, lanes_two)):
                    inner[row, rows, to] = jnp.concatenate(
                        [pair[side] for pair in pairs], axis=0
                    ).astype(BF16)
        return carry

    lax.fori_loop(0, ROWS * SLOTS, one, 0)

    lane = lax.broadcasted_iota(jnp.int32, (1, WIDE), 1) % 128
    for base, first, fraction in (
        (0, depart_col[...] + lane - 1, frac_col),
        (8, depart_row[...] + (BAND - 1), frac_row),
    ):
        for k, value in enumerate((first.astype(F32),) + cubic_weights(fraction[...])):
            for row in range(BAND):
                points[row, base + k : base + k + 1, :] = value[row : row + 1, :]

    def one_pair(pair, carry):
        def row_of(item, block):
            return jnp.concatenate(
                [
                    points[2 * pair + half, item : item + 1, 128 * block : 128 * block + 128]
                    for half in range(2)
                ],
                axis=1,
            )

        for block in range(BLOCKS):
            start = row_of(0, block)
            weights = [row_of(1 + k, block) for k in range(4)]
            source = lax.broadcasted_iota(jnp.int32, (144, 256), 0).astype(F32)
            columns[pair, block, 0:144, :] = picked_weight(source - start, weights).astype(BF16)
            columns[pair, block, 144:240, :] = jnp.zeros((96, 256), BF16)
            source = lax.broadcasted_iota(jnp.int32, (16, 256), 0).astype(F32) - 16.0
            columns[pair, block, 240:256, :] = picked_weight(source - start, weights).astype(BF16)
            half = (lax.broadcasted_iota(jnp.int32, (1, 256), 1) >= 128).astype(F32)
            start = row_of(8, block) + half
            weights = [row_of(9 + k, block) for k in range(4)]
            source = lax.broadcasted_iota(jnp.int32, (24, 256), 0).astype(F32)
            rows_of[pair, block] = picked_weight(source - start, weights)
        return carry

    lax.fori_loop(0, BAND // 2, one_pair, 0)


def fourier_kernel(mine, other, inner, outer, message, sums, shuffled):
    def one(row, carry):
        left = jnp.concatenate([mine[row], other[row]], axis=1)
        base = pl.multiple_of(row * 512, 512)
        sums[pl.ds(base + 480, 32), :] = jnp.zeros((32, 128), F32)
        for slot in range(SLOTS):
            lanes = slice(256 * slot, 256 * slot + 256)
            parts = jnp.dot(left, inner[row, :, lanes], preferred_element_type=F32)
            real = jnp.zeros((SLICES, 128), F32)
            imag = jnp.zeros((SLICES, 128), F32)
            for block in range(BLOCKS):
                rows = slice(SLICES * block, SLICES * block + SLICES)
                cosine, sine = parts[rows, :128], parts[rows, 128:]
                c = outer[row, block : block + 1, 256 * slot : 256 * slot + 128]
                s = outer[row, block : block + 1, 256 * slot + 128 : 256 * slot + 256]
                real = real + (c * cosine - s * sine)
                imag = imag - (s * cosine + c * sine)
            sums[pl.ds(base + slot * 48, SLICES, stride=2), :] = real
            sums[pl.ds(base + slot * 48 + 1, SLICES, stride=2), :] = imag
        return carry

    lax.fori_loop(0, ROWS, one, 0)
    for part in range(16):
        shuffled[pl.ds(part, DEVICES, stride=16), :] = sums[128 * part : 128 * part + 128, :].T
    message[...] = shuffled[...].astype(BF16)


def legendre_kernel(place, waves, message, table, out, flat, sorted_rows, left, result, done):
    for band in range(16):
        for core in range(2):
            total = message[8 * band + core].astype(F32)
            for z in range(1, 4):
                total = total + message[8 * band + 2 * z + core].astype(F32)
            first = (2 * band + core) * 16
            flat[first : first + 16, :] = total
    for row in range(ROWS):
        for part in range(4):
            sorted_rows[pl.ds(128 * part + row, 32, stride=4), :] = flat[
                pl.ds(4 * row + part, 32, stride=16), :
            ]
    for part in range(4):
        rows = slice(128 * part, 128 * part + 128)
        left[rows, :] = sorted_rows[rows, :].T.astype(BF16)
    copies = []
    for slot in range(SLOTS):
        product = jnp.dot(left[48 * slot : 48 * slot + 48, :], table[slot], preferred_element_type=F32)
        degree = lax.broadcasted_iota(jnp.int32, product.shape, 1)
        result[slot] = jnp.where(degree >= waves[place[2] + slot], product, 0.0)
        copy = pltpu.make_async_copy(result.at[slot], out.at[slot], done.at[slot])
        copy.start()
        copies.append(copy)
    for copy in copies:
        copy.wait()


def local(fields, row_length, wave_order, depart_row, depart_col, frac_row, frac_col, legendre):
    wave_place = lax.axis_index("wave")
    lat_place = lax.axis_index("lat")
    core = wave_place % 2
    column_start = wave_place * WIDE
    live = row_length - column_start
    live_mask = jnp.arange(WIDE, dtype=jnp.int32)[None, :] < live[:, None]
    masked = jnp.where(live_mask[None], fields, jnp.zeros_like(fields))
    own = masked.transpose(1, 0, 2).reshape(BAND * SLICES, WIDE)
    ring = lax.axis_size("wave")
    first_slot = (lat_place * ring + wave_place) * SLOTS
    place = jnp.stack([core, wave_place, first_slot]).astype(jnp.int32)

    from_left = lax.ppermute(
        own[:, WIDE - 128 :], "wave", [(i, (i + 1) % ring) for i in range(ring)]
    )
    from_right = lax.ppermute(own[:, :128], "wave", [((i + 1) % ring, i) for i in range(ring)])
    rim = jnp.concatenate([from_right[:, :64], from_left[:, 64:]], axis=1)
    own = jnp.concatenate([own, rim], axis=1)
    bands = lax.axis_size("lat")
    above = lax.ppermute(own, "lat", [(i, i + 1) for i in range(bands - 1)])
    below = lax.ppermute(own, "lat", [(i + 1, i) for i in range(bands - 1)])

    lengths = lax.dynamic_slice_in_dim(row_length, core * ROWS, ROWS)
    ordered = wave_order.reshape(DEVICES, SLOTS).T.astype(F32)
    inner, outer, columns, rows_of = pl.pallas_call(
        table_kernel,
        out_shape=(
            jax.ShapeDtypeStruct((ROWS, 256, SLOTS * 256), BF16),
            jax.ShapeDtypeStruct((ROWS, 8, SLOTS * 256), F32),
            jax.ShapeDtypeStruct((BAND // 2, BLOCKS, 256, 256), BF16),
            jax.ShapeDtypeStruct((BAND // 2, BLOCKS, 24, 256), F32),
        ),
        in_specs=[SMEM, SMEM] + [VMEM] * 5,
        out_specs=(VMEM,) * 4,
        scratch_shapes=[pltpu.VMEM((BAND, 16, WIDE), F32)],
        compiler_params=pltpu.CompilerParams(vmem_limit_bytes=LIMIT),
        cost_estimate=pl.CostEstimate(flops=5_000_000_000, bytes_accessed=3_000_000, transcendentals=0),
        name="tables",
    )(place, lengths, ordered, depart_row, depart_col, frac_row, frac_col)

    keep, send = pl.pallas_call(
        interpolate_kernel,
        out_shape=(jax.ShapeDtypeStruct((ROWS, STACK, 128), BF16),) * 2,
        in_specs=[SMEM, SMEM] + [VMEM] * 5,
        out_specs=(VMEM, VMEM),
        scratch_shapes=[
            pltpu.VMEM((3 * BAND * SLICES, WIDE), BF16),
            pltpu.VMEM((3 * BAND * SLICES, WIDE), BF16),
            pltpu.VMEM((BAND, STACK, 128), F32),
        ],
        compiler_params=pltpu.CompilerParams(vmem_limit_bytes=LIMIT),
        name="interpolate",
    )(place, live, own, above, below, columns, rows_of)

    other = lax.ppermute(send, "wave", [(i, i ^ 1) for i in range(ring)])
    message = pl.pallas_call(
        fourier_kernel,
        out_shape=jax.ShapeDtypeStruct((DEVICES * 16, 128), BF16),
        in_specs=[VMEM] * 4,
        out_specs=VMEM,
        scratch_shapes=[
            pltpu.VMEM((ROWS * 512, 128), F32),
            pltpu.VMEM((DEVICES * 16, 128), F32),
        ],
        compiler_params=pltpu.CompilerParams(vmem_limit_bytes=LIMIT),
        name="fourier",
    )(keep, other, inner, outer)
    message = lax.all_to_all(
        message.reshape(DEVICES, 16, 128), ("lat", "wave"), split_axis=0, concat_axis=0, tiled=True
    )
    degrees = legendre.shape[2]
    return pl.pallas_call(
        legendre_kernel,
        out_shape=jax.ShapeDtypeStruct((SLOTS, 2 * SLICES, degrees), F32),
        in_specs=[SMEM, SMEM, VMEM, VMEM],
        out_specs=pl.BlockSpec(memory_space=pl.ANY),
        scratch_shapes=[
            pltpu.VMEM((512, 128), F32),
            pltpu.VMEM((512, 128), F32),
            pltpu.VMEM((512, 128), BF16),
            pltpu.VMEM((SLOTS, 2 * SLICES, degrees), F32),
            pltpu.SemaphoreType.DMA((SLOTS,)),
        ],
        compiler_params=pltpu.CompilerParams(vmem_limit_bytes=LIMIT),
        name="legendre",
    )(place, wave_order, message, legendre)


def solution(mesh):
    placed = (
        P(None, "lat", "wave"),
        P("lat"),
        P(),
        P("lat", "wave"),
        P("lat", "wave"),
        P("lat", "wave"),
        P("lat", "wave"),
        P(("lat", "wave"), None, None),
    )
    return jax.shard_map(
        local, mesh=mesh, in_specs=placed, out_specs=P(("lat", "wave"), None, None), check_vma=False
    )
```

time: 73.2 us -> 56.8 us (0.78)
  blocking collectives: 0 us -> 22.3 us
  waiting for transfers between devices: 21.6 us -> 1.94 us
  starting transfers between devices: 22.4 us -> 13 us
  Pallas kernels: 21.7 us -> 12.5 us
  local copies, waits for them, and re-layouts: 4.87 us -> 3.95 us
    all_to_all x0 -> x1, blocking collectives: none -> 22.3 us  [local(): lax.all_to_all(message.reshape(DEVICES, 16, 128), ('lat', 'wave'), split_...]
    all_to_all x1 -> x0, starting transfers between devices: 12.6 us -> none  [local(): lax.all_to_all(message.reshape(DEVICES, 16, 128), ('lat', 'wave'), split_...]
    all_to_all x1 -> x0, waiting for transfers between devices: 12.5 us -> none  [local(): lax.all_to_all(message.reshape(DEVICES, 16, 128), ('lat', 'wave'), split_...]
    pallas_call x1, Pallas kernels: 8.11 us -> 1.85 us  [local(): pl.pallas_call(fourier_kernel, out_shape=jax.ShapeDtypeStruct((DEVICES *...]
    ppermute x1, waiting for transfers between devices: 4.78 us -> 0.01 us  [local(): below = lax.ppermute(own, 'lat', [(i + 1, i) for i in range(bands - 1)])]
    ppermute x1, starting transfers between devices: 1.45 us -> 4.66 us  [local(): other = lax.ppermute(send, 'wave', [(i, i ^ 1) for i in range(ring)])]
    ppermute x1, waiting for transfers between devices: 2.25 us -> 0.01 us  [local(): lax.ppermute(own[:, :128], 'wave', [((i + 1) % ring, i) for i in range(ri...]
    pallas_call x2, Pallas kernels: 9.52 us -> 7.97 us  [the longest x1 5.51 us: local(): pl.pallas_call(table_kernel, out_shape=(jax.ShapeDtypeStruct((ROWS, 256,...]
  transfers between devices with their start and end apart: 6 -> 5, of which waited for: 5 -> 2; matrix products, arithmetic and copies ran while one was open for 2% -> 3% of each run, Pallas kernels for 5% -> 10%
where the time goes in v1:
time: 56.8 us; the launch traced here: 56.3 us
  blocking collectives  22.3 us (39%)
  starting transfers between devices  13 us (23%)
  Pallas kernels  12.5 us (22%)
  local copies, waits for them, and re-layouts  3.95 us (7%)
  other arithmetic  2.57 us (5%)
  waiting for transfers between devices  1.94 us (3%)
    all_to_all x1, blocking collectives, local(): lax.all_to_all(message.reshape(DEVICES, 16, 128), ('lat', 'wave'), split_...  22.3 us
    pallas_call x1, Pallas kernels, local(): pl.pallas_call(table_kernel, out_shape=(jax.ShapeDtypeStruct((ROWS, 256,...  5.51 us
    ppermute x1, starting transfers between devices, local(): other = lax.ppermute(send, 'wave', [(i, i ^ 1) for i in range(ring)])  4.66 us
    ppermute x1, starting transfers between devices, local(): above = lax.ppermute(own, 'lat', [(i, i + 1) for i in range(bands - 1)])  4 us
    unnamed x12, local copies, waits for them, and re-layouts  2.91 us
    pallas_call x1, Pallas kernels, local(): pl.pallas_call(interpolate_kernel, out_shape=(jax.ShapeDtypeStruct((ROWS,...  2.63 us
    pallas_call x1, Pallas kernels, local(): pl.pallas_call(legendre_kernel, out_shape=jax.ShapeDtypeStruct((SLOTS, 2...  2.46 us
    pallas_call x1, Pallas kernels, local(): pl.pallas_call(fourier_kernel, out_shape=jax.ShapeDtypeStruct((DEVICES *...  1.85 us
  transfers between devices with their start and end apart: 5, of which 2 were waited for; matrix products, arithmetic and copies ran while one was open for 3% of the time, Pallas kernels for 10%

profile of v1, /device:TPU:1, one launch (start us, length us, event | category | flops | bytes accessed | tf_op | source)
XLA Modules:
  0.0 56.3 jit_solution(13668593447825956421)
XLA Ops:
  0.0 0.7 %broadcast_subtract_fusion.live = s32[8]{0:T(128)S(1)} fusion(s32[8]{0:T(128)} %param.9, s32[]{:T(128)S(6)} %mul.14), kind=kLoop, calls=%fused_computation.4 | loop fusion | flops 8 | bytes 68 | tf_op jit(solution)/shard_map/sub | solution.py:256
  0.7 0.1 iota_compare_fusion
  0.7 1.0 %select_bitcast_fusion = bf16[8,24,640]{2,0,1:T(8,128)(2,1)S(1)} fusion(bf16[24,8,640]{2,1,0:T(8,128)(2,1)} %param.8, pred[8,640]{1,0:T(8,128)(4,1)S(1)} %iota_compare_fusion), kind=kLoop, calls=%fused_computation.1 | loop fusion | flops 122880 | bytes 496640 | tf_op jit(solution)/shard_map/transpose | solution.py:259
  1.8 1.4 %collective-permute-start = (bf16[192,128]{1,0:T(8,128)(2,1)S(1)}, bf16[192,128]{1,0:T(8,128)(2,1)S(1)}, u32[]{:S(2)}, u32[]{:S(2)}) collective-permute-start(bf16[192,128]{1,0:T(8,128)(2,1)S(1)} %get-tuple-element.17), channel_id=1, source_target_pairs={{1,0},{2,1},{3,2},{4,3},{5,4},{6,5},{7,6},{0,7},{9,8},{10,9},{11,1... | collective-permute-start | bytes 147464 | tf_op jit(solution)/shard_map/ppermute | solution.py:267
  3.2 1.6 %collective-permute-start.1 = (bf16[192,128]{1,0:T(8,128)(2,1)S(1)}, bf16[192,128]{1,0:T(8,128)(2,1)S(1)}, u32[]{:S(2)}, u32[]{:S(2)}) collective-permute-start(bf16[192,128]{1,0:T(8,128)(2,1)S(1)} %get-tuple-element.18), channel_id=1, source_target_pairs={{0,1},{1,2},{2,3},{3,4},{4,5},{5,6},{6,7},{7,0},{8,9},{9,10},{10,1... | collective-permute-start | bytes 147464 | tf_op jit(solution)/shard_map/ppermute | solution.py:264
  4.9 0.7 %dynamic_slice.3.lengths = s32[4]{0:T(128)S(1)} dynamic-slice(s32[8]{0:T(128)} %param.9, s32[]{:T(128)S(6)} %select_n.16), dynamic_slice_sizes={4} | dynamic-slice | bytes 36 | tf_op jit(solution)/shard_map/dynamic_slice | solution.py:274
  5.6 0.7 %convert_element_type.7 = f32[1280]{0:T(1024)S(1)} convert(s32[1280]{0:T(1024)} %waves.1) | non-fusion elementwise | flops 1280 | bytes 10240 | tf_op jit(solution)/shard_map/convert_element_type | solution.py:275
  6.3 0.1 convert_element_type.8
  6.5 0.9 %collective-permute-done.1 = bf16[192,128]{1,0:T(8,128)(2,1)S(1)} collective-permute-done((bf16[192,128]{1,0:T(8,128)(2,1)S(1)}, bf16[192,128]{1,0:T(8,128)(2,1)S(1)}, u32[]{:S(2)}, u32[]{:S(2)}) %collective-permute-start.1) | collective-permute-done | bytes 49184 | tf_op jit(solution)/shard_map/ppermute | solution.py:264
  7.5 0.1 slice.19
  7.6 0.1 pad_maximum_fusion.own
  7.7 1.3 %collective-permute-start.3 = (bf16[192,768]{1,0:T(8,128)(2,1)S(1)}, bf16[192,768]{1,0:T(8,128)(2,1)S(1)}, u32[]{:S(2)}, u32[]{:S(2)}) collective-permute-start(bf16[192,768]{1,0:T(8,128)(2,1)S(1)} %pad_maximum_fusion.own), channel_id=1, source_target_pairs={{8,0},{16,8},{24,16},{32,24},{40,32},{48,40},{56,48},{64,56},{72,6... | collective-permute-start | bytes 884744 | tf_op jit(solution)/shard_map/ppermute | solution.py:272
  9.0 4.0 %collective-permute-start.2 = (bf16[192,768]{1,0:T(8,128)(2,1)S(1)}, bf16[192,768]{1,0:T(8,128)(2,1)S(1)}, u32[]{:S(2)}, u32[]{:S(2)}) collective-permute-start(bf16[192,768]{1,0:T(8,128)(2,1)S(1)} %pad_maximum_fusion.own), channel_id=1, source_target_pairs={{0,8},{8,16},{16,24},{24,32},{32,40},{40,48},{48,56},{56,64},{64,7... | collective-permute-start | bytes 884744 | tf_op jit(solution)/shard_map/ppermute | solution.py:271
  13.0 0.7 %copy-done.2 = s32[8,640]{1,0:T(8,128)S(1)} copy-done((s32[8,640]{1,0:T(8,128)S(1)}, s32[8,640]{1,0:T(8,128)}, u32[]{:S(2)}) %copy-start.2) | copy-done | bytes 20504
  13.7 0.7 %copy-done.3 = s32[8,640]{1,0:T(8,128)S(1)} copy-done((s32[8,640]{1,0:T(8,128)S(1)}, s32[8,640]{1,0:T(8,128)}, u32[]{:S(2)}) %copy-start.3) | copy-done | bytes 20504
  14.4 0.7 %copy-done.4 = f32[8,640]{1,0:T(8,128)S(1)} copy-done((f32[8,640]{1,0:T(8,128)S(1)}, f32[8,640]{1,0:T(8,128)}, u32[]{:S(2)}) %copy-start.4) | copy-done | bytes 20504
  15.2 0.7 %copy-done.5 = f32[8,640]{1,0:T(8,128)S(1)} copy-done((f32[8,640]{1,0:T(8,128)S(1)}, f32[8,640]{1,0:T(8,128)}, u32[]{:S(2)}) %copy-start.5) | copy-done | bytes 20504
  15.9 5.5 %tables.1 = (bf16[4,256,2560]{2,1,0:T(8,128)(2,1)S(1)}, f32[4,8,2560]{2,1,0:T(8,128)S(1)}, bf16[4,5,256,256]{3,2,1,0:T(8,128)(2,1)S(1)}, f32[4,5,24,256]{3,2,1,0:T(8,128)S(1)}) custom-call(s32[3]{0:T(128)S(1)} %pad_add_fusion.place, s32[4]{0:T(128)S(1)} %dynamic_slice.3.lengths, f32[10,128]{1,0:T(8,128)S(1)} %bitcast.10, s32[8,640]{1,0:T(8,128)S(1)} %copy-done.2, ...), custom_call_target="tpu_custom_call" | custom-call | flops 5000000000 | bytes 3000000 | tf_op jit(solution)/shard_map/tables/pallas_call | solution.py:276
  21.4 2.6 %interpolate.1 = (bf16[4,128,128]{2,1,0:T(8,128)(2,1)S(1)}, bf16[4,128,128]{2,1,0:T(8,128)(2,1)S(1)}) custom-call(s32[3]{0:T(128)S(1)} %pad_add_fusion.place, s32[8]{0:T(128)S(1)} %broadcast_subtract_fusion.live, bf16[192,768]{1,0:T(8,128)(2,1)S(1)} %pad_maximum_fusion.own, bf16[192,768]{1,0:T(8,128)(2,1)S(1)} %collective-permute-done.2.above, ...), custom_call_target="tpu_custom_call" | custom-call | tf_op jit(solution)/shard_map/interpolate/pallas_call | solution.py:292
  24.1 4.7 %collective-permute-start.4 = (bf16[4,128,128]{2,1,0:T(8,128)(2,1)S(1)}, bf16[4,128,128]{2,1,0:T(8,128)(2,1)S(1)}, u32[]{:S(2)}, u32[]{:S(2)}) collective-permute-start(bf16[4,128,128]{2,1,0:T(8,128)(2,1)S(1)} %get-tuple-element.14), channel_id=1, source_target_pairs={{0,1},{1,0},{2,3},{3,2},{4,5},{5,4},{6,7},{7,6},{8,9},{9,8},{10,11... | collective-permute-start | bytes 393224 | tf_op jit(solution)/shard_map/ppermute | solution.py:306
  28.7 1.0 %collective-permute-done.4.other = bf16[4,128,128]{2,1,0:T(8,128)(2,1)S(1)} collective-permute-done((bf16[4,128,128]{2,1,0:T(8,128)(2,1)S(1)}, bf16[4,128,128]{2,1,0:T(8,128)(2,1)S(1)}, u32[]{:S(2)}, u32[]{:S(2)}) %collective-permute-start.4) | collective-permute-done | bytes 131104 | tf_op jit(solution)/shard_map/ppermute | solution.py:306
  29.7 1.9 %fourier.1 = bf16[2048,128]{1,0:T(8,128)(2,1)S(1)} custom-call(bf16[4,128,128]{2,1,0:T(8,128)(2,1)S(1)} %get-tuple-element.13.mine, bf16[4,128,128]{2,1,0:T(8,128)(2,1)S(1)} %collective-permute-done.4.other, bf16[4,256,2560]{2,1,0:T(8,128)(2,1)S(1)} %get-tuple-element.15.inner, f32[4,8,2560]{2,1,0:T(8,128)S(1)} %get-tuple-element.16.outer), custom_call_target="tpu_custom_call" | custom-call | tf_op jit(solution)/shard_map/fourier/pallas_call | solution.py:307
  31.6 22.3 %all_to_all.5.message = bf16[128,16,128]{2,1,0:T(8,128)(2,1)S(1)} all-to-all(bf16[128,16,128]{2,1,0:T(8,128)(2,1)S(1)} %bitcast.9), channel_id=1, replica_groups=mesh['lat'=16,'wave'=8] {'lat','wave'}, dimensions={0} | all-to-all | bytes 1048576 | tf_op jit(solution)/shard_map/all_to_all | solution.py:319
  53.9 2.5 %legendre.1 = f32[10,48,1280]{2,1,0:T(8,128)} custom-call(s32[3]{0:T(128)S(1)} %pad_add_fusion.place, s32[1280]{0:T(1024)S(1)} %copy-done.1, bf16[128,16,128]{2,1,0:T(8,128)(2,1)S(1)} %all_to_all.5.message, bf16[10,128,1280]{2,1,0:T(8,128)(2,1)S(1)} %copy-done), custom_call_target="tpu_custom_call" | custom-call | tf_op jit(solution)/shard_map/legendre/pallas_call | solution.py:323
  (15 shorter events, 0.2 us)
Async XLA Ops:
  1.8 5.8 %collective-permute-start = (bf16[192,128]{1,0:T(8,128)(2,1)S(1)}, bf16[192,128]{1,0:T(8,128)(2,1)S(1)}, u32[]{:S(2)}, u32[]{:S(2)}) collective-permute-start(bf16[192,128]{1,0:T(8,128)(2,1)S(1)} %get-tuple-element.17), channel_id=1, source_target_pairs={{1,0},{2,1},{3,2},{4,3},{5,4},{6,5},{7,6},{0,7},{9,8},{10,9},{11,1... | collective-permute-start | bytes 147464 | tf_op jit(solution)/shard_map/ppermute | solution.py:267
  3.2 4.3 %collective-permute-start.1 = (bf16[192,128]{1,0:T(8,128)(2,1)S(1)}, bf16[192,128]{1,0:T(8,128)(2,1)S(1)}, u32[]{:S(2)}, u32[]{:S(2)}) collective-permute-start(bf16[192,128]{1,0:T(8,128)(2,1)S(1)} %get-tuple-element.18), channel_id=1, source_target_pairs={{0,1},{1,2},{2,3},{3,4},{4,5},{5,6},{6,7},{7,0},{8,9},{9,10},{10,1... | collective-permute-start | bytes 147464 | tf_op jit(solution)/shard_map/ppermute | solution.py:264
  7.7 13.7 %collective-permute-start.3 = (bf16[192,768]{1,0:T(8,128)(2,1)S(1)}, bf16[192,768]{1,0:T(8,128)(2,1)S(1)}, u32[]{:S(2)}, u32[]{:S(2)}) collective-permute-start(bf16[192,768]{1,0:T(8,128)(2,1)S(1)} %pad_maximum_fusion.own), channel_id=1, source_target_pairs={{8,0},{16,8},{24,16},{32,24},{40,32},{48,40},{56,48},{64,56},{72,6... | collective-permute-start | bytes 884744 | tf_op jit(solution)/shard_map/ppermute | solution.py:272
  9.0 12.5 %collective-permute-start.2 = (bf16[192,768]{1,0:T(8,128)(2,1)S(1)}, bf16[192,768]{1,0:T(8,128)(2,1)S(1)}, u32[]{:S(2)}, u32[]{:S(2)}) collective-permute-start(bf16[192,768]{1,0:T(8,128)(2,1)S(1)} %pad_maximum_fusion.own), channel_id=1, source_target_pairs={{0,8},{8,16},{16,24},{24,32},{32,40},{40,48},{48,56},{56,64},{64,7... | collective-permute-start | bytes 884744 | tf_op jit(solution)/shard_map/ppermute | solution.py:271
  13.0 0.7 %copy-start.2 = (s32[8,640]{1,0:T(8,128)S(1)}, s32[8,640]{1,0:T(8,128)}, u32[]{:S(2)}) copy-start(s32[8,640]{1,0:T(8,128)} %depart_row.1) | copy-start | bytes 61444
  13.7 0.7 %copy-start.3 = (s32[8,640]{1,0:T(8,128)S(1)}, s32[8,640]{1,0:T(8,128)}, u32[]{:S(2)}) copy-start(s32[8,640]{1,0:T(8,128)} %depart_col.1) | copy-start | bytes 61444
  14.4 0.7 %copy-start.4 = (f32[8,640]{1,0:T(8,128)S(1)}, f32[8,640]{1,0:T(8,128)}, u32[]{:S(2)}) copy-start(f32[8,640]{1,0:T(8,128)} %frac_row.1) | copy-start | bytes 61444
  15.2 0.7 %copy-start.5 = (f32[8,640]{1,0:T(8,128)S(1)}, f32[8,640]{1,0:T(8,128)}, u32[]{:S(2)}) copy-start(f32[8,640]{1,0:T(8,128)} %frac_col.1) | copy-start | bytes 61444
  24.1 5.6 %collective-permute-start.4 = (bf16[4,128,128]{2,1,0:T(8,128)(2,1)S(1)}, bf16[4,128,128]{2,1,0:T(8,128)(2,1)S(1)}, u32[]{:S(2)}, u32[]{:S(2)}) collective-permute-start(bf16[4,128,128]{2,1,0:T(8,128)(2,1)S(1)} %get-tuple-element.14), channel_id=1, source_target_pairs={{0,1},{1,0},{2,3},{3,2},{4,5},{5,4},{6,7},{7,6},{8,9},{9,8},{10,11... | collective-permute-start | bytes 393224 | tf_op jit(solution)/shard_map/ppermute | solution.py:306
  29.7 24.1 %copy-start = (bf16[10,128,1280]{2,1,0:T(8,128)(2,1)S(1)}, bf16[10,128,1280]{2,1,0:T(8,128)(2,1)}, u32[]{:S(2)}) copy-start(bf16[10,128,1280]{2,1,0:T(8,128)(2,1)} %table.1) | copy-start | bytes 9830404
  29.7 24.1 %copy-start.1 = (s32[1280]{0:T(1024)S(1)}, s32[1280]{0:T(1024)}, u32[]{:S(2)}) copy-start(s32[1280]{0:T(1024)} %waves.1) | copy-start | bytes 15364

commit v2 on v1

--- a/solution.py
+++ b/solution.py
@@ -21,6 +21,9 @@
 DEVICES = 128
 ROWS = 4
 STACK = 128
+COUNT = 3 * BAND * SLICES
+GROUP = 48
+LENGTHS = 4
 
 
 def cubic_weights(fraction):
@@ -39,21 +42,48 @@
     return chosen
 
 
-def interpolate_kernel(
-    place, live, own, above, below, columns, rows_of, keep, send, main, edge, stack
-):
-    count = BAND * SLICES
-    for part, ref in enumerate((above, own, below)):
-        rows = pl.ds(part * count, count)
-        main[rows, :] = ref[:, :WIDE]
-        for block in range(BLOCKS):
-            right = block + 1
-            left = block - 1 if block else BLOCKS
-            edge[rows, 128 * block : 128 * block + 128] = jnp.concatenate(
-                [ref[:, 128 * right : 128 * right + 64], ref[:, 128 * left + 64 : 128 * left + 128]],
-                axis=1,
-            )
+def pack_kernel(place, own, first, second, main, to_left, to_right):
+    size = BAND * SLICES
+    odd = place[3]
+    main[pl.ds(pl.multiple_of(odd * 2 * size, size), size), :] = first[...]
+    main[size : 2 * size, :] = own[...]
+    main[pl.ds(pl.multiple_of((1 - odd) * 2 * size, size), size), :] = second[...]
+    lane = lax.broadcasted_iota(jnp.int32, (GROUP, 128), 1)
+    left = jnp.zeros((GROUP, 128), F32)
+    right = jnp.zeros((GROUP, 128), F32)
+    for group in range(COUNT // GROUP):
+        rows = slice(GROUP * group, GROUP * group + GROUP)
+        head = jnp.where(lane < 8, main[rows, :128].astype(F32), 0.0)
+        tail = jnp.where(lane >= 120, main[rows, WIDE - 128 :].astype(F32), 0.0)
+        left = left + pltpu.roll(head, 8 * group, 1)
+        right = right + pltpu.roll(tail, 8 * group + 8, 1)
+    to_left[...] = left.astype(BF16)
+    to_right[...] = right.astype(BF16)
+
+
+def weighted(spread, rows_of, half):
+    side = slice(128 * half, 128 * half + 128)
+    total = jnp.zeros((SLICES, 128), F32)
+    for row in range(half, half + 17):
+        total = total + rows_of[row : row + 1, side] * spread[
+            SLICES * row : SLICES * row + SLICES, side
+        ]
+    return total
+
+
+def interior_kernel(place, main, columns, rows_of, stack, edge):
+    for block in range(BLOCKS):
+        sides = [
+            main[:, 128 * block + 128 : 128 * block + 192]
+            if block < BLOCKS - 1
+            else jnp.zeros((COUNT, 64), BF16),
+            main[:, 128 * block - 64 : 128 * block] if block else jnp.zeros((COUNT, 64), BF16),
+        ]
+        edge[:, 128 * block : 128 * block + 128] = jnp.concatenate(sides, axis=1)
+    for row in range(BAND):
+        stack[row, BLOCKS * SLICES :, :] = jnp.zeros((STACK - BLOCKS * SLICES, 128), F32)
     core = place[0]
+    start = place[1] * WIDE
 
     def one_pair(step, carry):
         pair = step ^ (2 * core)
@@ -62,23 +92,58 @@
             lanes = slice(128 * block, 128 * block + 128)
             left = jnp.concatenate([main[window, lanes], edge[window, lanes]], axis=1)
             spread = jnp.dot(left, columns[pair, block], preferred_element_type=F32)
+            position = lax.broadcasted_iota(jnp.int32, (SLICES, 128), 1) + 128 * block
             for half in range(2):
-                side = slice(128 * half, 128 * half + 128)
-                total = jnp.zeros((SLICES, 128), F32)
-                for row in range(half, half + 17):
-                    total = total + rows_of[pair, block, row : row + 1, side] * spread[
-                        SLICES * row : SLICES * row + SLICES, side
-                    ]
-                position = lax.broadcasted_iota(jnp.int32, (SLICES, 128), 1) + 128 * block
-                total = jnp.where(position < live[2 * pair + half], total, 0.0)
+                total = weighted(spread, rows_of.at[pair, block], half)
+                live = place[LENGTHS + 2 * pair + half] - start
+                total = jnp.where(position < live, total, 0.0)
                 stack[2 * step + half, SLICES * block : SLICES * block + SLICES, :] = total
         return carry
 
-    for row in range(BAND):
-        stack[row, BLOCKS * SLICES :, :] = jnp.zeros((STACK - BLOCKS * SLICES, 128), F32)
     lax.fori_loop(0, BAND // 2, one_pair, 0)
-    keep[...] = stack[0:ROWS].astype(BF16)
-    send[...] = stack[ROWS:].astype(BF16)
+
+
+def border_kernel(
+    place, from_left, from_right, wrap_columns, wrap_rows, stack, keep, send, edge, extra
+):
+    lane = lax.broadcasted_iota(jnp.int32, (GROUP, 128), 1)
+    left = from_left[...].astype(F32)
+    right = from_right[...].astype(F32)
+    for group in range(COUNT // GROUP):
+        one = pltpu.roll(right, (128 - 8 * group) % 128, 1)
+        two = pltpu.roll(left, 120 - 8 * group, 1)
+        edge[GROUP * group : GROUP * group + GROUP, :] = jnp.where(lane < 64, one, two).astype(BF16)
+    core = place[0]
+    start = place[1] * WIDE
+    column = lax.broadcasted_iota(jnp.int32, (SLICES, 128), 1)
+    position = jnp.where(column < 64, column, column + (WIDE - 128))
+
+    def one_pair(step, carry):
+        pair = step ^ (2 * core)
+        window = pl.ds(pl.multiple_of(pair * (2 * SLICES), 2 * SLICES), 18 * SLICES)
+        spread = jnp.dot(edge[window, :], wrap_columns[pair], preferred_element_type=F32)
+        for half in range(2):
+            total = weighted(spread, wrap_rows.at[pair], half)
+            live = place[LENGTHS + 2 * pair + half] - start
+            extra[2 * step + half] = jnp.where(position < live, total, 0.0)
+        return carry
+
+    lax.fori_loop(0, BAND // 2, one_pair, 0)
+    last = SLICES * (BLOCKS - 1)
+    for ref, first in ((keep, 0), (send, ROWS)):
+        for row in range(ROWS):
+            more = extra[first + row]
+            full = stack[first + row]
+            full = jnp.concatenate(
+                [
+                    full[:SLICES] + jnp.where(column < 64, more, 0.0),
+                    full[SLICES:last],
+                    full[last : last + SLICES] + jnp.where(column >= 64, more, 0.0),
+                    full[last + SLICES :],
+                ],
+                axis=0,
+            )
+            ref[row] = full.astype(BF16)
 
 
 def turn(count, length, inverse):
@@ -111,9 +176,9 @@
 
 
 def table_kernel(
-    place, lengths, waves, depart_row, depart_col, frac_row, frac_col,
-    inner, outer, columns, rows_of, points,
+    place, waves, stencil, inner, outer, columns, rows_of, wrap_columns, wrap_rows, points
 ):
+    first_row = place[0] * ROWS
     wave_place = place[1]
     step = lax.broadcasted_iota(jnp.int32, (8, 128), 0)
     away = ((wave_place ^ 1) - wave_place) * WIDE
@@ -124,7 +189,7 @@
     def one(index, carry):
         row = index // SLOTS
         slot = index % SLOTS
-        length = jnp.full((1, 128), lengths[row], jnp.int32).astype(F32)
+        length = jnp.full((1, 128), place[LENGTHS + first_row + row], jnp.int32).astype(F32)
         inverse = 1.0 / length
         wave = waves[pl.ds(slot, 1), :]
         lanes = pl.ds(pl.multiple_of(slot * 256, 256), 128)
@@ -158,10 +223,10 @@
 
     lane = lax.broadcasted_iota(jnp.int32, (1, WIDE), 1) % 128
     for base, first, fraction in (
-        (0, depart_col[...] + lane - 1, frac_col),
-        (8, depart_row[...] + (BAND - 1), frac_row),
+        (0, stencil[1] + (lane - 1).astype(F32), stencil[3]),
+        (8, stencil[0] + (BAND - 1.0), stencil[2]),
     ):
-        for k, value in enumerate((first.astype(F32),) + cubic_weights(fraction[...])):
+        for k, value in enumerate((first,) + cubic_weights(fraction)):
             for row in range(BAND):
                 points[row, base + k : base + k + 1, :] = value[row : row + 1, :]
 
@@ -188,6 +253,12 @@
             weights = [row_of(9 + k, block) for k in range(4)]
             source = lax.broadcasted_iota(jnp.int32, (24, 256), 0).astype(F32)
             rows_of[pair, block] = picked_weight(source - start, weights)
+        ends = (0, BLOCKS - 1, 0, BLOCKS - 1)
+        wrap_columns[pair] = jnp.concatenate(
+            [columns[pair, end, 128:, 64 * k : 64 * k + 64] for k, end in enumerate(ends)], axis=1
+        )
+        side = lax.broadcasted_iota(jnp.int32, (24, 256), 1) % 128
+        wrap_rows[pair] = jnp.where(side < 64, rows_of[pair, 0], rows_of[pair, BLOCKS - 1])
         return carry
 
     lax.fori_loop(0, BAND // 2, one_pair, 0)
@@ -251,57 +322,76 @@
 def local(fields, row_length, wave_order, depart_row, depart_col, frac_row, frac_col, legendre):
     wave_place = lax.axis_index("wave")
     lat_place = lax.axis_index("lat")
-    core = wave_place % 2
-    column_start = wave_place * WIDE
-    live = row_length - column_start
-    live_mask = jnp.arange(WIDE, dtype=jnp.int32)[None, :] < live[:, None]
+    ring = lax.axis_size("wave")
+    bands = lax.axis_size("lat")
+    first_slot = (lat_place * ring + wave_place) * SLOTS
+    own_place = jnp.stack([wave_place % 2, wave_place, first_slot, lat_place % 2])
+    place = jnp.concatenate([own_place.astype(jnp.int32), row_length])
+    limit = place[LENGTHS:] - wave_place * WIDE
+    live_mask = jnp.arange(WIDE, dtype=jnp.int32)[None, :] < limit[:, None]
     masked = jnp.where(live_mask[None], fields, jnp.zeros_like(fields))
     own = masked.transpose(1, 0, 2).reshape(BAND * SLICES, WIDE)
-    ring = lax.axis_size("wave")
-    first_slot = (lat_place * ring + wave_place) * SLOTS
-    place = jnp.stack([core, wave_place, first_slot]).astype(jnp.int32)
-
-    from_left = lax.ppermute(
-        own[:, WIDE - 128 :], "wave", [(i, (i + 1) % ring) for i in range(ring)]
-    )
-    from_right = lax.ppermute(own[:, :128], "wave", [((i + 1) % ring, i) for i in range(ring)])
-    rim = jnp.concatenate([from_right[:, :64], from_left[:, 64:]], axis=1)
-    own = jnp.concatenate([own, rim], axis=1)
-    bands = lax.axis_size("lat")
-    above = lax.ppermute(own, "lat", [(i, i + 1) for i in range(bands - 1)])
-    below = lax.ppermute(own, "lat", [(i + 1, i) for i in range(bands - 1)])
-
-    lengths = lax.dynamic_slice_in_dim(row_length, core * ROWS, ROWS)
+
+    def swapped(first):
+        pairs = [(i, i + 1) for i in range(first, bands - 1, 2)]
+        return lax.ppermute(own, "lat", pairs + [(j, i) for i, j in pairs])
+
+    over = swapped(1)
+    under = swapped(0)
+
+    stencil = jnp.stack([depart_row.astype(F32), depart_col.astype(F32), frac_row, frac_col])
     ordered = wave_order.reshape(DEVICES, SLOTS).T.astype(F32)
-    inner, outer, columns, rows_of = pl.pallas_call(
+    inner, outer, columns, rows_of, wrap_columns, wrap_rows = pl.pallas_call(
         table_kernel,
         out_shape=(
             jax.ShapeDtypeStruct((ROWS, 256, SLOTS * 256), BF16),
             jax.ShapeDtypeStruct((ROWS, 8, SLOTS * 256), F32),
             jax.ShapeDtypeStruct((BAND // 2, BLOCKS, 256, 256), BF16),
             jax.ShapeDtypeStruct((BAND // 2, BLOCKS, 24, 256), F32),
+            jax.ShapeDtypeStruct((BAND // 2, 128, 256), BF16),
+            jax.ShapeDtypeStruct((BAND // 2, 24, 256), F32),
         ),
-        in_specs=[SMEM, SMEM] + [VMEM] * 5,
-        out_specs=(VMEM,) * 4,
+        in_specs=[SMEM, VMEM, VMEM],
+        out_specs=(VMEM,) * 6,
         scratch_shapes=[pltpu.VMEM((BAND, 16, WIDE), F32)],
         compiler_params=pltpu.CompilerParams(vmem_limit_bytes=LIMIT),
         cost_estimate=pl.CostEstimate(flops=5_000_000_000, bytes_accessed=3_000_000, transcendentals=0),
         name="tables",
-    )(place, lengths, ordered, depart_row, depart_col, frac_row, frac_col)
-
+    )(place, ordered, stencil)
+
+    main, to_left, to_right = pl.pallas_call(
+        pack_kernel,
+        out_shape=(
+            jax.ShapeDtypeStruct((COUNT, WIDE), BF16),
+            jax.ShapeDtypeStruct((GROUP, 128), BF16),
+            jax.ShapeDtypeStruct((GROUP, 128), BF16),
+        ),
+        in_specs=[SMEM] + [VMEM] * 3,
+        out_specs=(VMEM,) * 3,
+        compiler_params=pltpu.CompilerParams(vmem_limit_bytes=LIMIT),
+        name="pack",
+    )(place, own, over, under)
+    from_left = lax.ppermute(to_right, "wave", [(i, (i + 1) % ring) for i in range(ring)])
+    from_right = lax.ppermute(to_left, "wave", [((i + 1) % ring, i) for i in range(ring)])
+    stack = pl.pallas_call(
+        interior_kernel,
+        out_shape=jax.ShapeDtypeStruct((BAND, STACK, 128), F32),
+        in_specs=[SMEM] + [VMEM] * 3,
+        out_specs=VMEM,
+        scratch_shapes=[pltpu.VMEM((COUNT, WIDE), BF16)],
+        compiler_params=pltpu.CompilerParams(vmem_limit_bytes=LIMIT),
+        cost_estimate=pl.CostEstimate(flops=5_000_000_000, bytes_accessed=3_000_000, transcendentals=0),
+        name="interior",
+    )(place, main, columns, rows_of)
     keep, send = pl.pallas_call(
-        interpolate_kernel,
+        border_kernel,
         out_shape=(jax.ShapeDtypeStruct((ROWS, STACK, 128), BF16),) * 2,
-        in_specs=[SMEM, SMEM] + [VMEM] * 5,
+        in_specs=[SMEM] + [VMEM] * 5,
         out_specs=(VMEM, VMEM),
-        scratch_shapes=[
-            pltpu.VMEM((3 * BAND * SLICES, WIDE), BF16),
-            pltpu.VMEM((3 * BAND * SLICES, WIDE), BF16),
-            pltpu.VMEM((BAND, STACK, 128), F32),
-        ],
-        compiler_params=pltpu.CompilerParams(vmem_limit_bytes=LIMIT),
-        name="interpolate",
-    )(place, live, own, above, below, columns, rows_of)
+        scratch_shapes=[pltpu.VMEM((COUNT, 128), BF16), pltpu.VMEM((BAND, SLICES, 128), F32)],
+        compiler_params=pltpu.CompilerParams(vmem_limit_bytes=LIMIT),
+        name="border",
+    )(place, from_left, from_right, wrap_columns, wrap_rows, stack)
 
     other = lax.ppermute(send, "wave", [(i, i ^ 1) for i in range(ring)])
     message = pl.pallas_call(

time: 56.8 us -> 52.6 us (0.926)
  starting transfers between devices: 13 us -> 6.64 us
  local copies, waits for them, and re-layouts: 3.95 us -> 0.96 us
  Pallas kernels: 12.5 us -> 14.8 us
  blocking collectives: 22.3 us -> 24.3 us
  other arithmetic: 2.57 us -> 3.93 us
    ppermute x1, starting transfers between devices: 4.66 us -> 1.28 us  [local(): other = lax.ppermute(send, 'wave', [(i, i ^ 1) for i in range(ring)])]
    ppermute x4, starting transfers between devices: 8.36 us -> 5.36 us  [the longest x2 2.87 us: swapped(): return lax.ppermute(own, 'lat', pairs + [(j, i) for i, j in pairs])]
    unnamed x12 -> x4, local copies, waits for them, and re-layouts: 2.91 us -> 0.01 us
    pallas_call x1 -> x3, Pallas kernels: 2.63 us -> 4.87 us  [the longest x1 2.57 us: local(): pl.pallas_call(interior_kernel, out_shape=jax.ShapeDtypeStruct((BAND, STA...]
    all_to_all x1, blocking collectives: 22.3 us -> 24.3 us  [local(): lax.all_to_all(message.reshape(DEVICES, 16, 128), ('lat', 'wave'), split_...]
    another operation x1 -> x2, other arithmetic: 0.08 us -> 1.53 us  [local(): jnp.stack([depart_row.astype(F32), depart_col.astype(F32), frac_row, frac...]
    concatenate x0 -> x1, local copies, waits for them, and re-layouts: none -> 0.73 us  [local(): place = jnp.concatenate([own_place.astype(jnp.int32), row_length])]
    dynamic_slice x1 -> x0, local copies, waits for them, and re-layouts: 0.73 us -> none  [local(): lengths = lax.dynamic_slice_in_dim(row_length, core * ROWS, ROWS)]
  transfers between devices with their start and end apart: 5 -> 5, of which waited for: 2 -> 2; matrix products, arithmetic and copies ran while one was open for 3% -> 6% of each run, Pallas kernels for 10% -> 16%
where the time goes in v2:
time: 52.6 us; the launch traced here: 52.2 us
  blocking collectives  24.3 us (46%)
  Pallas kernels  14.8 us (28%)
  starting transfers between devices  6.64 us (13%)
  other arithmetic  3.93 us (7%)
  waiting for transfers between devices  1.53 us (3%)
  local copies, waits for them, and re-layouts  0.96 us (2%)
    all_to_all x1, blocking collectives, local(): lax.all_to_all(message.reshape(DEVICES, 16, 128), ('lat', 'wave'), split_...  24.3 us
    pallas_call x1, Pallas kernels, local(): pl.pallas_call(table_kernel, out_shape=(jax.ShapeDtypeStruct((ROWS, 256,...  5.6 us
    ppermute x2, starting transfers between devices, swapped(): return lax.ppermute(own, 'lat', pairs + [(j, i) for i, j in pairs])  2.87 us
    pallas_call x1, Pallas kernels, local(): pl.pallas_call(interior_kernel, out_shape=jax.ShapeDtypeStruct((BAND, STA...  2.57 us
    ppermute x1, starting transfers between devices, local(): lax.ppermute(to_right, 'wave', [(i, (i + 1) % ring) for i in range(ring)])  2.49 us
    pallas_call x1, Pallas kernels, local(): pl.pallas_call(legendre_kernel, out_shape=jax.ShapeDtypeStruct((SLOTS, 2...  2.46 us
    pallas_call x1, Pallas kernels, local(): pl.pallas_call(fourier_kernel, out_shape=jax.ShapeDtypeStruct((DEVICES *...  1.86 us
    pallas_call x1, Pallas kernels, local(): pl.pallas_call(border_kernel, out_shape=(jax.ShapeDtypeStruct((ROWS, STAC...  1.56 us
  transfers between devices with their start and end apart: 5, of which 2 were waited for; matrix products, arithmetic and copies ran while one was open for 6% of the time, Pallas kernels for 16%

profile of v2, /device:TPU:1, one launch (start us, length us, event | category | flops | bytes accessed | tf_op | source)
XLA Modules:
  0.0 52.2 jit_solution(8565488678795914985)
XLA Ops:
  0.0 0.7 %broadcast_subtract_fusion = s32[8]{0:T(128)S(1)} fusion(s32[8]{0:T(128)} %param.9, s32[]{:T(128)S(6)} %mul.11), kind=kLoop, calls=%fused_computation.5 | loop fusion | flops 8 | bytes 68 | tf_op jit(solution)/shard_map/sub | solution.py:330
  0.7 0.1 iota_compare_fusion
  0.7 1.0 %select_bitcast_fusion = bf16[8,24,640]{2,0,1:T(8,128)(2,1)S(1)} fusion(bf16[24,8,640]{2,1,0:T(8,128)(2,1)} %param.8, pred[8,640]{1,0:T(8,128)(4,1)S(1)} %iota_compare_fusion), kind=kLoop, calls=%fused_computation | loop fusion | flops 122880 | bytes 496640 | tf_op jit(solution)/shard_map/transpose | solution.py:333
  1.7 2.2 %collective-permute-start.1 = (bf16[192,640]{1,0:T(8,128)(2,1)S(1)}, bf16[192,640]{1,0:T(8,128)(2,1)S(1)}, u32[]{:S(2)}, u32[]{:S(2)}) collective-permute-start(bf16[192,640]{1,0:T(8,128)(2,1)S(1)} %bitcast.16), channel_id=1, source_target_pairs={{0,8},{16,24},{32,40},{48,56},{64,72},{80,88},{96,104},{112,120},{... | collective-permute-start | bytes 737288 | tf_op jit(solution)/shard_map/ppermute | solution.py:337
  4.0 0.7 %collective-permute-start = (bf16[192,640]{1,0:T(8,128)(2,1)S(1)}, bf16[192,640]{1,0:T(8,128)(2,1)S(1)}, u32[]{:S(2)}, u32[]{:S(2)}) collective-permute-start(bf16[192,640]{1,0:T(8,128)(2,1)S(1)} %bitcast.17), channel_id=1, source_target_pairs={{8,16},{24,32},{40,48},{56,64},{72,80},{88,96},{104,112},{16,8},{3... | collective-permute-start | bytes 737288 | tf_op jit(solution)/shard_map/ppermute | solution.py:337
  4.6 0.7 %convert_element_type.13 = f32[1280]{0:T(1024)S(1)} convert(s32[1280]{0:T(1024)} %waves.1) | non-fusion elementwise | flops 1280 | bytes 10240 | tf_op jit(solution)/shard_map/convert_element_type | solution.py:343
  5.3 0.1 convert_element_type.14
  5.5 0.1 copy.11
  5.5 0.8 %convert_bitcast_fusion = (f32[1,8,640]{2,1,0:T(8,128)S(1)}, f32[1,8,640]{2,1,0:T(8,128)S(1)}) fusion(s32[8,640]{1,0:T(8,128)} %param.12, s32[8,640]{1,0:T(8,128)} %param.11), kind=kLoop, calls=%fused_computation.2 | loop fusion | flops 10240 | bytes 81920 | tf_op jit(solution)/shard_map/stack | solution.py:342
  6.3 0.7 %concatenate.3.place = s32[12]{0:T(128)S(1)} concatenate(s32[1]{0:T(128)} %bitcast, s32[1]{0:T(128)} %bitcast.1, s32[1]{0:T(128)} %bitcast.2, s32[1]{0:T(128)} %bitcast.3, s32[8]{0:T(128)} %param.9), dimensions={0} | concatenate | bytes 96 | tf_op jit(solution)/shard_map/concatenate | solution.py:329
  7.0 0.8 %pad_maximum_fusion.stencil = f32[4,8,640]{2,1,0:T(8,128)S(1)} fusion(f32[1,8,640]{2,1,0:T(8,128)} %bitcast.20, f32[1,8,640]{2,1,0:T(8,128)} %bitcast.21, f32[1,8,640]{2,1,0:T(8,128)S(1)} %get-tuple-element.27, f32[1,8,640]{2,1,0:T(8,128)S(1)} %get-tuple-element.28), kind=kLoop, calls=%fused_computation.1 | loop fusion | flops 61440 | bytes 163840 | tf_op jit(solution)/shard_map/stack | solution.py:342
  7.8 5.6 %tables.1 = (bf16[4,256,2560]{2,1,0:T(8,128)(2,1)S(1)}, f32[4,8,2560]{2,1,0:T(8,128)S(1)}, bf16[4,5,256,256]{3,2,1,0:T(8,128)(2,1)S(1)}, f32[4,5,24,256]{3,2,1,0...) custom-call(s32[12]{0:T(128)S(1)} %concatenate.3.place, f32[10,128]{1,0:T(8,128)S(1)} %bitcast.19, ...), custom_call_target="tpu_custom_call" | custom-call | flops 5000000000 | bytes 3000000 | tf_op jit(solution)/shard_map/tables/pallas_call | solution.py:344
  13.4 0.0 collective-permute-done.1.second
  13.4 0.0 collective-permute-done.first
  13.4 0.7 %pack.1 = (bf16[576,640]{1,0:T(8,128)(2,1)S(1)}, bf16[48,128]{1,0:T(8,128)(2,1)S(1)}, bf16[48,128]{1,0:T(8,128)(2,1)S(1)}) custom-call(s32[12]{0:T(128)S(1)} %concatenate.3.place, bf16[192,640]{1,0:T(8,128)(2,1)S(1)} %bitcast.18, bf16[192,640]{1,0:T(8,128)(2,1)S(1)} %collective-permute-done.first, bf16[192,640]{1,0:T(8,128)(2,1)S(1)} %collective-permute-done.1.second), custom_call_target="tpu_custom_call" | custom-call | tf_op jit(solution)/shard_map/pack/pallas_call | solution.py:362
  14.2 2.5 %collective-permute-start.2 = (bf16[48,128]{1,0:T(8,128)(2,1)S(1)}, bf16[48,128]{1,0:T(8,128)(2,1)S(1)}, u32[]{:S(2)}, u32[]{:S(2)}) collective-permute-start(bf16[48,128]{1,0:T(8,128)(2,1)S(1)} %get-tuple-element.16), channel_id=1, source_target_pairs={{0,1},{1,2},{2,3},{3,4},{4,5},{5,6},{6,7},{7,0},{8,9},{9,10},{10,1... | collective-permute-start | bytes 36872 | tf_op jit(solution)/shard_map/ppermute | solution.py:374
  16.7 2.6 %interior.1.stack = f32[8,128,128]{2,1,0:T(8,128)S(1)} custom-call(s32[12]{0:T(128)S(1)} %concatenate.3.place, bf16[576,640]{1,0:T(8,128)(2,1)S(1)} %get-tuple-element.20.main, bf16[4,5,256,256]{3,2,1,0:T(8,128)(2,1)S(1)} %get-tuple-element.21.columns, f32[4,5,24,256]{3,2,1,0:T(8,128)S(1)} %get-tuple-element.22.rows_of), custom_call_target="tpu_custom_call" | custom-call | flops 5000000000 | bytes 3000000 | tf_op jit(solution)/shard_map/interior/pallas_call | solution.py:376
  19.3 0.5 %collective-permute-done.3.from_right = bf16[48,128]{1,0:T(8,128)(2,1)S(1)} collective-permute-done((bf16[48,128]{1,0:T(8,128)(2,1)S(1)}, bf16[48,128]{1,0:T(8,128)(2,1)S(1)}, u32[]{:S(2)}, u32[]{:S(2)}) %collective-permute-start.3) | collective-permute-done | bytes 12320 | tf_op jit(solution)/shard_map/ppermute | solution.py:375
  19.8 1.6 %border.1 = (bf16[4,128,128]{2,1,0:T(8,128)(2,1)S(1)}, bf16[4,128,128]{2,1,0:T(8,128)(2,1)S(1)}) custom-call(s32[12]{0:T(128)S(1)} %concatenate.3.place, bf16[48,128]{1,0:T(8,128)(2,1)S(1)} %collective-permute-done.2.from_left, bf16[48,128]{1,0:T(8,128)(2,1)S(1)} %collective-permute-done.3.from_right, ...), custom_call_target="tpu_custom_call" | custom-call | tf_op jit(solution)/shard_map/border/pallas_call | solution.py:386
  21.4 1.3 %collective-permute-start.4 = (bf16[4,128,128]{2,1,0:T(8,128)(2,1)S(1)}, bf16[4,128,128]{2,1,0:T(8,128)(2,1)S(1)}, u32[]{:S(2)}, u32[]{:S(2)}) collective-permute-start(bf16[4,128,128]{2,1,0:T(8,128)(2,1)S(1)} %get-tuple-element.24), channel_id=1, source_target_pairs={{0,1},{1,0},{2,3},{3,2},{4,5},{5,4},{6,7},{7,6},{8,9},{9,8},{10,11... | collective-permute-start | bytes 393224 | tf_op jit(solution)/shard_map/ppermute | solution.py:396
  22.6 1.0 %collective-permute-done.4.other = bf16[4,128,128]{2,1,0:T(8,128)(2,1)S(1)} collective-permute-done((bf16[4,128,128]{2,1,0:T(8,128)(2,1)S(1)}, bf16[4,128,128]{2,1,0:T(8,128)(2,1)S(1)}, u32[]{:S(2)}, u32[]{:S(2)}) %collective-permute-start.4) | collective-permute-done | bytes 131104 | tf_op jit(solution)/shard_map/ppermute | solution.py:396
  23.6 1.9 %fourier.1 = bf16[2048,128]{1,0:T(8,128)(2,1)S(1)} custom-call(bf16[4,128,128]{2,1,0:T(8,128)(2,1)S(1)} %get-tuple-element.23.mine, bf16[4,128,128]{2,1,0:T(8,128)(2,1)S(1)} %collective-permute-done.4.other, bf16[4,256,2560]{2,1,0:T(8,128)(2,1)S(1)} %get-tuple-element.25.inner, f32[4,8,2560]{2,1,0:T(8,128)S(1)} %get-tuple-element.26.outer), custom_call_target="tpu_custom_call" | custom-call | tf_op jit(solution)/shard_map/fourier/pallas_call | solution.py:397
  25.5 24.3 %all_to_all.5.message = bf16[128,16,128]{2,1,0:T(8,128)(2,1)S(1)} all-to-all(bf16[128,16,128]{2,1,0:T(8,128)(2,1)S(1)} %bitcast.15), channel_id=1, replica_groups=mesh['lat'=16,'wave'=8] {'lat','wave'}, dimensions={0} | all-to-all | bytes 1048576 | tf_op jit(solution)/shard_map/all_to_all | solution.py:409
  49.8 2.5 %legendre.1 = f32[10,48,1280]{2,1,0:T(8,128)} custom-call(s32[12]{0:T(128)S(1)} %concatenate.3.place, s32[1280]{0:T(1024)S(1)} %copy-done.1, bf16[128,16,128]{2,1,0:T(8,128)(2,1)S(1)} %all_to_all.5.message, bf16[10,128,1280]{2,1,0:T(8,128)(2,1)S(1)} %copy-done), custom_call_target="tpu_custom_call" | custom-call | tf_op jit(solution)/shard_map/legendre/pallas_call | solution.py:413
  (7 shorter events, 0.0 us)
Async XLA Ops:
  1.7 11.7 %collective-permute-start.1 = (bf16[192,640]{1,0:T(8,128)(2,1)S(1)}, bf16[192,640]{1,0:T(8,128)(2,1)S(1)}, u32[]{:S(2)}, u32[]{:S(2)}) collective-permute-start(bf16[192,640]{1,0:T(8,128)(2,1)S(1)} %bitcast.16), channel_id=1, source_target_pairs={{0,8},{16,24},{32,40},{48,56},{64,72},{80,88},{96,104},{112,120},{... | collective-permute-start | bytes 737288 | tf_op jit(solution)/shard_map/ppermute | solution.py:337
  4.0 9.5 %collective-permute-start = (bf16[192,640]{1,0:T(8,128)(2,1)S(1)}, bf16[192,640]{1,0:T(8,128)(2,1)S(1)}, u32[]{:S(2)}, u32[]{:S(2)}) collective-permute-start(bf16[192,640]{1,0:T(8,128)(2,1)S(1)} %bitcast.17), channel_id=1, source_target_pairs={{8,16},{24,32},{40,48},{56,64},{72,80},{88,96},{104,112},{16,8},{3... | collective-permute-start | bytes 737288 | tf_op jit(solution)/shard_map/ppermute | solution.py:337
  14.2 5.1 %collective-permute-start.2 = (bf16[48,128]{1,0:T(8,128)(2,1)S(1)}, bf16[48,128]{1,0:T(8,128)(2,1)S(1)}, u32[]{:S(2)}, u32[]{:S(2)}) collective-permute-start(bf16[48,128]{1,0:T(8,128)(2,1)S(1)} %get-tuple-element.16), channel_id=1, source_target_pairs={{0,1},{1,2},{2,3},{3,4},{4,5},{5,6},{6,7},{7,0},{8,9},{9,10},{10,1... | collective-permute-start | bytes 36872 | tf_op jit(solution)/shard_map/ppermute | solution.py:374
  16.7 3.1 %collective-permute-start.3 = (bf16[48,128]{1,0:T(8,128)(2,1)S(1)}, bf16[48,128]{1,0:T(8,128)(2,1)S(1)}, u32[]{:S(2)}, u32[]{:S(2)}) collective-permute-start(bf16[48,128]{1,0:T(8,128)(2,1)S(1)} %get-tuple-element.17), channel_id=1, source_target_pairs={{1,0},{2,1},{3,2},{4,3},{5,4},{6,5},{7,6},{0,7},{9,8},{10,9},{11,1... | collective-permute-start | bytes 36872 | tf_op jit(solution)/shard_map/ppermute | solution.py:375
  21.4 2.3 %collective-permute-start.4 = (bf16[4,128,128]{2,1,0:T(8,128)(2,1)S(1)}, bf16[4,128,128]{2,1,0:T(8,128)(2,1)S(1)}, u32[]{:S(2)}, u32[]{:S(2)}) collective-permute-start(bf16[4,128,128]{2,1,0:T(8,128)(2,1)S(1)} %get-tuple-element.24), channel_id=1, source_target_pairs={{0,1},{1,0},{2,3},{3,2},{4,5},{5,4},{6,7},{7,6},{8,9},{9,8},{10,11... | collective-permute-start | bytes 393224 | tf_op jit(solution)/shard_map/ppermute | solution.py:396
  23.6 26.1 %copy-start = (bf16[10,128,1280]{2,1,0:T(8,128)(2,1)S(1)}, bf16[10,128,1280]{2,1,0:T(8,128)(2,1)}, u32[]{:S(2)}) copy-start(bf16[10,128,1280]{2,1,0:T(8,128)(2,1)} %table.1) | copy-start | bytes 9830404
  23.6 26.1 %copy-start.1 = (s32[1280]{0:T(1024)S(1)}, s32[1280]{0:T(1024)}, u32[]{:S(2)}) copy-start(s32[1280]{0:T(1024)} %waves.1) | copy-start | bytes 15364

commit v3 on v2

--- a/solution.py
+++ b/solution.py
@@ -36,15 +36,15 @@
 
 
 def picked_weight(distance, weights):
-    chosen = jnp.where(distance == 3, weights[3], 0.0)
+    chosen = jnp.where(distance == 3, weights[3], jnp.zeros_like(weights[3]))
     for step in (2, 1, 0):
         chosen = jnp.where(distance == step, weights[step], chosen)
     return chosen
 
 
-def pack_kernel(place, own, first, second, main, to_left, to_right):
+def pack_kernel(own, first, second, main, to_left, to_right):
     size = BAND * SLICES
-    odd = place[3]
+    odd = lax.axis_index("lat") % 2
     main[pl.ds(pl.multiple_of(odd * 2 * size, size), size), :] = first[...]
     main[size : 2 * size, :] = own[...]
     main[pl.ds(pl.multiple_of((1 - odd) * 2 * size, size), size), :] = second[...]
@@ -71,7 +71,7 @@
     return total
 
 
-def interior_kernel(place, main, columns, rows_of, stack, edge):
+def interior_kernel(main, columns, rows_of, stack, edge):
     for block in range(BLOCKS):
         sides = [
             main[:, 128 * block + 128 : 128 * block + 192]
@@ -82,8 +82,7 @@
         edge[:, 128 * block : 128 * block + 128] = jnp.concatenate(sides, axis=1)
     for row in range(BAND):
         stack[row, BLOCKS * SLICES :, :] = jnp.zeros((STACK - BLOCKS * SLICES, 128), F32)
-    core = place[0]
-    start = place[1] * WIDE
+    core = lax.axis_index("wave") % 2
 
     def one_pair(step, carry):
         pair = step ^ (2 * core)
@@ -92,48 +91,25 @@
             lanes = slice(128 * block, 128 * block + 128)
             left = jnp.concatenate([main[window, lanes], edge[window, lanes]], axis=1)
             spread = jnp.dot(left, columns[pair, block], preferred_element_type=F32)
-            position = lax.broadcasted_iota(jnp.int32, (SLICES, 128), 1) + 128 * block
             for half in range(2):
                 total = weighted(spread, rows_of.at[pair, block], half)
-                live = place[LENGTHS + 2 * pair + half] - start
-                total = jnp.where(position < live, total, 0.0)
                 stack[2 * step + half, SLICES * block : SLICES * block + SLICES, :] = total
         return carry
 
     lax.fori_loop(0, BAND // 2, one_pair, 0)
 
 
-def border_kernel(
-    place, from_left, from_right, wrap_columns, wrap_rows, stack, keep, send, edge, extra
-):
-    lane = lax.broadcasted_iota(jnp.int32, (GROUP, 128), 1)
-    left = from_left[...].astype(F32)
-    right = from_right[...].astype(F32)
-    for group in range(COUNT // GROUP):
-        one = pltpu.roll(right, (128 - 8 * group) % 128, 1)
-        two = pltpu.roll(left, 120 - 8 * group, 1)
-        edge[GROUP * group : GROUP * group + GROUP, :] = jnp.where(lane < 64, one, two).astype(BF16)
-    core = place[0]
-    start = place[1] * WIDE
+def border(steps, edge, wrap_columns, wrap_rows, stack, out):
+    core = lax.axis_index("wave") % 2
     column = lax.broadcasted_iota(jnp.int32, (SLICES, 128), 1)
-    position = jnp.where(column < 64, column, column + (WIDE - 128))
-
-    def one_pair(step, carry):
+    last = SLICES * (BLOCKS - 1)
+    for step in steps:
         pair = step ^ (2 * core)
         window = pl.ds(pl.multiple_of(pair * (2 * SLICES), 2 * SLICES), 18 * SLICES)
         spread = jnp.dot(edge[window, :], wrap_columns[pair], preferred_element_type=F32)
         for half in range(2):
-            total = weighted(spread, wrap_rows.at[pair], half)
-            live = place[LENGTHS + 2 * pair + half] - start
-            extra[2 * step + half] = jnp.where(position < live, total, 0.0)
-        return carry
-
-    lax.fori_loop(0, BAND // 2, one_pair, 0)
-    last = SLICES * (BLOCKS - 1)
-    for ref, first in ((keep, 0), (send, ROWS)):
-        for row in range(ROWS):
-            more = extra[first + row]
-            full = stack[first + row]
+            more = weighted(spread, wrap_rows.at[pair], half)
+            full = stack[2 * step + half]
             full = jnp.concatenate(
                 [
                     full[:SLICES] + jnp.where(column < 64, more, 0.0),
@@ -143,7 +119,22 @@
                 ],
                 axis=0,
             )
-            ref[row] = full.astype(BF16)
+            out[(2 * step + half) % ROWS] = full.astype(BF16)
+
+
+def border_send_kernel(from_left, from_right, wrap_columns, wrap_rows, stack, send, edge):
+    lane = lax.broadcasted_iota(jnp.int32, (GROUP, 128), 1)
+    left = from_left[...].astype(F32)
+    right = from_right[...].astype(F32)
+    for group in range(COUNT // GROUP):
+        one = pltpu.roll(right, (128 - 8 * group) % 128, 1)
+        two = pltpu.roll(left, 120 - 8 * group, 1)
+        edge[GROUP * group : GROUP * group + GROUP, :] = jnp.where(lane < 64, one, two).astype(BF16)
+    border((2, 3), edge, wrap_columns, wrap_rows, stack, send)
+
+
+def border_keep_kernel(edge, wrap_columns, wrap_rows, stack, keep):
+    border((0, 1), edge, wrap_columns, wrap_rows, stack, keep)
 
 
 def turn(count, length, inverse):
@@ -178,57 +169,60 @@
 def table_kernel(
     place, waves, stencil, inner, outer, columns, rows_of, wrap_columns, wrap_rows, points
 ):
+    wave_place = place[1]
     first_row = place[0] * ROWS
-    wave_place = place[1]
     step = lax.broadcasted_iota(jnp.int32, (8, 128), 0)
     away = ((wave_place ^ 1) - wave_place) * WIDE
     shift = jnp.where(step == 5, away, jnp.where(step == 6, 64, 128 * step + wave_place * WIDE))
     shift = shift.astype(F32)
     fine = step.astype(F32)
 
-    def one(index, carry):
-        row = index // SLOTS
-        slot = index % SLOTS
+    def one(row, carry):
         length = jnp.full((1, 128), place[LENGTHS + first_row + row], jnp.int32).astype(F32)
         inverse = 1.0 / length
-        wave = waves[pl.ds(slot, 1), :]
-        lanes = pl.ds(pl.multiple_of(slot * 256, 256), 128)
-        lanes_two = pl.ds(pl.multiple_of(slot * 256 + 128, 128), 128)
-        moved = turn(shift * wave, length, inverse)
         norm = lax.rsqrt(length)
-        outer[row, :, lanes] = moved[0] * norm
-        outer[row, :, lanes_two] = moved[1] * norm
-        other = [part[5:6] for part in moved]
-        half = [part[6:7] for part in moved]
-        small = turn(fine * wave, length, inverse)
-        low = turn(8.0 * fine * wave, length, inverse)
-        for tile in range(2):
-            if tile:
-                low = rotated(low, other)
-            high = rotated(low, half)
-            for coarse in range(0, 16, 2):
-                source = low if coarse < 8 else high
-                at = coarse % 8
-                pairs = [
-                    rotated([part[k : k + 1] for part in source], small) for k in (at, at + 1)
-                ]
-                rows = slice(128 * tile + 8 * coarse, 128 * tile + 8 * coarse + 16)
-                for side, to in enumerate((lanes, lanes_two)):
-                    inner[row, rows, to] = jnp.concatenate(
-                        [pair[side] for pair in pairs], axis=0
-                    ).astype(BF16)
+        for slot in range(SLOTS):
+            wave = waves[slot : slot + 1, :]
+            lanes = slice(slot * 256, slot * 256 + 128)
+            lanes_two = slice(slot * 256 + 128, slot * 256 + 256)
+            moved = turn(shift * wave, length, inverse)
+            outer[row, :, lanes] = moved[0] * norm
+            outer[row, :, lanes_two] = moved[1] * norm
+            other = [part[5:6] for part in moved]
+            half = [part[6:7] for part in moved]
+            small = turn(fine * wave, length, inverse)
+            low = turn(8.0 * fine * wave, length, inverse)
+            for tile in range(2):
+                if tile:
+                    low = rotated(low, other)
+                high = rotated(low, half)
+                for coarse in range(0, 16, 2):
+                    source = low if coarse < 8 else high
+                    at = coarse % 8
+                    pairs = [
+                        rotated([part[k : k + 1] for part in source], small) for k in (at, at + 1)
+                    ]
+                    rows = slice(128 * tile + 8 * coarse, 128 * tile + 8 * coarse + 16)
+                    for side, to in enumerate((lanes, lanes_two)):
+                        inner[row, rows, to] = jnp.concatenate(
+                            [pair[side] for pair in pairs], axis=0
+                        ).astype(BF16)
         return carry
 
-    lax.fori_loop(0, ROWS * SLOTS, one, 0)
-
-    lane = lax.broadcasted_iota(jnp.int32, (1, WIDE), 1) % 128
+    lax.fori_loop(0, ROWS, one, 0)
+
+    column = lax.broadcasted_iota(jnp.int32, (1, WIDE), 1)
+    lane = (column % 128).astype(F32)
     for base, first, fraction in (
-        (0, stencil[1] + (lane - 1).astype(F32), stencil[3]),
+        (0, stencil[1] + (lane - 1.0), stencil[3]),
         (8, stencil[0] + (BAND - 1.0), stencil[2]),
     ):
         for k, value in enumerate((first,) + cubic_weights(fraction)):
             for row in range(BAND):
-                points[row, base + k : base + k + 1, :] = value[row : row + 1, :]
+                part = value[row : row + 1, :]
+                if base and k:
+                    part = jnp.where(column < place[LENGTHS + row] - wave_place * WIDE, part, 0.0)
+                points[row, base + k : base + k + 1, :] = part
 
     def one_pair(pair, carry):
         def row_of(item, block):
@@ -241,13 +235,13 @@
             )
 
         for block in range(BLOCKS):
-            start = row_of(0, block)
-            weights = [row_of(1 + k, block) for k in range(4)]
-            source = lax.broadcasted_iota(jnp.int32, (144, 256), 0).astype(F32)
-            columns[pair, block, 0:144, :] = picked_weight(source - start, weights).astype(BF16)
+            start = row_of(0, block).astype(BF16)
+            weights = [row_of(1 + k, block).astype(BF16) for k in range(4)]
+            source = lax.broadcasted_iota(jnp.int32, (144, 256), 0).astype(F32).astype(BF16)
+            columns[pair, block, 0:144, :] = picked_weight(source - start, weights)
             columns[pair, block, 144:240, :] = jnp.zeros((96, 256), BF16)
             source = lax.broadcasted_iota(jnp.int32, (16, 256), 0).astype(F32) - 16.0
-            columns[pair, block, 240:256, :] = picked_weight(source - start, weights).astype(BF16)
+            columns[pair, block, 240:256, :] = picked_weight(source.astype(BF16) - start, weights)
             half = (lax.broadcasted_iota(jnp.int32, (1, 256), 1) >= 128).astype(F32)
             start = row_of(8, block) + half
             weights = [row_of(9 + k, block) for k in range(4)]
@@ -326,7 +320,10 @@
     bands = lax.axis_size("lat")
     first_slot = (lat_place * ring + wave_place) * SLOTS
     own_place = jnp.stack([wave_place % 2, wave_place, first_slot, lat_place % 2])
-    place = jnp.concatenate([own_place.astype(jnp.int32), row_length])
+    scalars = jnp.concatenate([own_place.astype(jnp.int32), row_length, wave_order])
+    scalars = lax.optimization_barrier(scalars)
+    place = scalars[: LENGTHS + BAND]
+    ordered = scalars[LENGTHS + BAND :].reshape(DEVICES, SLOTS).T.astype(F32)
     limit = place[LENGTHS:] - wave_place * WIDE
     live_mask = jnp.arange(WIDE, dtype=jnp.int32)[None, :] < limit[:, None]
     masked = jnp.where(live_mask[None], fields, jnp.zeros_like(fields))
@@ -340,7 +337,6 @@
     under = swapped(0)
 
     stencil = jnp.stack([depart_row.astype(F32), depart_col.astype(F32), frac_row, frac_col])
-    ordered = wave_order.reshape(DEVICES, SLOTS).T.astype(F32)
     inner, outer, columns, rows_of, wrap_columns, wrap_rows = pl.pallas_call(
         table_kernel,
         out_shape=(
@@ -366,34 +362,44 @@
             jax.ShapeDtypeStruct((GROUP, 128), BF16),
             jax.ShapeDtypeStruct((GROUP, 128), BF16),
         ),
-        in_specs=[SMEM] + [VMEM] * 3,
+        in_specs=[VMEM] * 3,
         out_specs=(VMEM,) * 3,
         compiler_params=pltpu.CompilerParams(vmem_limit_bytes=LIMIT),
         name="pack",
-    )(place, own, over, under)
+    )(own, over, under)
     from_left = lax.ppermute(to_right, "wave", [(i, (i + 1) % ring) for i in range(ring)])
     from_right = lax.ppermute(to_left, "wave", [((i + 1) % ring, i) for i in range(ring)])
     stack = pl.pallas_call(
         interior_kernel,
         out_shape=jax.ShapeDtypeStruct((BAND, STACK, 128), F32),
-        in_specs=[SMEM] + [VMEM] * 3,
+        in_specs=[VMEM] * 3,
         out_specs=VMEM,
         scratch_shapes=[pltpu.VMEM((COUNT, WIDE), BF16)],
         compiler_params=pltpu.CompilerParams(vmem_limit_bytes=LIMIT),
         cost_estimate=pl.CostEstimate(flops=5_000_000_000, bytes_accessed=3_000_000, transcendentals=0),
         name="interior",
-    )(place, main, columns, rows_of)
-    keep, send = pl.pallas_call(
-        border_kernel,
-        out_shape=(jax.ShapeDtypeStruct((ROWS, STACK, 128), BF16),) * 2,
-        in_specs=[SMEM] + [VMEM] * 5,
+    )(main, columns, rows_of)
+    send, edge = pl.pallas_call(
+        border_send_kernel,
+        out_shape=(
+            jax.ShapeDtypeStruct((ROWS, STACK, 128), BF16),
+            jax.ShapeDtypeStruct((COUNT, 128), BF16),
+        ),
+        in_specs=[VMEM] * 5,
         out_specs=(VMEM, VMEM),
-        scratch_shapes=[pltpu.VMEM((COUNT, 128), BF16), pltpu.VMEM((BAND, SLICES, 128), F32)],
-        compiler_params=pltpu.CompilerParams(vmem_limit_bytes=LIMIT),
-        name="border",
-    )(place, from_left, from_right, wrap_columns, wrap_rows, stack)
-
+        compiler_params=pltpu.CompilerParams(vmem_limit_bytes=LIMIT),
+        name="border_send",
+    )(from_left, from_right, wrap_columns, wrap_rows, stack)
     other = lax.ppermute(send, "wave", [(i, i ^ 1) for i in range(ring)])
+    keep = pl.pallas_call(
+        border_keep_kernel,
+        out_shape=jax.ShapeDtypeStruct((ROWS, STACK, 128), BF16),
+        in_specs=[VMEM] * 4,
+        out_specs=VMEM,
+        compiler_params=pltpu.CompilerParams(vmem_limit_bytes=LIMIT),
+        cost_estimate=pl.CostEstimate(flops=5_000_000_000, bytes_accessed=3_000_000, transcendentals=0),
+        name="border_keep",
+    )(edge, wrap_columns, wrap_rows, stack)
     message = pl.pallas_call(
         fourier_kernel,
         out_shape=jax.ShapeDtypeStruct((DEVICES * 16, 128), BF16),

time: 52.6 us -> 50 us (0.951)
  Pallas kernels: 14.8 us -> 11.1 us
  blocking collectives: 24.3 us -> 26.9 us
  other arithmetic: 3.93 us -> 2.73 us
  starting transfers between devices: 6.64 us -> 6.07 us
    all_to_all x1, blocking collectives: 24.3 us -> 26.9 us  [local(): lax.all_to_all(message.reshape(DEVICES, 16, 128), ('lat', 'wave'), split_...]
    pallas_call x1, Pallas kernels: 5.6 us -> 3.9 us  [local(): pl.pallas_call(table_kernel, out_shape=(jax.ShapeDtypeStruct((ROWS, 256,...]
    pallas_call x1 -> x2, Pallas kernels: 1.56 us -> 0.66 us  [the longest x1 0.39 us: local(): pl.pallas_call(border_send_kernel, out_shape=(jax.ShapeDtypeStruct((ROWS,...]
    convert_element_type x1, other arithmetic: 0.7 us -> 0.07 us  [local(): ordered = scalars[LENGTHS + BAND:].reshape(DEVICES, SLOTS).T.astype(F32)]
    sub x1, other arithmetic: 0.66 us -> 0.08 us  [local(): limit = place[LENGTHS:] - wave_place * WIDE]
    ppermute x1, starting transfers between devices: 1.28 us -> 0.71 us  [local(): other = lax.ppermute(send, 'wave', [(i, i ^ 1) for i in range(ring)])]
    pallas_call x1, Pallas kernels: 0.75 us -> 0.19 us  [local(): pl.pallas_call(pack_kernel, out_shape=(jax.ShapeDtypeStruct((COUNT, WIDE)...]
    pallas_call x1, Pallas kernels: 2.57 us -> 2.02 us  [local(): pl.pallas_call(interior_kernel, out_shape=jax.ShapeDtypeStruct((BAND, STA...]
  transfers between devices with their start and end apart: 5 -> 5, of which waited for: 2 -> 2; matrix products, arithmetic and copies ran while one was open for 6% -> 4% of each run, Pallas kernels for 16% -> 12%
where the time goes in v3:
time: 50 us; the launch traced here: 49.7 us
  blocking collectives  26.9 us (54%)
  Pallas kernels  11.1 us (22%)
  starting transfers between devices  6.07 us (12%)
  other arithmetic  2.73 us (5%)
  waiting for transfers between devices  1.8 us (4%)
  local copies, waits for them, and re-layouts  1.03 us (2%)
    all_to_all x1, blocking collectives, local(): lax.all_to_all(message.reshape(DEVICES, 16, 128), ('lat', 'wave'), split_...  26.9 us
    pallas_call x1, Pallas kernels, local(): pl.pallas_call(table_kernel, out_shape=(jax.ShapeDtypeStruct((ROWS, 256,...  3.9 us
    ppermute x2, starting transfers between devices, swapped(): return lax.ppermute(own, 'lat', pairs + [(j, i) for i, j in pairs])  2.87 us
    ppermute x1, starting transfers between devices, local(): lax.ppermute(to_right, 'wave', [(i, (i + 1) % ring) for i in range(ring)])  2.49 us
    pallas_call x1, Pallas kernels, local(): pl.pallas_call(legendre_kernel, out_shape=jax.ShapeDtypeStruct((SLOTS, 2...  2.46 us
    pallas_call x1, Pallas kernels, local(): pl.pallas_call(interior_kernel, out_shape=jax.ShapeDtypeStruct((BAND, STA...  2.02 us
    pallas_call x1, Pallas kernels, local(): pl.pallas_call(fourier_kernel, out_shape=jax.ShapeDtypeStruct((DEVICES *...  1.86 us
    another operation x2, other arithmetic, local(): jnp.stack([depart_row.astype(F32), depart_col.astype(F32), frac_row, frac...  1.53 us
  transfers between devices with their start and end apart: 5, of which 2 were waited for; matrix products, arithmetic and copies ran while one was open for 4% of the time, Pallas kernels for 12%

profile of v3, /device:TPU:1, one launch (start us, length us, event | category | flops | bytes accessed | tf_op | source)
XLA Modules:
  0.0 49.7 jit_solution(8825604574903832689)
XLA Ops:
  0.0 0.8 %concatenate.3 = s32[1292]{0:T(1024)S(1)} concatenate(s32[1]{0:T(128)} %bitcast, s32[1]{0:T(128)} %bitcast.1, s32[1]{0:T(128)} %bitcast.2, s32[1]{0:T(128)} %bitcast.3, s32[8]{0:T(128)} %param.9, s32[1280]{0:T(1024)} %waves.1), dimensions={0} | concatenate | bytes 10336 | tf_op jit(solution)/shard_map/concatenate | solution.py:323
  0.8 0.1 slice_subtract_fusion
  0.9 0.1 iota_compare_fusion
  0.9 1.0 %select_bitcast_fusion = bf16[8,24,640]{2,0,1:T(8,128)(2,1)S(1)} fusion(bf16[24,8,640]{2,1,0:T(8,128)(2,1)} %param.8, pred[8,640]{1,0:T(8,128)(4,1)S(1)} %iota_compare_fusion), kind=kLoop, calls=%fused_computation | loop fusion | flops 122880 | bytes 496640 | tf_op jit(solution)/shard_map/transpose | solution.py:330
  2.0 2.2 %collective-permute-start.1 = (bf16[192,640]{1,0:T(8,128)(2,1)S(1)}, bf16[192,640]{1,0:T(8,128)(2,1)S(1)}, u32[]{:S(2)}, u32[]{:S(2)}) collective-permute-start(bf16[192,640]{1,0:T(8,128)(2,1)S(1)} %bitcast.16), channel_id=1, source_target_pairs={{0,8},{16,24},{32,40},{48,56},{64,72},{80,88},{96,104},{112,120},{... | collective-permute-start | bytes 737288 | tf_op jit(solution)/shard_map/ppermute | solution.py:334
  4.2 0.7 %collective-permute-start = (bf16[192,640]{1,0:T(8,128)(2,1)S(1)}, bf16[192,640]{1,0:T(8,128)(2,1)S(1)}, u32[]{:S(2)}, u32[]{:S(2)}) collective-permute-start(bf16[192,640]{1,0:T(8,128)(2,1)S(1)} %bitcast.17), channel_id=1, source_target_pairs={{8,16},{24,32},{40,48},{56,64},{72,80},{88,96},{104,112},{16,8},{3... | collective-permute-start | bytes 737288 | tf_op jit(solution)/shard_map/ppermute | solution.py:334
  4.8 0.1 slice_convert_fusion
  4.9 0.1 convert_element_type.14
  5.1 0.1 copy.11
  5.1 0.8 %convert_bitcast_fusion = (f32[1,8,640]{2,1,0:T(8,128)S(1)}, f32[1,8,640]{2,1,0:T(8,128)S(1)}) fusion(s32[8,640]{1,0:T(8,128)} %param.12, s32[8,640]{1,0:T(8,128)} %param.11), kind=kLoop, calls=%fused_computation.2 | loop fusion | flops 10240 | bytes 81920 | tf_op jit(solution)/shard_map/stack | solution.py:339
  5.9 0.8 %pad_maximum_fusion.stencil = f32[4,8,640]{2,1,0:T(8,128)S(1)} fusion(f32[1,8,640]{2,1,0:T(8,128)} %bitcast.20, f32[1,8,640]{2,1,0:T(8,128)} %bitcast.21, f32[1,8,640]{2,1,0:T(8,128)S(1)} %get-tuple-element.27, f32[1,8,640]{2,1,0:T(8,128)S(1)} %get-tuple-element.28), kind=kLoop, calls=%fused_computation.1 | loop fusion | flops 61440 | bytes 163840 | tf_op jit(solution)/shard_map/stack | solution.py:339
  6.7 3.9 %tables.1 = (bf16[4,256,2560]{2,1,0:T(8,128)(2,1)S(1)}, f32[4,8,2560]{2,1,0:T(8,128)S(1)}, bf16[4,5,256,256]{3,2,1,0:T(8,128)(2,1)S(1)}, f32[4,5,24,256]{3,2,1,0...) custom-call(s32[12]{0:T(128)S(1)} %slice.13.place, f32[10,128]{1,0:T(8,128)S(1)} %bitcast.19, ...), custom_call_target="tpu_custom_call" | custom-call | flops 5000000000 | bytes 3000000 | tf_op jit(solution)/shard_map/tables/pallas_call | solution.py:340
  10.6 0.0 collective-permute-done.1.second
  10.6 0.2 pack.1
  10.8 2.5 %collective-permute-start.2 = (bf16[48,128]{1,0:T(8,128)(2,1)S(1)}, bf16[48,128]{1,0:T(8,128)(2,1)S(1)}, u32[]{:S(2)}, u32[]{:S(2)}) collective-permute-start(bf16[48,128]{1,0:T(8,128)(2,1)S(1)} %get-tuple-element.16), channel_id=1, source_target_pairs={{0,1},{1,2},{2,3},{3,4},{4,5},{5,6},{6,7},{7,0},{8,9},{9,10},{10,1... | collective-permute-start | bytes 36872 | tf_op jit(solution)/shard_map/ppermute | solution.py:370
  13.3 2.0 %interior.1.stack = f32[8,128,128]{2,1,0:T(8,128)S(1)} custom-call(bf16[576,640]{1,0:T(8,128)(2,1)S(1)} %get-tuple-element.20.main, bf16[4,5,256,256]{3,2,1,0:T(8,128)(2,1)S(1)} %get-tuple-element.21.columns, f32[4,5,24,256]{3,2,1,0:T(8,128)S(1)} %get-tuple-element.22.rows_of), custom_call_target="tpu_custom_call" | custom-call | flops 5000000000 | bytes 3000000 | tf_op jit(solution)/shard_map/interior/pallas_call | solution.py:372
  15.3 1.1 %collective-permute-done.3.from_right = bf16[48,128]{1,0:T(8,128)(2,1)S(1)} collective-permute-done((bf16[48,128]{1,0:T(8,128)(2,1)S(1)}, bf16[48,128]{1,0:T(8,128)(2,1)S(1)}, u32[]{:S(2)}, u32[]{:S(2)}) %collective-permute-start.3) | collective-permute-done | bytes 12320 | tf_op jit(solution)/shard_map/ppermute | solution.py:371
  16.4 0.4 border_send.1
  16.8 0.7 %collective-permute-start.4 = (bf16[4,128,128]{2,1,0:T(8,128)(2,1)S(1)}, bf16[4,128,128]{2,1,0:T(8,128)(2,1)S(1)}, u32[]{:S(2)}, u32[]{:S(2)}) collective-permute-start(bf16[4,128,128]{2,1,0:T(8,128)(2,1)S(1)} %get-tuple-element.24), channel_id=1, source_target_pairs={{0,1},{1,0},{2,3},{3,2},{4,5},{5,4},{6,7},{7,6},{8,9},{9,8},{10,11... | collective-permute-start | bytes 393224 | tf_op jit(solution)/shard_map/ppermute | solution.py:393
  17.5 0.3 border_keep.1.mine
  17.8 0.7 %collective-permute-done.4.other = bf16[4,128,128]{2,1,0:T(8,128)(2,1)S(1)} collective-permute-done((bf16[4,128,128]{2,1,0:T(8,128)(2,1)S(1)}, bf16[4,128,128]{2,1,0:T(8,128)(2,1)S(1)}, u32[]{:S(2)}, u32[]{:S(2)}) %collective-permute-start.4) | collective-permute-done | bytes 131104 | tf_op jit(solution)/shard_map/ppermute | solution.py:393
  18.5 1.9 %fourier.1 = bf16[2048,128]{1,0:T(8,128)(2,1)S(1)} custom-call(bf16[4,128,128]{2,1,0:T(8,128)(2,1)S(1)} %border_keep.1.mine, bf16[4,128,128]{2,1,0:T(8,128)(2,1)S(1)} %collective-permute-done.4.other, bf16[4,256,2560]{2,1,0:T(8,128)(2,1)S(1)} %get-tuple-element.25.inner, f32[4,8,2560]{2,1,0:T(8,128)S(1)} %get-tuple-element.26.outer), custom_call_target="tpu_custom_call" | custom-call | tf_op jit(solution)/shard_map/fourier/pallas_call | solution.py:403
  20.4 26.9 %all_to_all.5.message = bf16[128,16,128]{2,1,0:T(8,128)(2,1)S(1)} all-to-all(bf16[128,16,128]{2,1,0:T(8,128)(2,1)S(1)} %bitcast.15), channel_id=1, replica_groups=mesh['lat'=16,'wave'=8] {'lat','wave'}, dimensions={0} | all-to-all | bytes 1048576 | tf_op jit(solution)/shard_map/all_to_all | solution.py:415
  47.3 2.5 %legendre.1 = f32[10,48,1280]{2,1,0:T(8,128)} custom-call(s32[12]{0:T(128)S(1)} %slice.13.place, s32[1280]{0:T(1024)S(1)} %copy-done.1, bf16[128,16,128]{2,1,0:T(8,128)(2,1)S(1)} %all_to_all.5.message, bf16[10,128,1280]{2,1,0:T(8,128)(2,1)S(1)} %copy-done), custom_call_target="tpu_custom_call" | custom-call | tf_op jit(solution)/shard_map/legendre/pallas_call | solution.py:419
  (9 shorter events, 0.0 us)
Async XLA Ops:
  2.0 8.6 %collective-permute-start.1 = (bf16[192,640]{1,0:T(8,128)(2,1)S(1)}, bf16[192,640]{1,0:T(8,128)(2,1)S(1)}, u32[]{:S(2)}, u32[]{:S(2)}) collective-permute-start(bf16[192,640]{1,0:T(8,128)(2,1)S(1)} %bitcast.16), channel_id=1, source_target_pairs={{0,8},{16,24},{32,40},{48,56},{64,72},{80,88},{96,104},{112,120},{... | collective-permute-start | bytes 737288 | tf_op jit(solution)/shard_map/ppermute | solution.py:334
  4.2 6.4 %collective-permute-start = (bf16[192,640]{1,0:T(8,128)(2,1)S(1)}, bf16[192,640]{1,0:T(8,128)(2,1)S(1)}, u32[]{:S(2)}, u32[]{:S(2)}) collective-permute-start(bf16[192,640]{1,0:T(8,128)(2,1)S(1)} %bitcast.17), channel_id=1, source_target_pairs={{8,16},{24,32},{40,48},{56,64},{72,80},{88,96},{104,112},{16,8},{3... | collective-permute-start | bytes 737288 | tf_op jit(solution)/shard_map/ppermute | solution.py:334
  10.8 4.5 %collective-permute-start.2 = (bf16[48,128]{1,0:T(8,128)(2,1)S(1)}, bf16[48,128]{1,0:T(8,128)(2,1)S(1)}, u32[]{:S(2)}, u32[]{:S(2)}) collective-permute-start(bf16[48,128]{1,0:T(8,128)(2,1)S(1)} %get-tuple-element.16), channel_id=1, source_target_pairs={{0,1},{1,2},{2,3},{3,4},{4,5},{5,6},{6,7},{7,0},{8,9},{9,10},{10,1... | collective-permute-start | bytes 36872 | tf_op jit(solution)/shard_map/ppermute | solution.py:370
  13.3 3.1 %collective-permute-start.3 = (bf16[48,128]{1,0:T(8,128)(2,1)S(1)}, bf16[48,128]{1,0:T(8,128)(2,1)S(1)}, u32[]{:S(2)}, u32[]{:S(2)}) collective-permute-start(bf16[48,128]{1,0:T(8,128)(2,1)S(1)} %get-tuple-element.17), channel_id=1, source_target_pairs={{1,0},{2,1},{3,2},{4,3},{5,4},{6,5},{7,6},{0,7},{9,8},{10,9},{11,1... | collective-permute-start | bytes 36872 | tf_op jit(solution)/shard_map/ppermute | solution.py:371
  16.8 1.7 %collective-permute-start.4 = (bf16[4,128,128]{2,1,0:T(8,128)(2,1)S(1)}, bf16[4,128,128]{2,1,0:T(8,128)(2,1)S(1)}, u32[]{:S(2)}, u32[]{:S(2)}) collective-permute-start(bf16[4,128,128]{2,1,0:T(8,128)(2,1)S(1)} %get-tuple-element.24), channel_id=1, source_target_pairs={{0,1},{1,0},{2,3},{3,2},{4,5},{5,4},{6,7},{7,6},{8,9},{9,8},{10,11... | collective-permute-start | bytes 393224 | tf_op jit(solution)/shard_map/ppermute | solution.py:393
  18.5 28.8 %copy-start = (bf16[10,128,1280]{2,1,0:T(8,128)(2,1)S(1)}, bf16[10,128,1280]{2,1,0:T(8,128)(2,1)}, u32[]{:S(2)}) copy-start(bf16[10,128,1280]{2,1,0:T(8,128)(2,1)} %table.1) | copy-start | bytes 9830404
  18.5 28.8 %copy-start.1 = (s32[1280]{0:T(1024)S(1)}, s32[1280]{0:T(1024)}, u32[]{:S(2)}) copy-start(s32[1280]{0:T(1024)} %waves.1) | copy-start | bytes 15364

commit v4 on v3

v4 whole, which is shorter than its diff:
```python
import math

import jax
import jax.numpy as jnp
from jax import lax
from jax.experimental import pallas as pl
from jax.experimental.pallas import tpu as pltpu
from jax.sharding import PartitionSpec as P

F32 = jnp.float32
BF16 = jnp.bfloat16
VMEM = pl.BlockSpec(memory_space=pltpu.VMEM)
LIMIT = 24 * 1024 * 1024

SLICES = 24
BAND = 8
WIDE = 640
BLOCKS = 5
SLOTS = 10
DEVICES = 128
ROWS = 4
STACK = 144
COUNT = 3 * BAND * SLICES


def cubic_weights(fraction):
    return (
        -fraction * (fraction - 1.0) * (fraction - 2.0) / 6.0,
        (fraction + 1.0) * (fraction - 1.0) * (fraction - 2.0) / 2.0,
        -(fraction + 1.0) * fraction * (fraction - 2.0) / 2.0,
        (fraction + 1.0) * fraction * (fraction - 1.0) / 6.0,
    )


def picked_weight(distance, weights):
    chosen = jnp.where(distance == 3, weights[3], jnp.zeros_like(weights[3]))
    for step in (2, 1, 0):
        chosen = jnp.where(distance == step, weights[step], chosen)
    return chosen


def weighted(spread, rows_of, half):
    side = slice(128 * half, 128 * half + 128)
    total = jnp.zeros((SLICES, 128), F32)
    for row in range(half, half + 17):
        total = total + rows_of[row : row + 1, side] * spread[
            SLICES * row : SLICES * row + SLICES, side
        ]
    return total


def interpolate(steps, main, edge, columns, rows_of, wrap_columns, wrap_rows, out):
    core = lax.axis_index("wave") % 2
    for step in steps:
        pair = step ^ (2 * core)
        window = pl.ds(pl.multiple_of(pair * (2 * SLICES), 2 * SLICES), 18 * SLICES)
        totals = ([], [])
        for block in range(BLOCKS + 1):
            lanes = slice(128 * block, 128 * block + 128)
            if block < BLOCKS:
                left = jnp.concatenate([main[window, lanes], edge[window, lanes]], axis=1)
                table, rows = columns[pair, block], rows_of.at[pair, block]
            else:
                left, table, rows = edge[window, lanes], wrap_columns[pair], wrap_rows.at[pair]
            spread = jnp.dot(left, table, preferred_element_type=F32)
            for half in range(2):
                totals[half].append(weighted(spread, rows, half))
        for half in range(2):
            out[(2 * step + half) % ROWS] = jnp.concatenate(totals[half], axis=0).astype(BF16)


def send_kernel(
    own, first, second, columns, rows_of, wrap_columns, wrap_rows, send, main, edge
):
    size = BAND * SLICES
    odd = lax.axis_index("lat") % 2
    main[pl.ds(pl.multiple_of(odd * 2 * size, size), size), :] = first[...]
    main[size : 2 * size, :] = own[...]
    main[pl.ds(pl.multiple_of((1 - odd) * 2 * size, size), size), :] = second[...]
    nothing = jnp.zeros((COUNT, 64), BF16)
    for block in range(BLOCKS):
        at = 128 * block
        sides = [
            main[:, at + 128 : at + 192] if block < BLOCKS - 1 else nothing,
            main[:, at - 64 : at] if block else nothing,
        ]
        edge[:, at : at + 128] = jnp.concatenate(sides, axis=1)
    edge[:, WIDE:] = jnp.concatenate([main[:, :64], main[:, WIDE - 64 :]], axis=1)
    interpolate((2, 3), main, edge, columns, rows_of, wrap_columns, wrap_rows, send)


def keep_kernel(main, edge, columns, rows_of, wrap_columns, wrap_rows, keep):
    interpolate((0, 1), main, edge, columns, rows_of, wrap_columns, wrap_rows, keep)


def turn(count, length, inverse):
    whole = jnp.floor(count * inverse + 0.5)
    angle = (count - whole * length) * (inverse * math.pi)
    square = angle * angle
    sine = angle * (
        1.0
        + square
        * (
            -1.0 / 6
            + square
            * (1.0 / 120 + square * (-1.0 / 5040 + square * (1.0 / 362880 - square / 39916800)))
        )
    )
    cosine = 1.0 + square * (
        -0.5
        + square
        * (
            1.0 / 24
            + square
            * (-1.0 / 720 + square * (1.0 / 40320 + square * (-1.0 / 3628800 + square / 479001600)))
        )
    )
    return 1.0 - 2.0 * sine * sine, 2.0 * sine * cosine


def rotated(one, two):
    return one[0] * two[0] - one[1] * two[1], one[1] * two[0] + one[0] * two[1]


def ring_start(place):
    return lax.rem(place + 8, 8) * WIDE


def table_kernel(
    lengths, waves, stencil, from_left, from_right,
    inner, outer, columns, rows_of, wrap_columns, wrap_rows, own_waves,
    points, wrap_points, length_rows,
):
    wave_place = lax.axis_index("wave")
    core = wave_place % 2
    owner = lax.axis_index("lat") * 8 + wave_place
    lane = lax.broadcasted_iota(jnp.int32, (SLOTS, 128), 1)
    mine = jnp.sum(jnp.where(lane == owner, waves[...], 0.0), axis=1, keepdims=True)
    own_waves[...] = jnp.broadcast_to(mine, (SLOTS, 128))
    for row in range(BAND):
        length_rows[row] = lengths[row : row + 1, :]
    first_row = core * ROWS
    step = lax.broadcasted_iota(jnp.int32, (8, 128), 0)
    other_place = wave_place ^ 1
    away = (other_place - wave_place) * WIDE
    before = ring_start(wave_place - 1) + (WIDE - 128)
    behind = ring_start(wave_place + 1)
    other_before = ring_start(other_place - 1) + (WIDE - 128)
    other_behind = ring_start(other_place + 1)
    outside = jnp.where(core == 0, before, behind)
    other_outside = jnp.where(core == 0, other_behind, other_before) - away
    shift = 128 * step + wave_place * WIDE
    for at, value in ((5, outside), (6, other_outside), (7, away)):
        shift = jnp.where(step == at, value, shift)
    shift = shift.astype(F32)
    fine = step.astype(F32)

    def one(row, carry):
        length = length_rows[first_row + row]
        inverse = 1.0 / length
        norm = lax.rsqrt(length)
        for slot in range(SLOTS):
            wave = waves[slot : slot + 1, :]
            lanes = slice(slot * 256, slot * 256 + 128)
            lanes_two = slice(slot * 256 + 128, slot * 256 + 256)
            moved = turn(shift * wave, length, inverse)
            outer[row, :, lanes] = moved[0] * norm
            outer[row, :, lanes_two] = moved[1] * norm
            other = [part[7:8] for part in moved]
            small = turn(fine * wave, length, inverse)
            low = turn(8.0 * fine * wave, length, inverse)
            half = rotated([part[7:8] for part in low], [part[1:2] for part in low])
            for tile in range(2):
                if tile:
                    low = rotated(low, other)
                high = rotated(low, half)
                for coarse in range(0, 16, 2):
                    source = low if coarse < 8 else high
                    at = coarse % 8
                    pairs = [
                        rotated([part[k : k + 1] for part in source], small) for k in (at, at + 1)
                    ]
                    rows = slice(128 * tile + 8 * coarse, 128 * tile + 8 * coarse + 16)
                    for side, to in enumerate((lanes, lanes_two)):
                        inner[row, rows, to] = jnp.concatenate(
                            [pair[side] for pair in pairs], axis=0
                        ).astype(BF16)
        return carry

    lax.fori_loop(0, ROWS, one, 0)

    def spread_points(target, values, width, position):
        lane = (lax.broadcasted_iota(jnp.int32, (1, width), 1) % 128).astype(F32)
        limit = jnp.concatenate([lengths[...]] * (width // 128), axis=1)
        live = position.astype(F32) < limit
        for base, first, fraction in (
            (0, values[1] + (lane - 1.0), values[3]),
            (8, values[0] + (BAND - 1.0), values[2]),
        ):
            for k, value in enumerate((first,) + cubic_weights(fraction)):
                if base and k:
                    value = jnp.where(live, value, 0.0)
                for row in range(BAND):
                    target[row, base + k : base + k + 1, :] = value[row : row + 1, :]

    column = lax.broadcasted_iota(jnp.int32, (BAND, WIDE), 1)
    spread_points(points, [stencil[k] for k in range(4)], WIDE, column + wave_place * WIDE)
    column = lax.broadcasted_iota(jnp.int32, (BAND, 128), 1)
    values = [jnp.where(column < 64, from_right[k], from_left[k]) for k in range(4)]
    spread_points(wrap_points, values, 128, column + jnp.where(column < 64, behind, before))

    def one_pair(pair, carry):
        def row_of(ref, item, block):
            return jnp.concatenate(
                [
                    ref[2 * pair + half, item : item + 1, 128 * block : 128 * block + 128]
                    for half in range(2)
                ],
                axis=1,
            )

        def picks(ref, block):
            start = row_of(ref, 0, block).astype(BF16)
            weights = [row_of(ref, 1 + k, block).astype(BF16) for k in range(4)]

            def pick(count, first):
                source = lax.broadcasted_iota(jnp.int32, (count, 256), 0) + first
                return picked_weight(source.astype(F32).astype(BF16) - start, weights)

            return pick

        def row_table(ref, block):
            half = (lax.broadcasted_iota(jnp.int32, (1, 256), 1) >= 128).astype(F32)
            start = row_of(ref, 8, block) + half
            weights = [row_of(ref, 9 + k, block) for k in range(4)]
            source = lax.broadcasted_iota(jnp.int32, (24, 256), 0).astype(F32)
            return picked_weight(source - start, weights)

        for block in range(BLOCKS):
            pick = picks(points, block)
            columns[pair, block, 0:144, :] = pick(144, 0)
            columns[pair, block, 144:240, :] = jnp.zeros((96, 256), BF16)
            columns[pair, block, 240:256, :] = pick(16, -16)
            rows_of[pair, block] = row_table(points, block)
        pick = picks(wrap_points, 0)
        wrap_columns[pair, 0:16, :] = pick(16, 128)
        wrap_columns[pair, 16:112, :] = jnp.zeros((96, 256), BF16)
        wrap_columns[pair, 112:128, :] = pick(16, -16)
        wrap_rows[pair] = row_table(wrap_points, 0)
        return carry

    lax.fori_loop(0, BAND // 2, one_pair, 0)


def fourier_kernel(mine, other, inner, outer, message, sums, shuffled):
    odd = jnp.full((SLICES, 128), lax.axis_index("wave") % 2, jnp.int32).astype(F32)
    low = (lax.broadcasted_iota(jnp.int32, (SLICES, 128), 1) < 64).astype(F32)
    to_mine = (low * odd, (1.0 - low) * (1.0 - odd))
    to_other = (low * (1.0 - odd), (1.0 - low) * odd)
    last = SLICES * (BLOCKS - 1)
    nothing = jnp.zeros((SLICES, 128), F32)

    def one(row, carry):
        own = mine[row].astype(F32)
        far = other[row].astype(F32)
        own_wrap, far_wrap = own[last + SLICES :], far[last + SLICES :]
        halves = [
            [
                own[:SLICES] + far_wrap * to_mine[0],
                own[SLICES:last],
                own[last : last + SLICES] + far_wrap * to_mine[1],
                own_wrap * (to_mine[0] + to_mine[1]),
                nothing,
                nothing[:8],
            ],
            [
                far[:SLICES] + own_wrap * to_other[0],
                far[SLICES:last],
                far[last : last + SLICES] + own_wrap * to_other[1],
                nothing,
                far_wrap * (to_other[0] + to_other[1]),
                nothing[:8],
            ],
        ]
        left = jnp.concatenate([jnp.concatenate(half, axis=0) for half in halves], axis=1)
        left = left.astype(BF16)
        base = pl.multiple_of(row * 512, 512)
        sums[pl.ds(base + 480, 32), :] = jnp.zeros((32, 128), F32)
        for slot in range(SLOTS):
            lanes = slice(256 * slot, 256 * slot + 256)
            parts = jnp.dot(left, inner[row, :, lanes], preferred_element_type=F32)
            real = jnp.zeros((SLICES, 128), F32)
            imag = jnp.zeros((SLICES, 128), F32)
            for block in range(BLOCKS + 2):
                rows = slice(SLICES * block, SLICES * block + SLICES)
                cosine, sine = parts[rows, :128], parts[rows, 128:]
                c = outer[row, block : block + 1, 256 * slot : 256 * slot + 128]
                s = outer[row, block : block + 1, 256 * slot + 128 : 256 * slot + 256]
                real = real + (c * cosine - s * sine)
                imag = imag - (s * cosine + c * sine)
            sums[pl.ds(base + slot * 48, SLICES, stride=2), :] = real
            sums[pl.ds(base + slot * 48 + 1, SLICES, stride=2), :] = imag
        return carry

    lax.fori_loop(0, ROWS, one, 0)
    for part in range(16):
        shuffled[pl.ds(part, DEVICES, stride=16), :] = sums[128 * part : 128 * part + 128, :].T
    message[...] = shuffled[...].astype(BF16)


def legendre_kernel(waves, message, table, out, flat, sorted_rows, left, result, done):
    for band in range(16):
        for core in range(2):
            total = message[8 * band + core].astype(F32)
            for z in range(1, 4):
                total = total + message[8 * band + 2 * z + core].astype(F32)
            first = (2 * band + core) * 16
            flat[first : first + 16, :] = total
    for row in range(ROWS):
        for part in range(4):
            sorted_rows[pl.ds(128 * part + row, 32, stride=4), :] = flat[
                pl.ds(4 * row + part, 32, stride=16), :
            ]
    for part in range(4):
        rows = slice(128 * part, 128 * part + 128)
        left[rows, :] = sorted_rows[rows, :].T.astype(BF16)
    copies = []
    for slot in range(SLOTS):
        product = jnp.dot(left[48 * slot : 48 * slot + 48, :], table[slot], preferred_element_type=F32)
        wave = jnp.concatenate([waves[slot : slot + 1, :]] * (product.shape[1] // 128), axis=1)
        degree = lax.broadcasted_iota(jnp.int32, product.shape, 1).astype(F32)
        result[slot] = jnp.where(degree >= wave, product, 0.0)
        copy = pltpu.make_async_copy(result.at[slot], out.at[slot], done.at[slot])
        copy.start()
        copies.append(copy)
    for copy in copies:
        copy.wait()


def local(fields, row_length, wave_order, depart_row, depart_col, frac_row, frac_col, legendre):
    ring = lax.axis_size("wave")
    bands = lax.axis_size("lat")
    scalars = lax.optimization_barrier(jnp.concatenate([row_length, wave_order]))
    lengths = scalars[:BAND]
    ordered = scalars[BAND:].reshape(DEVICES, SLOTS).T.astype(F32)
    limit = lengths - lax.axis_index("wave") * WIDE
    live_mask = jnp.arange(WIDE, dtype=jnp.int32)[None, :] < limit[:, None]
    masked = jnp.where(live_mask[None], fields, jnp.zeros_like(fields))
    own = masked.transpose(1, 0, 2).reshape(BAND * SLICES, WIDE)

    def swapped(first):
        pairs = [(i, i + 1) for i in range(first, bands - 1, 2)]
        return lax.ppermute(own, "lat", pairs + [(j, i) for i, j in pairs])

    over = swapped(1)
    under = swapped(0)

    own, depart_row = lax.optimization_barrier((own, depart_row))
    stencil = jnp.stack([depart_row.astype(F32), depart_col.astype(F32), frac_row, frac_col])
    from_left = lax.ppermute(
        stencil[:, :, WIDE - 128 :], "wave", [(i, (i + 1) % ring) for i in range(ring)]
    )
    from_right = lax.ppermute(
        stencil[:, :, :128], "wave", [((i + 1) % ring, i) for i in range(ring)]
    )
    length_table = jnp.broadcast_to(lengths.astype(F32)[:, None], (BAND, 128))
    inner, outer, columns, rows_of, wrap_columns, wrap_rows, own_waves = pl.pallas_call(
        table_kernel,
        out_shape=(
            jax.ShapeDtypeStruct((ROWS, 256, SLOTS * 256), BF16),
            jax.ShapeDtypeStruct((ROWS, 8, SLOTS * 256), F32),
            jax.ShapeDtypeStruct((BAND // 2, BLOCKS, 256, 256), BF16),
            jax.ShapeDtypeStruct((BAND // 2, BLOCKS, 24, 256), F32),
            jax.ShapeDtypeStruct((BAND // 2, 128, 256), BF16),
            jax.ShapeDtypeStruct((BAND // 2, 24, 256), F32),
            jax.ShapeDtypeStruct((SLOTS, 128), F32),
        ),
        in_specs=[VMEM] * 5,
        out_specs=(VMEM,) * 7,
        scratch_shapes=[
            pltpu.VMEM((BAND, 16, WIDE), F32),
            pltpu.VMEM((BAND, 16, 128), F32),
            pltpu.VMEM((BAND, 1, 128), F32),
        ],
        compiler_params=pltpu.CompilerParams(vmem_limit_bytes=LIMIT),
        cost_estimate=pl.CostEstimate(flops=5_000_000_000, bytes_accessed=3_000_000, transcendentals=0),
        name="tables",
    )(length_table, ordered, stencil, from_left, from_right)

    weights = (columns, rows_of, wrap_columns, wrap_rows)
    part = jax.ShapeDtypeStruct((ROWS, STACK, 128), BF16)
    send, main, edge = pl.pallas_call(
        send_kernel,
        out_shape=(
            part,
            jax.ShapeDtypeStruct((COUNT, WIDE), BF16),
            jax.ShapeDtypeStruct((COUNT, WIDE + 128), BF16),
        ),
        in_specs=[VMEM] * 7,
        out_specs=(VMEM,) * 3,
        compiler_params=pltpu.CompilerParams(vmem_limit_bytes=LIMIT),
        name="interpolate_send",
    )(own, over, under, *weights)
    other = lax.ppermute(send, "wave", [(i, i ^ 1) for i in range(ring)])
    keep = pl.pallas_call(
        keep_kernel,
        out_shape=part,
        in_specs=[VMEM] * 6,
        out_specs=VMEM,
        compiler_params=pltpu.CompilerParams(vmem_limit_bytes=LIMIT),
        cost_estimate=pl.CostEstimate(flops=5_000_000_000, bytes_accessed=3_000_000, transcendentals=0),
        name="interpolate_keep",
    )(main, edge, *weights)
    message = pl.pallas_call(
        fourier_kernel,
        out_shape=jax.ShapeDtypeStruct((DEVICES * 16, 128), BF16),
        in_specs=[VMEM] * 4,
        out_specs=VMEM,
        scratch_shapes=[
            pltpu.VMEM((ROWS * 512, 128), F32),
            pltpu.VMEM((DEVICES * 16, 128), F32),
        ],
        compiler_params=pltpu.CompilerParams(vmem_limit_bytes=LIMIT),
        name="fourier",
    )(keep, other, inner, outer)
    message = lax.all_to_all(
        message.reshape(DEVICES, 16, 128), ("lat", "wave"), split_axis=0, concat_axis=0, tiled=True
    )
    degrees = legendre.shape[2]
    return pl.pallas_call(
        legendre_kernel,
        out_shape=jax.ShapeDtypeStruct((SLOTS, 2 * SLICES, degrees), F32),
        in_specs=[VMEM] * 3,
        out_specs=pl.BlockSpec(memory_space=pl.ANY),
        scratch_shapes=[
            pltpu.VMEM((512, 128), F32),
            pltpu.VMEM((512, 128), F32),
            pltpu.VMEM((512, 128), BF16),
            pltpu.VMEM((SLOTS, 2 * SLICES, degrees), F32),
            pltpu.SemaphoreType.DMA((SLOTS,)),
        ],
        compiler_params=pltpu.CompilerParams(vmem_limit_bytes=LIMIT),
        name="legendre",
    )(own_waves, message, legendre)


def solution(mesh):
    placed = (
        P(None, "lat", "wave"),
        P("lat"),
        P(),
        P("lat", "wave"),
        P("lat", "wave"),
        P("lat", "wave"),
        P("lat", "wave"),
        P(("lat", "wave"), None, None),
    )
    return jax.shard_map(
        local, mesh=mesh, in_specs=placed, out_specs=P(("lat", "wave"), None, None), check_vma=False
    )
```

time: 50 us -> 46.8 us (0.936)
  blocking collectives: 26.9 us -> 22 us
  starting transfers between devices: 6.07 us -> 9.15 us
  Pallas kernels: 11.1 us -> 9.39 us
  local copies, waits for them, and re-layouts: 1.03 us -> 0.3 us
  other arithmetic: 2.73 us -> 3.4 us
    all_to_all x1, blocking collectives: 26.9 us -> 22 us  [local(): lax.all_to_all(message.reshape(DEVICES, 16, 128), ('lat', 'wave'), split_...]
    ppermute x1, starting transfers between devices: 0.71 us -> 3.76 us  [local(): other = lax.ppermute(send, 'wave', [(i, i ^ 1) for i in range(ring)])]
    ppermute x2, waiting for transfers between devices: 1.08 us -> 2.05 us  [the longest x1 1.42 us: local(): lax.ppermute(stencil[:, :, :128], 'wave', [((i + 1) % ring, i) for i in r...]
    pallas_call x4 -> x2, Pallas kernels: 2.87 us -> 1.97 us  [the longest x1 1.1 us: local(): pl.pallas_call(send_kernel, out_shape=(part, jax.ShapeDtypeStruct((COUNT,...]
    concatenate x1 -> x0, local copies, waits for them, and re-layouts: 0.79 us -> none  [local(): jnp.concatenate([own_place.astype(jnp.int32), row_length, wave_order])]
    concatenate x0 -> x1, other arithmetic: none -> 0.77 us  [local(): jnp.concatenate([row_length, wave_order])]
    pallas_call x1, Pallas kernels: 2.46 us -> 1.86 us  [local(): pl.pallas_call(legendre_kernel, out_shape=jax.ShapeDtypeStruct((SLOTS, 2...]
    ppermute x1, waiting for transfers between devices: 0.71 us -> 0.13 us  [local(): other = lax.ppermute(send, 'wave', [(i, i ^ 1) for i in range(ring)])]
  transfers between devices with their start and end apart: 5 -> 5, of which waited for: 2 -> 3; matrix products, arithmetic and copies ran while one was open for 4% -> 4% of each run, Pallas kernels for 12% -> 9%
where the time goes in v4:
time: 46.8 us; the launch traced here: 46.5 us
  blocking collectives  22 us (47%)
  Pallas kernels  9.39 us (20%)
  starting transfers between devices  9.15 us (20%)
  other arithmetic  3.4 us (7%)
  waiting for transfers between devices  2.18 us (5%)
    all_to_all x1, blocking collectives, local(): lax.all_to_all(message.reshape(DEVICES, 16, 128), ('lat', 'wave'), split_...  22 us
    ppermute x1, starting transfers between devices, local(): other = lax.ppermute(send, 'wave', [(i, i ^ 1) for i in range(ring)])  3.76 us
    pallas_call x1, Pallas kernels, local(): pl.pallas_call(table_kernel, out_shape=(jax.ShapeDtypeStruct((ROWS, 256,...  3.44 us
    ppermute x2, starting transfers between devices, swapped(): return lax.ppermute(own, 'lat', pairs + [(j, i) for i, j in pairs])  2.87 us
    pallas_call x1, Pallas kernels, local(): pl.pallas_call(fourier_kernel, out_shape=jax.ShapeDtypeStruct((DEVICES *...  2.12 us
    pallas_call x1, Pallas kernels, local(): pl.pallas_call(legendre_kernel, out_shape=jax.ShapeDtypeStruct((SLOTS, 2...  1.86 us
    ppermute x1, starting transfers between devices, local(): lax.ppermute(stencil[:, :, WIDE - 128:], 'wave', [(i, (i + 1) % ring) for...  1.55 us
    another operation x2, other arithmetic, local(): jnp.stack([depart_row.astype(F32), depart_col.astype(F32), frac_row, frac...  1.51 us
  transfers between devices with their start and end apart: 5, of which 3 were waited for; matrix products, arithmetic and copies ran while one was open for 4% of the time, Pallas kernels for 9%

profile of v4, /device:TPU:1, one launch (start us, length us, event | category | flops | bytes accessed | tf_op | source)
XLA Modules:
  0.0 46.5 jit_solution(2178851619175115458)
XLA Ops:
  0.0 0.8 %pad_add_fusion = s32[1288]{0:T(1024)S(1)} fusion(s32[1280]{0:T(1024)} %param.10, s32[8]{0:T(128)} %param.9), kind=kLoop, calls=%fused_computation.6 | loop fusion | flops 1288 | bytes 10304 | tf_op jit(solution)/shard_map/concatenate | solution.py:343
  0.8 0.1 iota_compare_fusion
  0.9 1.0 %select_bitcast_fusion = bf16[8,24,640]{2,0,1:T(8,128)(2,1)S(1)} fusion(bf16[24,8,640]{2,1,0:T(8,128)(2,1)} %param.8, pred[8,640]{1,0:T(8,128)(4,1)S(1)} %iota_compare_fusion), kind=kLoop, calls=%fused_computation | loop fusion | flops 122880 | bytes 496640 | tf_op jit(solution)/shard_map/transpose | solution.py:349
  1.9 2.2 %collective-permute-start.3 = (bf16[192,640]{1,0:T(8,128)(2,1)S(1)}, bf16[192,640]{1,0:T(8,128)(2,1)S(1)}, u32[]{:S(2)}, u32[]{:S(2)}) collective-permute-start(bf16[192,640]{1,0:T(8,128)(2,1)S(1)} %bitcast.12), channel_id=1, source_target_pairs={{0,8},{16,24},{32,40},{48,56},{64,72},{80,88},{96,104},{112,120},{... | collective-permute-start | bytes 737288 | tf_op jit(solution)/shard_map/ppermute | solution.py:353
  4.1 0.7 %collective-permute-start.2 = (bf16[192,640]{1,0:T(8,128)(2,1)S(1)}, bf16[192,640]{1,0:T(8,128)(2,1)S(1)}, u32[]{:S(2)}, u32[]{:S(2)}) collective-permute-start(bf16[192,640]{1,0:T(8,128)(2,1)S(1)} %bitcast.13), channel_id=1, source_target_pairs={{8,16},{24,32},{40,48},{56,64},{72,80},{88,96},{104,112},{16,8},{3... | collective-permute-start | bytes 737288 | tf_op jit(solution)/shard_map/ppermute | solution.py:353
  4.7 0.8 %convert_bitcast_fusion = (f32[1,8,640]{2,1,0:T(8,128)S(1)}, f32[1,8,640]{2,1,0:T(8,128)S(1)}) fusion(s32[8,640]{1,0:T(8,128)} %param.12, s32[8,640]{1,0:T(8,128)} %param.11), kind=kLoop, calls=%fused_computation.2 | loop fusion | flops 10240 | bytes 81920 | tf_op jit(solution)/shard_map/stack | solution.py:359
  5.5 0.8 %pad_maximum_fusion.stencil = f32[4,8,640]{2,1,0:T(8,128)S(1)} fusion(f32[1,8,640]{2,1,0:T(8,128)} %bitcast.16, f32[1,8,640]{2,1,0:T(8,128)} %bitcast.17, f32[1,8,640]{2,1,0:T(8,128)S(1)} %get-tuple-element.33, f32[1,8,640]{2,1,0:T(8,128)S(1)} %get-tuple-element.34), kind=kLoop, calls=%fused_computation.1 | loop fusion | flops 61440 | bytes 163840 | tf_op jit(solution)/shard_map/stack | solution.py:359
  6.3 1.0 %collective-permute-start.1 = (f32[4,8,128]{2,1,0:T(8,128)S(1)}, f32[4,8,128]{2,1,0:T(8,128)S(1)}, u32[]{:S(2)}, u32[]{:S(2)}) collective-permute-start(f32[4,8,128]{2,1,0:T(8,128)S(1)} %get-tuple-element.29), channel_id=1, source_target_pairs={{1,0},{2,1},{3,2},{4,3},{5,4},{6,5},{7,6},{0,7},{9,8},{10,9},{11,1... | collective-permute-start | bytes 49160 | tf_op jit(solution)/shard_map/ppermute | solution.py:363
  7.2 1.5 %collective-permute-start = (f32[4,8,128]{2,1,0:T(8,128)S(1)}, f32[4,8,128]{2,1,0:T(8,128)S(1)}, u32[]{:S(2)}, u32[]{:S(2)}) collective-permute-start(f32[4,8,128]{2,1,0:T(8,128)S(1)} %get-tuple-element.30), channel_id=1, source_target_pairs={{0,1},{1,2},{2,3},{3,4},{4,5},{5,6},{6,7},{7,0},{8,9},{9,10},{10,1... | collective-permute-start | bytes 49160 | tf_op jit(solution)/shard_map/ppermute | solution.py:360
  8.8 0.1 slice_convert_fusion
  8.8 0.1 convert_element_type.18
  9.0 0.1 copy.10
  9.0 1.4 %collective-permute-done.1.from_right = f32[4,8,128]{2,1,0:T(8,128)S(1)} collective-permute-done((f32[4,8,128]{2,1,0:T(8,128)S(1)}, f32[4,8,128]{2,1,0:T(8,128)S(1)}, u32[]{:S(2)}, u32[]{:S(2)}) %collective-permute-start.1) | collective-permute-done | bytes 16416 | tf_op jit(solution)/shard_map/ppermute | solution.py:363
  10.5 0.6 %collective-permute-done.from_left = f32[4,8,128]{2,1,0:T(8,128)S(1)} collective-permute-done((f32[4,8,128]{2,1,0:T(8,128)S(1)}, f32[4,8,128]{2,1,0:T(8,128)S(1)}, u32[]{:S(2)}, u32[]{:S(2)}) %collective-permute-start) | collective-permute-done | bytes 16416 | tf_op jit(solution)/shard_map/ppermute | solution.py:360
  11.1 0.1 broadcast_in_dim.12.lengths
  11.2 3.4 %tables.1 = (bf16[4,256,2560]{2,1,0:T(8,128)(2,1)S(1)}, f32[4,8,2560]{2,1,0:T(8,128)S(1)}, bf16[4,5,256,256]{3,2,1,0:T(8,128)(2,1)S(1)}, f32[4,5,24,256]{3,2,1,0...) custom-call(f32[8,128]{1,0:T(8,128)S(1)} %broadcast_in_dim.12.lengths, ...), custom_call_target="tpu_custom_call" | custom-call | flops 5000000000 | bytes 3000000 | tf_op jit(solution)/shard_map/tables/pallas_call | solution.py:367
  14.6 0.0 collective-permute-done.2.first
  14.6 1.1 %interpolate_send.1 = (bf16[4,144,128]{2,1,0:T(8,128)(2,1)S(1)}, bf16[576,640]{1,0:T(8,128)(2,1)S(1)}, bf16[576,768]{1,0:T(8,128)(2,1)S(1)}) custom-call(bf16[192,640]{1,0:T(8,128)(2,1)S(1)} %bitcast.14, bf16[192,640]{1,0:T(8,128)(2,1)S(1)} %collective-permute-done.2.first, bf16[192,640]{1,0:T(8,128)(2,1)S(1)} %collective-permute-done.3.second, ...), custom_call_target="tpu_custom_call" | custom-call | tf_op jit(solution)/shard_map/interpolate_send/pallas_call | solution.py:392
  15.7 3.8 %collective-permute-start.4 = (bf16[4,144,128]{2,1,0:T(8,128)(2,1)S(1)}, bf16[4,144,128]{2,1,0:T(8,128)(2,1)S(1)}, u32[]{:S(2)}, u32[]{:S(2)}) collective-permute-start(bf16[4,144,128]{2,1,0:T(8,128)(2,1)S(1)} %get-tuple-element.26), channel_id=1, source_target_pairs={{0,1},{1,0},{2,3},{3,2},{4,5},{5,4},{6,7},{7,6},{8,9},{9,8},{10,11... | collective-permute-start | bytes 442376 | tf_op jit(solution)/shard_map/ppermute | solution.py:404
  19.5 0.9 %interpolate_keep.1.mine = bf16[4,144,128]{2,1,0:T(8,128)(2,1)S(1)} custom-call(bf16[576,640]{1,0:T(8,128)(2,1)S(1)} %get-tuple-element.24.main, bf16[576,768]{1,0:T(8,128)(2,1)S(1)} %get-tuple-element.25.edge, bf16[4,5,256,256]{3,2,1,0:T(8,128)(2,1)S(1)} %get-tuple-element.20.columns, f32[4,5,24,256]{3,2,1,0:T(8,128)S(1)} %get-tuple-element.21.rows_of, ...), custom_call_target="tpu_custom_call" | custom-call | flops 5000000000 | bytes 3000000 | tf_op jit(solution)/shard_map/interpolate_keep/pallas_call | solution.py:405
  20.4 0.1 collective-permute-done.4.other
  20.5 2.1 %fourier.1 = bf16[2048,128]{1,0:T(8,128)(2,1)S(1)} custom-call(bf16[4,144,128]{2,1,0:T(8,128)(2,1)S(1)} %interpolate_keep.1.mine, bf16[4,144,128]{2,1,0:T(8,128)(2,1)S(1)} %collective-permute-done.4.other, bf16[4,256,2560]{2,1,0:T(8,128)(2,1)S(1)} %get-tuple-element.27.inner, f32[4,8,2560]{2,1,0:T(8,128)S(1)} %get-tuple-element.28.outer), custom_call_target="tpu_custom_call" | custom-call | tf_op jit(solution)/shard_map/fourier/pallas_call | solution.py:414
  22.6 22.0 %all_to_all.5.message = bf16[128,16,128]{2,1,0:T(8,128)(2,1)S(1)} all-to-all(bf16[128,16,128]{2,1,0:T(8,128)(2,1)S(1)} %bitcast.11), channel_id=1, replica_groups=mesh['lat'=16,'wave'=8] {'lat','wave'}, dimensions={0} | all-to-all | bytes 1048576 | tf_op jit(solution)/shard_map/all_to_all | solution.py:426
  44.6 1.9 %legendre.1 = f32[10,48,1280]{2,1,0:T(8,128)} custom-call(f32[10,128]{1,0:T(8,128)S(1)} %get-tuple-element.18.waves, bf16[128,16,128]{2,1,0:T(8,128)(2,1)S(1)} %all_to_all.5.message, bf16[10,128,1280]{2,1,0:T(8,128)(2,1)S(1)} %copy-done), custom_call_target="tpu_custom_call" | custom-call | tf_op jit(solution)/shard_map/legendre/pallas_call | solution.py:430
  (6 shorter events, 0.0 us)
Async XLA Ops:
  1.9 12.8 %collective-permute-start.3 = (bf16[192,640]{1,0:T(8,128)(2,1)S(1)}, bf16[192,640]{1,0:T(8,128)(2,1)S(1)}, u32[]{:S(2)}, u32[]{:S(2)}) collective-permute-start(bf16[192,640]{1,0:T(8,128)(2,1)S(1)} %bitcast.12), channel_id=1, source_target_pairs={{0,8},{16,24},{32,40},{48,56},{64,72},{80,88},{96,104},{112,120},{... | collective-permute-start | bytes 737288 | tf_op jit(solution)/shard_map/ppermute | solution.py:353
  4.1 10.6 %collective-permute-start.2 = (bf16[192,640]{1,0:T(8,128)(2,1)S(1)}, bf16[192,640]{1,0:T(8,128)(2,1)S(1)}, u32[]{:S(2)}, u32[]{:S(2)}) collective-permute-start(bf16[192,640]{1,0:T(8,128)(2,1)S(1)} %bitcast.13), channel_id=1, source_target_pairs={{8,16},{24,32},{40,48},{56,64},{72,80},{88,96},{104,112},{16,8},{3... | collective-permute-start | bytes 737288 | tf_op jit(solution)/shard_map/ppermute | solution.py:353
  6.3 4.2 %collective-permute-start.1 = (f32[4,8,128]{2,1,0:T(8,128)S(1)}, f32[4,8,128]{2,1,0:T(8,128)S(1)}, u32[]{:S(2)}, u32[]{:S(2)}) collective-permute-start(f32[4,8,128]{2,1,0:T(8,128)S(1)} %get-tuple-element.29), channel_id=1, source_target_pairs={{1,0},{2,1},{3,2},{4,3},{5,4},{6,5},{7,6},{0,7},{9,8},{10,9},{11,1... | collective-permute-start | bytes 49160 | tf_op jit(solution)/shard_map/ppermute | solution.py:363
  7.2 3.9 %collective-permute-start = (f32[4,8,128]{2,1,0:T(8,128)S(1)}, f32[4,8,128]{2,1,0:T(8,128)S(1)}, u32[]{:S(2)}, u32[]{:S(2)}) collective-permute-start(f32[4,8,128]{2,1,0:T(8,128)S(1)} %get-tuple-element.30), channel_id=1, source_target_pairs={{0,1},{1,2},{2,3},{3,4},{4,5},{5,6},{6,7},{7,0},{8,9},{9,10},{10,1... | collective-permute-start | bytes 49160 | tf_op jit(solution)/shard_map/ppermute | solution.py:360
  15.7 4.8 %collective-permute-start.4 = (bf16[4,144,128]{2,1,0:T(8,128)(2,1)S(1)}, bf16[4,144,128]{2,1,0:T(8,128)(2,1)S(1)}, u32[]{:S(2)}, u32[]{:S(2)}) collective-permute-start(bf16[4,144,128]{2,1,0:T(8,128)(2,1)S(1)} %get-tuple-element.26), channel_id=1, source_target_pairs={{0,1},{1,0},{2,3},{3,2},{4,5},{5,4},{6,7},{7,6},{8,9},{9,8},{10,11... | collective-permute-start | bytes 442376 | tf_op jit(solution)/shard_map/ppermute | solution.py:404
  20.5 24.1 %copy-start = (bf16[10,128,1280]{2,1,0:T(8,128)(2,1)S(1)}, bf16[10,128,1280]{2,1,0:T(8,128)(2,1)}, u32[]{:S(2)}) copy-start(bf16[10,128,1280]{2,1,0:T(8,128)(2,1)} %table.1) | copy-start | bytes 9830404

commit v5 on v4

--- a/solution.py
+++ b/solution.py
@@ -126,10 +126,52 @@
     return lax.rem(place + 8, 8) * WIDE
 
 
+def spread_points(target, lengths, values, width, position):
+    lane = (lax.broadcasted_iota(jnp.int32, (1, width), 1) % 128).astype(F32)
+    limit = jnp.concatenate([lengths[...]] * (width // 128), axis=1)
+    live = position.astype(F32) < limit
+    for base, first, fraction in (
+        (0, values[1] + (lane - 1.0), values[3]),
+        (8, values[0] + (BAND - 1.0), values[2]),
+    ):
+        for k, value in enumerate((first,) + cubic_weights(fraction)):
+            if base and k:
+                value = jnp.where(live, value, 0.0)
+            for row in range(BAND):
+                target[row, base + k : base + k + 1, :] = value[row : row + 1, :]
+
+
+def row_of(ref, pair, item, block):
+    return jnp.concatenate(
+        [
+            ref[2 * pair + half, item : item + 1, 128 * block : 128 * block + 128]
+            for half in range(2)
+        ],
+        axis=1,
+    )
+
+
+def picks(ref, pair, block):
+    start = row_of(ref, pair, 0, block).astype(BF16)
+    weights = [row_of(ref, pair, 1 + k, block).astype(BF16) for k in range(4)]
+
+    def pick(count, first):
+        source = lax.broadcasted_iota(jnp.int32, (count, 256), 0) + first
+        return picked_weight(source.astype(F32).astype(BF16) - start, weights)
+
+    return pick
+
+
+def row_table(ref, pair, block):
+    half = (lax.broadcasted_iota(jnp.int32, (1, 256), 1) >= 128).astype(F32)
+    start = row_of(ref, pair, 8, block) + half
+    weights = [row_of(ref, pair, 9 + k, block) for k in range(4)]
+    source = lax.broadcasted_iota(jnp.int32, (24, 256), 0).astype(F32)
+    return picked_weight(source - start, weights)
+
+
 def table_kernel(
-    lengths, waves, stencil, from_left, from_right,
-    inner, outer, columns, rows_of, wrap_columns, wrap_rows, own_waves,
-    points, wrap_points, length_rows,
+    lengths, waves, stencil, inner, outer, columns, rows_of, own_waves, points, length_rows
 ):
     wave_place = lax.axis_index("wave")
     core = wave_place % 2
@@ -189,67 +231,36 @@
 
     lax.fori_loop(0, ROWS, one, 0)
 
-    def spread_points(target, values, width, position):
-        lane = (lax.broadcasted_iota(jnp.int32, (1, width), 1) % 128).astype(F32)
-        limit = jnp.concatenate([lengths[...]] * (width // 128), axis=1)
-        live = position.astype(F32) < limit
-        for base, first, fraction in (
-            (0, values[1] + (lane - 1.0), values[3]),
-            (8, values[0] + (BAND - 1.0), values[2]),
-        ):
-            for k, value in enumerate((first,) + cubic_weights(fraction)):
-                if base and k:
-                    value = jnp.where(live, value, 0.0)
-                for row in range(BAND):
-                    target[row, base + k : base + k + 1, :] = value[row : row + 1, :]
-
     column = lax.broadcasted_iota(jnp.int32, (BAND, WIDE), 1)
-    spread_points(points, [stencil[k] for k in range(4)], WIDE, column + wave_place * WIDE)
-    column = lax.broadcasted_iota(jnp.int32, (BAND, 128), 1)
-    values = [jnp.where(column < 64, from_right[k], from_left[k]) for k in range(4)]
-    spread_points(wrap_points, values, 128, column + jnp.where(column < 64, behind, before))
+    values = [stencil[k] for k in range(4)]
+    spread_points(points, lengths, values, WIDE, column + wave_place * WIDE)
 
     def one_pair(pair, carry):
-        def row_of(ref, item, block):
-            return jnp.concatenate(
-                [
-                    ref[2 * pair + half, item : item + 1, 128 * block : 128 * block + 128]
-                    for half in range(2)
-                ],
-                axis=1,
-            )
-
-        def picks(ref, block):
-            start = row_of(ref, 0, block).astype(BF16)
-            weights = [row_of(ref, 1 + k, block).astype(BF16) for k in range(4)]
-
-            def pick(count, first):
-                source = lax.broadcasted_iota(jnp.int32, (count, 256), 0) + first
-                return picked_weight(source.astype(F32).astype(BF16) - start, weights)
-
-            return pick
-
-        def row_table(ref, block):
-            half = (lax.broadcasted_iota(jnp.int32, (1, 256), 1) >= 128).astype(F32)
-            start = row_of(ref, 8, block) + half
-            weights = [row_of(ref, 9 + k, block) for k in range(4)]
-            source = lax.broadcasted_iota(jnp.int32, (24, 256), 0).astype(F32)
-            return picked_weight(source - start, weights)
-
         for block in range(BLOCKS):
-            pick = picks(points, block)
+            pick = picks(points, pair, block)
             columns[pair, block, 0:144, :] = pick(144, 0)
             columns[pair, block, 144:240, :] = jnp.zeros((96, 256), BF16)
             columns[pair, block, 240:256, :] = pick(16, -16)
-            rows_of[pair, block] = row_table(points, block)
-        pick = picks(wrap_points, 0)
+            rows_of[pair, block] = row_table(points, pair, block)
+        return carry
+
+    lax.fori_loop(0, BAND // 2, one_pair, 0)
+
+
+def wrap_kernel(lengths, from_left, from_right, wrap_columns, wrap_rows, points):
+    wave_place = lax.axis_index("wave")
+    before = ring_start(wave_place - 1) + (WIDE - 128)
+    behind = ring_start(wave_place + 1)
+    column = lax.broadcasted_iota(jnp.int32, (BAND, 128), 1)
+    values = [jnp.where(column < 64, from_right[k], from_left[k]) for k in range(4)]
+    position = column + jnp.where(column < 64, behind, before)
+    spread_points(points, lengths, values, 128, position)
+    for pair in range(BAND // 2):
+        pick = picks(points, pair, 0)
         wrap_columns[pair, 0:16, :] = pick(16, 128)
         wrap_columns[pair, 16:112, :] = jnp.zeros((96, 256), BF16)
         wrap_columns[pair, 112:128, :] = pick(16, -16)
-        wrap_rows[pair] = row_table(wrap_points, 0)
-        return carry
-
-    lax.fori_loop(0, BAND // 2, one_pair, 0)
+        wrap_rows[pair] = row_table(points, pair, 0)
 
 
 def fourier_kernel(mine, other, inner, outer, message, sums, shuffled):
@@ -342,7 +353,6 @@
     bands = lax.axis_size("lat")
     scalars = lax.optimization_barrier(jnp.concatenate([row_length, wave_order]))
     lengths = scalars[:BAND]
-    ordered = scalars[BAND:].reshape(DEVICES, SLOTS).T.astype(F32)
     limit = lengths - lax.axis_index("wave") * WIDE
     live_mask = jnp.arange(WIDE, dtype=jnp.int32)[None, :] < limit[:, None]
     masked = jnp.where(live_mask[None], fields, jnp.zeros_like(fields))
@@ -357,6 +367,8 @@
 
     own, depart_row = lax.optimization_barrier((own, depart_row))
     stencil = jnp.stack([depart_row.astype(F32), depart_col.astype(F32), frac_row, frac_col])
+    stencil, scalars = lax.optimization_barrier((stencil, scalars))
+    ordered = scalars[BAND:].reshape(DEVICES, SLOTS).T.astype(F32)
     from_left = lax.ppermute(
         stencil[:, :, WIDE - 128 :], "wave", [(i, (i + 1) % ring) for i in range(ring)]
     )
@@ -364,28 +376,34 @@
         stencil[:, :, :128], "wave", [((i + 1) % ring, i) for i in range(ring)]
     )
     length_table = jnp.broadcast_to(lengths.astype(F32)[:, None], (BAND, 128))
-    inner, outer, columns, rows_of, wrap_columns, wrap_rows, own_waves = pl.pallas_call(
+    inner, outer, columns, rows_of, own_waves = pl.pallas_call(
         table_kernel,
         out_shape=(
             jax.ShapeDtypeStruct((ROWS, 256, SLOTS * 256), BF16),
             jax.ShapeDtypeStruct((ROWS, 8, SLOTS * 256), F32),
             jax.ShapeDtypeStruct((BAND // 2, BLOCKS, 256, 256), BF16),
             jax.ShapeDtypeStruct((BAND // 2, BLOCKS, 24, 256), F32),
+            jax.ShapeDtypeStruct((SLOTS, 128), F32),
+        ),
+        in_specs=[VMEM] * 3,
+        out_specs=(VMEM,) * 5,
+        scratch_shapes=[pltpu.VMEM((BAND, 16, WIDE), F32), pltpu.VMEM((BAND, 1, 128), F32)],
+        compiler_params=pltpu.CompilerParams(vmem_limit_bytes=LIMIT),
+        cost_estimate=pl.CostEstimate(flops=5_000_000_000, bytes_accessed=3_000_000, transcendentals=0),
+        name="tables",
+    )(length_table, ordered, stencil)
+    wrap_columns, wrap_rows = pl.pallas_call(
+        wrap_kernel,
+        out_shape=(
             jax.ShapeDtypeStruct((BAND // 2, 128, 256), BF16),
             jax.ShapeDtypeStruct((BAND // 2, 24, 256), F32),
-            jax.ShapeDtypeStruct((SLOTS, 128), F32),
         ),
-        in_specs=[VMEM] * 5,
-        out_specs=(VMEM,) * 7,
-        scratch_shapes=[
-            pltpu.VMEM((BAND, 16, WIDE), F32),
-            pltpu.VMEM((BAND, 16, 128), F32),
-            pltpu.VMEM((BAND, 1, 128), F32),
-        ],
-        compiler_params=pltpu.CompilerParams(vmem_limit_bytes=LIMIT),
-        cost_estimate=pl.CostEstimate(flops=5_000_000_000, bytes_accessed=3_000_000, transcendentals=0),
-        name="tables",
-    )(length_table, ordered, stencil, from_left, from_right)
+        in_specs=[VMEM] * 3,
+        out_specs=(VMEM,) * 2,
+        scratch_shapes=[pltpu.VMEM((BAND, 16, 128), F32)],
+        compiler_params=pltpu.CompilerParams(vmem_limit_bytes=LIMIT),
+        name="wrap_tables",
+    )(length_table, from_left, from_right)
 
     weights = (columns, rows_of, wrap_columns, wrap_rows)
     part = jax.ShapeDtypeStruct((ROWS, STACK, 128), BF16)

time: 46.8 us -> 45.7 us (0.976)
  blocking collectives: 22 us -> 24.3 us
  waiting for transfers between devices: 2.18 us -> 0.14 us
  starting transfers between devices: 9.15 us -> 7.72 us
    all_to_all x1, blocking collectives: 22 us -> 24.3 us  [local(): lax.all_to_all(message.reshape(DEVICES, 16, 128), ('lat', 'wave'), split_...]
    ppermute x1, starting transfers between devices: 3.76 us -> 2.34 us  [local(): other = lax.ppermute(send, 'wave', [(i, i ^ 1) for i in range(ring)])]
    ppermute x1, waiting for transfers between devices: 1.42 us -> 0.01 us  [local(): lax.ppermute(stencil[:, :, :128], 'wave', [((i + 1) % ring, i) for i in r...]
    ppermute x1, waiting for transfers between devices: 0.63 us -> 0.01 us  [local(): lax.ppermute(stencil[:, :, WIDE - 128:], 'wave', [(i, (i + 1) % ring) for...]
  transfers between devices with their start and end apart: 5 -> 5, of which waited for: 3 -> 1; matrix products, arithmetic and copies ran while one was open for 4% -> 4% of each run, Pallas kernels for 9% -> 10%
where the time goes in v5:
time: 45.7 us; the launch traced here: 45.4 us
  blocking collectives  24.3 us (53%)
  Pallas kernels  9.41 us (21%)
  starting transfers between devices  7.72 us (17%)
  other arithmetic  3.4 us (7%)
    all_to_all x1, blocking collectives, local(): lax.all_to_all(message.reshape(DEVICES, 16, 128), ('lat', 'wave'), split_...  24.3 us
    pallas_call x1, Pallas kernels, local(): pl.pallas_call(table_kernel, out_shape=(jax.ShapeDtypeStruct((ROWS, 256,...  3.37 us
    ppermute x2, starting transfers between devices, swapped(): return lax.ppermute(own, 'lat', pairs + [(j, i) for i, j in pairs])  2.87 us
    ppermute x1, starting transfers between devices, local(): other = lax.ppermute(send, 'wave', [(i, i ^ 1) for i in range(ring)])  2.34 us
    pallas_call x1, Pallas kernels, local(): pl.pallas_call(fourier_kernel, out_shape=jax.ShapeDtypeStruct((DEVICES *...  2.12 us
    pallas_call x1, Pallas kernels, local(): pl.pallas_call(legendre_kernel, out_shape=jax.ShapeDtypeStruct((SLOTS, 2...  1.86 us
    ppermute x1, starting transfers between devices, local(): lax.ppermute(stencil[:, :, WIDE - 128:], 'wave', [(i, (i + 1) % ring) for...  1.55 us
    another operation x2, other arithmetic, local(): jnp.stack([depart_row.astype(F32), depart_col.astype(F32), frac_row, frac...  1.51 us
  transfers between devices with their start and end apart: 5, of which 1 were waited for; matrix products, arithmetic and copies ran while one was open for 4% of the time, Pallas kernels for 10%

profile of v5, /device:TPU:1, one launch (start us, length us, event | category | flops | bytes accessed | tf_op | source)
XLA Modules:
  0.0 45.4 jit_solution(7668695301489185107)
XLA Ops:
  0.0 0.8 %pad_add_fusion = s32[1288]{0:T(1024)S(1)} fusion(s32[1280]{0:T(1024)} %param.10, s32[8]{0:T(128)} %param.9), kind=kLoop, calls=%fused_computation.5 | loop fusion | flops 1288 | bytes 10304 | tf_op jit(solution)/shard_map/concatenate | solution.py:354
  0.8 0.1 iota_compare_fusion
  0.9 1.0 %select_bitcast_fusion = bf16[8,24,640]{2,0,1:T(8,128)(2,1)S(1)} fusion(bf16[24,8,640]{2,1,0:T(8,128)(2,1)} %param.8, pred[8,640]{1,0:T(8,128)(4,1)S(1)} %iota_compare_fusion), kind=kLoop, calls=%fused_computation | loop fusion | flops 122880 | bytes 496640 | tf_op jit(solution)/shard_map/transpose | solution.py:359
  1.9 2.2 %collective-permute-start.1 = (bf16[192,640]{1,0:T(8,128)(2,1)S(1)}, bf16[192,640]{1,0:T(8,128)(2,1)S(1)}, u32[]{:S(2)}, u32[]{:S(2)}) collective-permute-start(bf16[192,640]{1,0:T(8,128)(2,1)S(1)} %bitcast.12), channel_id=1, source_target_pairs={{0,8},{16,24},{32,40},{48,56},{64,72},{80,88},{96,104},{112,120},{... | collective-permute-start | bytes 737288 | tf_op jit(solution)/shard_map/ppermute | solution.py:363
  4.1 0.7 %collective-permute-start = (bf16[192,640]{1,0:T(8,128)(2,1)S(1)}, bf16[192,640]{1,0:T(8,128)(2,1)S(1)}, u32[]{:S(2)}, u32[]{:S(2)}) collective-permute-start(bf16[192,640]{1,0:T(8,128)(2,1)S(1)} %bitcast.13), channel_id=1, source_target_pairs={{8,16},{24,32},{40,48},{56,64},{72,80},{88,96},{104,112},{16,8},{3... | collective-permute-start | bytes 737288 | tf_op jit(solution)/shard_map/ppermute | solution.py:363
  4.7 0.8 %convert_bitcast_fusion = (f32[1,8,640]{2,1,0:T(8,128)S(1)}, f32[1,8,640]{2,1,0:T(8,128)S(1)}) fusion(s32[8,640]{1,0:T(8,128)} %param.12, s32[8,640]{1,0:T(8,128)} %param.11), kind=kLoop, calls=%fused_computation.2 | loop fusion | flops 10240 | bytes 81920 | tf_op jit(solution)/shard_map/stack | solution.py:369
  5.5 0.8 %pad_maximum_fusion.stencil = f32[4,8,640]{2,1,0:T(8,128)S(1)} fusion(f32[1,8,640]{2,1,0:T(8,128)} %bitcast.16, f32[1,8,640]{2,1,0:T(8,128)} %bitcast.17, f32[1,8,640]{2,1,0:T(8,128)S(1)} %get-tuple-element.37, f32[1,8,640]{2,1,0:T(8,128)S(1)} %get-tuple-element.38), kind=kLoop, calls=%fused_computation.1 | loop fusion | flops 61440 | bytes 163840 | tf_op jit(solution)/shard_map/stack | solution.py:369
  6.3 1.0 %collective-permute-start.3 = (f32[4,8,128]{2,1,0:T(8,128)S(1)}, f32[4,8,128]{2,1,0:T(8,128)S(1)}, u32[]{:S(2)}, u32[]{:S(2)}) collective-permute-start(f32[4,8,128]{2,1,0:T(8,128)S(1)} %get-tuple-element.33), channel_id=1, source_target_pairs={{1,0},{2,1},{3,2},{4,3},{5,4},{6,5},{7,6},{0,7},{9,8},{10,9},{11,1... | collective-permute-start | bytes 49160 | tf_op jit(solution)/shard_map/ppermute | solution.py:375
  7.2 1.5 %collective-permute-start.2 = (f32[4,8,128]{2,1,0:T(8,128)S(1)}, f32[4,8,128]{2,1,0:T(8,128)S(1)}, u32[]{:S(2)}, u32[]{:S(2)}) collective-permute-start(f32[4,8,128]{2,1,0:T(8,128)S(1)} %get-tuple-element.34), channel_id=1, source_target_pairs={{0,1},{1,2},{2,3},{3,4},{4,5},{5,6},{6,7},{7,0},{8,9},{9,10},{10,1... | collective-permute-start | bytes 49160 | tf_op jit(solution)/shard_map/ppermute | solution.py:372
  8.8 0.1 slice_convert_fusion
  8.8 0.1 convert_element_type.20
  9.0 0.1 copy.11
  9.0 0.1 broadcast_in_dim.12.lengths
  9.1 3.4 %tables.1 = (bf16[4,256,2560]{2,1,0:T(8,128)(2,1)S(1)}, f32[4,8,2560]{2,1,0:T(8,128)S(1)}, bf16[4,5,256,256]{3,2,1,0:T(8,128)(2,1)S(1)}, f32[4,5,24,256]{3,2,1,0:T(8,128)S(1)}, f32[10,128]{1,0:T(8,128)S(1)}) custom-call(f32[8,128]{1,0:T(8,128)S(1)} %broadcast_in_dim.12.lengths, f32[10,128]{1,0:T(8,128)S(1)} %bitcast.15, f32[4,8,640]{2,1,0:T(8,128)S(1)} %pad_maximum_fusion.stencil), custom_call_target="tpu_custom_call" | custom-call | flops 5000000000 | bytes 3000000 | tf_op jit(solution)/shard_map/tables/pallas_call | solution.py:379
  12.5 0.0 collective-permute-done.3.from_right
  12.5 0.1 wrap_tables.1
  12.6 0.0 collective-permute-done.1.second
  12.6 1.1 %interpolate_send.1 = (bf16[4,144,128]{2,1,0:T(8,128)(2,1)S(1)}, bf16[576,640]{1,0:T(8,128)(2,1)S(1)}, bf16[576,768]{1,0:T(8,128)(2,1)S(1)}) custom-call(bf16[192,640]{1,0:T(8,128)(2,1)S(1)} %bitcast.14, bf16[192,640]{1,0:T(8,128)(2,1)S(1)} %collective-permute-done.first, bf16[192,640]{1,0:T(8,128)(2,1)S(1)} %collective-permute-done.1.second, ...), custom_call_target="tpu_custom_call" | custom-call | tf_op jit(solution)/shard_map/interpolate_send/pallas_call | solution.py:410
  13.7 2.3 %collective-permute-start.4 = (bf16[4,144,128]{2,1,0:T(8,128)(2,1)S(1)}, bf16[4,144,128]{2,1,0:T(8,128)(2,1)S(1)}, u32[]{:S(2)}, u32[]{:S(2)}) collective-permute-start(bf16[4,144,128]{2,1,0:T(8,128)(2,1)S(1)} %get-tuple-element.30), channel_id=1, source_target_pairs={{0,1},{1,0},{2,3},{3,2},{4,5},{5,4},{6,7},{7,6},{8,9},{9,8},{10,11... | collective-permute-start | bytes 442376 | tf_op jit(solution)/shard_map/ppermute | solution.py:422
  16.1 0.9 %interpolate_keep.1.mine = bf16[4,144,128]{2,1,0:T(8,128)(2,1)S(1)} custom-call(bf16[576,640]{1,0:T(8,128)(2,1)S(1)} %get-tuple-element.28.main, bf16[576,768]{1,0:T(8,128)(2,1)S(1)} %get-tuple-element.29.edge, bf16[4,5,256,256]{3,2,1,0:T(8,128)(2,1)S(1)} %get-tuple-element.24.columns, f32[4,5,24,256]{3,2,1,0:T(8,128)S(1)} %get-tuple-element.25.rows_of, ...), custom_call_target="tpu_custom_call" | custom-call | flops 5000000000 | bytes 3000000 | tf_op jit(solution)/shard_map/interpolate_keep/pallas_call | solution.py:423
  17.0 0.1 collective-permute-done.4.other
  17.1 2.1 %fourier.1 = bf16[2048,128]{1,0:T(8,128)(2,1)S(1)} custom-call(bf16[4,144,128]{2,1,0:T(8,128)(2,1)S(1)} %interpolate_keep.1.mine, bf16[4,144,128]{2,1,0:T(8,128)(2,1)S(1)} %collective-permute-done.4.other, bf16[4,256,2560]{2,1,0:T(8,128)(2,1)S(1)} %get-tuple-element.31.inner, f32[4,8,2560]{2,1,0:T(8,128)S(1)} %get-tuple-element.32.outer), custom_call_target="tpu_custom_call" | custom-call | tf_op jit(solution)/shard_map/fourier/pallas_call | solution.py:432
  19.2 24.3 %all_to_all.5.message = bf16[128,16,128]{2,1,0:T(8,128)(2,1)S(1)} all-to-all(bf16[128,16,128]{2,1,0:T(8,128)(2,1)S(1)} %bitcast.11), channel_id=1, replica_groups=mesh['lat'=16,'wave'=8] {'lat','wave'}, dimensions={0} | all-to-all | bytes 1048576 | tf_op jit(solution)/shard_map/all_to_all | solution.py:444
  43.6 1.9 %legendre.1 = f32[10,48,1280]{2,1,0:T(8,128)} custom-call(f32[10,128]{1,0:T(8,128)S(1)} %get-tuple-element.22.waves, bf16[128,16,128]{2,1,0:T(8,128)(2,1)S(1)} %all_to_all.5.message, bf16[10,128,1280]{2,1,0:T(8,128)(2,1)S(1)} %copy-done), custom_call_target="tpu_custom_call" | custom-call | tf_op jit(solution)/shard_map/legendre/pallas_call | solution.py:448
  (7 shorter events, 0.0 us)
Async XLA Ops:
  1.9 10.8 %collective-permute-start.1 = (bf16[192,640]{1,0:T(8,128)(2,1)S(1)}, bf16[192,640]{1,0:T(8,128)(2,1)S(1)}, u32[]{:S(2)}, u32[]{:S(2)}) collective-permute-start(bf16[192,640]{1,0:T(8,128)(2,1)S(1)} %bitcast.12), channel_id=1, source_target_pairs={{0,8},{16,24},{32,40},{48,56},{64,72},{80,88},{96,104},{112,120},{... | collective-permute-start | bytes 737288 | tf_op jit(solution)/shard_map/ppermute | solution.py:363
  4.1 8.6 %collective-permute-start = (bf16[192,640]{1,0:T(8,128)(2,1)S(1)}, bf16[192,640]{1,0:T(8,128)(2,1)S(1)}, u32[]{:S(2)}, u32[]{:S(2)}) collective-permute-start(bf16[192,640]{1,0:T(8,128)(2,1)S(1)} %bitcast.13), channel_id=1, source_target_pairs={{8,16},{24,32},{40,48},{56,64},{72,80},{88,96},{104,112},{16,8},{3... | collective-permute-start | bytes 737288 | tf_op jit(solution)/shard_map/ppermute | solution.py:363
  6.3 6.2 %collective-permute-start.3 = (f32[4,8,128]{2,1,0:T(8,128)S(1)}, f32[4,8,128]{2,1,0:T(8,128)S(1)}, u32[]{:S(2)}, u32[]{:S(2)}) collective-permute-start(f32[4,8,128]{2,1,0:T(8,128)S(1)} %get-tuple-element.33), channel_id=1, source_target_pairs={{1,0},{2,1},{3,2},{4,3},{5,4},{6,5},{7,6},{0,7},{9,8},{10,9},{11,1... | collective-permute-start | bytes 49160 | tf_op jit(solution)/shard_map/ppermute | solution.py:375
  7.2 5.3 %collective-permute-start.2 = (f32[4,8,128]{2,1,0:T(8,128)S(1)}, f32[4,8,128]{2,1,0:T(8,128)S(1)}, u32[]{:S(2)}, u32[]{:S(2)}) collective-permute-start(f32[4,8,128]{2,1,0:T(8,128)S(1)} %get-tuple-element.34), channel_id=1, source_target_pairs={{0,1},{1,2},{2,3},{3,4},{4,5},{5,6},{6,7},{7,0},{8,9},{9,10},{10,1... | collective-permute-start | bytes 49160 | tf_op jit(solution)/shard_map/ppermute | solution.py:372
  13.7 3.3 %collective-permute-start.4 = (bf16[4,144,128]{2,1,0:T(8,128)(2,1)S(1)}, bf16[4,144,128]{2,1,0:T(8,128)(2,1)S(1)}, u32[]{:S(2)}, u32[]{:S(2)}) collective-permute-start(bf16[4,144,128]{2,1,0:T(8,128)(2,1)S(1)} %get-tuple-element.30), channel_id=1, source_target_pairs={{0,1},{1,0},{2,3},{3,2},{4,5},{5,4},{6,7},{7,6},{8,9},{9,8},{10,11... | collective-permute-start | bytes 442376 | tf_op jit(solution)/shard_map/ppermute | solution.py:422
  17.1 26.5 %copy-start = (bf16[10,128,1280]{2,1,0:T(8,128)(2,1)S(1)}, bf16[10,128,1280]{2,1,0:T(8,128)(2,1)}, u32[]{:S(2)}) copy-start(bf16[10,128,1280]{2,1,0:T(8,128)(2,1)} %table.1) | copy-start | bytes 9830404

commit v6 on v5

--- a/solution.py
+++ b/solution.py
@@ -17,7 +17,8 @@
 WIDE = 640
 BLOCKS = 5
 SLOTS = 10
-DEVICES = 128
+PEERS = 64
+GROUPS = 5
 ROWS = 4
 STACK = 144
 COUNT = 3 * BAND * SLICES
@@ -50,10 +51,8 @@
 
 
 def interpolate(steps, main, edge, columns, rows_of, wrap_columns, wrap_rows, out):
-    core = lax.axis_index("wave") % 2
-    for step in steps:
-        pair = step ^ (2 * core)
-        window = pl.ds(pl.multiple_of(pair * (2 * SLICES), 2 * SLICES), 18 * SLICES)
+    for pair in steps:
+        window = slice(pair * 2 * SLICES, pair * 2 * SLICES + 18 * SLICES)
         totals = ([], [])
         for block in range(BLOCKS + 1):
             lanes = slice(128 * block, 128 * block + 128)
@@ -66,11 +65,11 @@
             for half in range(2):
                 totals[half].append(weighted(spread, rows, half))
         for half in range(2):
-            out[(2 * step + half) % ROWS] = jnp.concatenate(totals[half], axis=0).astype(BF16)
-
-
-def send_kernel(
-    own, first, second, columns, rows_of, wrap_columns, wrap_rows, send, main, edge
+            out[(2 * pair + half) % ROWS] = jnp.concatenate(totals[half], axis=0).astype(BF16)
+
+
+def upper_kernel(
+    own, first, second, columns, rows_of, wrap_columns, wrap_rows, out, main, edge
 ):
     size = BAND * SLICES
     odd = lax.axis_index("lat") % 2
@@ -86,11 +85,11 @@
         ]
         edge[:, at : at + 128] = jnp.concatenate(sides, axis=1)
     edge[:, WIDE:] = jnp.concatenate([main[:, :64], main[:, WIDE - 64 :]], axis=1)
-    interpolate((2, 3), main, edge, columns, rows_of, wrap_columns, wrap_rows, send)
-
-
-def keep_kernel(main, edge, columns, rows_of, wrap_columns, wrap_rows, keep):
-    interpolate((0, 1), main, edge, columns, rows_of, wrap_columns, wrap_rows, keep)
+    interpolate((0, 1), main, edge, columns, rows_of, wrap_columns, wrap_rows, out)
+
+
+def lower_kernel(main, edge, columns, rows_of, wrap_columns, wrap_rows, out):
+    interpolate((2, 3), main, edge, columns, rows_of, wrap_columns, wrap_rows, out)
 
 
 def turn(count, length, inverse):
@@ -175,13 +174,17 @@
 ):
     wave_place = lax.axis_index("wave")
     core = wave_place % 2
-    owner = lax.axis_index("lat") * 8 + wave_place
-    lane = lax.broadcasted_iota(jnp.int32, (SLOTS, 128), 1)
-    mine = jnp.sum(jnp.where(lane == owner, waves[...], 0.0), axis=1, keepdims=True)
+    peer = lax.axis_index("lat") * 4 + wave_place // 2
+    slots = jnp.where(core == 0, waves[:SLOTS, :], waves[SLOTS:, :])
+    lane = lax.broadcasted_iota(jnp.int32, (SLOTS, PEERS), 1)
+    mine = jnp.sum(jnp.where(lane == peer, slots, 0.0), axis=1, keepdims=True)
     own_waves[...] = jnp.broadcast_to(mine, (SLOTS, 128))
+    groups = [
+        jnp.concatenate([slots[k : k + 1], slots[k + 1 : k + 2]], axis=1)
+        for k in range(0, SLOTS, 2)
+    ]
     for row in range(BAND):
         length_rows[row] = lengths[row : row + 1, :]
-    first_row = core * ROWS
     step = lax.broadcasted_iota(jnp.int32, (8, 128), 0)
     other_place = wave_place ^ 1
     away = (other_place - wave_place) * WIDE
@@ -198,13 +201,12 @@
     fine = step.astype(F32)
 
     def one(row, carry):
-        length = length_rows[first_row + row]
+        length = length_rows[row]
         inverse = 1.0 / length
         norm = lax.rsqrt(length)
-        for slot in range(SLOTS):
-            wave = waves[slot : slot + 1, :]
-            lanes = slice(slot * 256, slot * 256 + 128)
-            lanes_two = slice(slot * 256 + 128, slot * 256 + 256)
+        for group, wave in enumerate(groups):
+            lanes = slice(group * 256, group * 256 + 128)
+            lanes_two = slice(group * 256 + 128, group * 256 + 256)
             moved = turn(shift * wave, length, inverse)
             outer[row, :, lanes] = moved[0] * norm
             outer[row, :, lanes_two] = moved[1] * norm
@@ -229,7 +231,7 @@
                         ).astype(BF16)
         return carry
 
-    lax.fori_loop(0, ROWS, one, 0)
+    lax.fori_loop(0, BAND, one, 0)
 
     column = lax.broadcasted_iota(jnp.int32, (BAND, WIDE), 1)
     values = [stencil[k] for k in range(4)]
@@ -263,7 +265,7 @@
         wrap_rows[pair] = row_table(points, pair, 0)
 
 
-def fourier_kernel(mine, other, inner, outer, message, sums, shuffled):
+def fourier(first, mine, other, inner, outer, sums, shuffled):
     odd = jnp.full((SLICES, 128), lax.axis_index("wave") % 2, jnp.int32).astype(F32)
     low = (lax.broadcasted_iota(jnp.int32, (SLICES, 128), 1) < 64).astype(F32)
     to_mine = (low * odd, (1.0 - low) * (1.0 - odd))
@@ -271,7 +273,7 @@
     last = SLICES * (BLOCKS - 1)
     nothing = jnp.zeros((SLICES, 128), F32)
 
-    def one(row, carry):
+    for row in range(ROWS):
         own = mine[row].astype(F32)
         far = other[row].astype(F32)
         own_wrap, far_wrap = own[last + SLICES :], far[last + SLICES :]
@@ -295,49 +297,60 @@
         ]
         left = jnp.concatenate([jnp.concatenate(half, axis=0) for half in halves], axis=1)
         left = left.astype(BF16)
-        base = pl.multiple_of(row * 512, 512)
-        sums[pl.ds(base + 480, 32), :] = jnp.zeros((32, 128), F32)
-        for slot in range(SLOTS):
-            lanes = slice(256 * slot, 256 * slot + 256)
-            parts = jnp.dot(left, inner[row, :, lanes], preferred_element_type=F32)
+        base = 256 * row
+        sums[base + 240 : base + 256, :] = jnp.zeros((16, 128), F32)
+        for group in range(GROUPS):
+            lanes = slice(256 * group, 256 * group + 256)
+            parts = jnp.dot(left, inner[first + row, :, lanes], preferred_element_type=F32)
             real = jnp.zeros((SLICES, 128), F32)
             imag = jnp.zeros((SLICES, 128), F32)
             for block in range(BLOCKS + 2):
                 rows = slice(SLICES * block, SLICES * block + SLICES)
                 cosine, sine = parts[rows, :128], parts[rows, 128:]
-                c = outer[row, block : block + 1, 256 * slot : 256 * slot + 128]
-                s = outer[row, block : block + 1, 256 * slot + 128 : 256 * slot + 256]
+                factor = outer[first + row, block : block + 1, lanes]
+                c, s = factor[:, :128], factor[:, 128:]
                 real = real + (c * cosine - s * sine)
                 imag = imag - (s * cosine + c * sine)
-            sums[pl.ds(base + slot * 48, SLICES, stride=2), :] = real
-            sums[pl.ds(base + slot * 48 + 1, SLICES, stride=2), :] = imag
-        return carry
-
-    lax.fori_loop(0, ROWS, one, 0)
-    for part in range(16):
-        shuffled[pl.ds(part, DEVICES, stride=16), :] = sums[128 * part : 128 * part + 128, :].T
+            sums[pl.ds(base + group * 48, SLICES, stride=2), :] = real
+            sums[pl.ds(base + group * 48 + 1, SLICES, stride=2), :] = imag
+        for half in range(2):
+            turned = sums[base + 128 * half : base + 128 * half + 128, :].T
+            for side in range(2):
+                at = 4 * row + 2 * side + half
+                shuffled[pl.ds(at, PEERS, stride=16), :] = turned[PEERS * side : PEERS * side + PEERS]
+
+
+def upper_fourier_kernel(mine, other, inner, outer, message, sums, shuffled):
+    fourier(0, mine, other, inner, outer, sums, shuffled)
     message[...] = shuffled[...].astype(BF16)
+
+
+def lower_fourier_kernel(mine, other, inner, outer, upper, message, sums, shuffled):
+    fourier(ROWS, mine, other, inner, outer, sums, shuffled)
+    for peer in range(PEERS):
+        rows = slice(16 * peer, 16 * peer + 16)
+        message[32 * peer : 32 * peer + 16, :] = upper[rows, :]
+        message[32 * peer + 16 : 32 * peer + 32, :] = shuffled[rows, :].astype(BF16)
 
 
 def legendre_kernel(waves, message, table, out, flat, sorted_rows, left, result, done):
     for band in range(16):
-        for core in range(2):
-            total = message[8 * band + core].astype(F32)
-            for z in range(1, 4):
-                total = total + message[8 * band + 2 * z + core].astype(F32)
-            first = (2 * band + core) * 16
-            flat[first : first + 16, :] = total
-    for row in range(ROWS):
+        total = message[4 * band].astype(F32)
+        for z in range(1, 4):
+            total = total + message[4 * band + z].astype(F32)
+        flat[32 * band : 32 * band + 32, :] = total
+    for row in range(BAND):
         for part in range(4):
-            sorted_rows[pl.ds(128 * part + row, 32, stride=4), :] = flat[
-                pl.ds(4 * row + part, 32, stride=16), :
+            sorted_rows[pl.ds(128 * part + row, 16, stride=8), :] = flat[
+                pl.ds(4 * row + part, 16, stride=32), :
             ]
     for part in range(4):
         rows = slice(128 * part, 128 * part + 128)
         left[rows, :] = sorted_rows[rows, :].T.astype(BF16)
     copies = []
     for slot in range(SLOTS):
-        product = jnp.dot(left[48 * slot : 48 * slot + 48, :], table[slot], preferred_element_type=F32)
+        first = 256 * (slot % 2) + 48 * (slot // 2)
+        product = jnp.dot(left[first : first + 48, :], table[slot], preferred_element_type=F32)
         wave = jnp.concatenate([waves[slot : slot + 1, :]] * (product.shape[1] // 128), axis=1)
         degree = lax.broadcasted_iota(jnp.int32, product.shape, 1).astype(F32)
         result[slot] = jnp.where(degree >= wave, product, 0.0)
@@ -368,7 +381,7 @@
     own, depart_row = lax.optimization_barrier((own, depart_row))
     stencil = jnp.stack([depart_row.astype(F32), depart_col.astype(F32), frac_row, frac_col])
     stencil, scalars = lax.optimization_barrier((stencil, scalars))
-    ordered = scalars[BAND:].reshape(DEVICES, SLOTS).T.astype(F32)
+    ordered = scalars[BAND:].reshape(PEERS, 2 * SLOTS).T.astype(F32)
     from_left = lax.ppermute(
         stencil[:, :, WIDE - 128 :], "wave", [(i, (i + 1) % ring) for i in range(ring)]
     )
@@ -379,8 +392,8 @@
     inner, outer, columns, rows_of, own_waves = pl.pallas_call(
         table_kernel,
         out_shape=(
-            jax.ShapeDtypeStruct((ROWS, 256, SLOTS * 256), BF16),
-            jax.ShapeDtypeStruct((ROWS, 8, SLOTS * 256), F32),
+            jax.ShapeDtypeStruct((BAND, 256, GROUPS * 256), BF16),
+            jax.ShapeDtypeStruct((BAND, 8, GROUPS * 256), F32),
             jax.ShapeDtypeStruct((BAND // 2, BLOCKS, 256, 256), BF16),
             jax.ShapeDtypeStruct((BAND // 2, BLOCKS, 24, 256), F32),
             jax.ShapeDtypeStruct((SLOTS, 128), F32),
@@ -407,8 +420,8 @@
 
     weights = (columns, rows_of, wrap_columns, wrap_rows)
     part = jax.ShapeDtypeStruct((ROWS, STACK, 128), BF16)
-    send, main, edge = pl.pallas_call(
-        send_kernel,
+    upper, main, edge = pl.pallas_call(
+        upper_kernel,
         out_shape=(
             part,
             jax.ShapeDtypeStruct((COUNT, WIDE), BF16),
@@ -417,32 +430,47 @@
         in_specs=[VMEM] * 7,
         out_specs=(VMEM,) * 3,
         compiler_params=pltpu.CompilerParams(vmem_limit_bytes=LIMIT),
-        name="interpolate_send",
+        name="interpolate_upper",
     )(own, over, under, *weights)
-    other = lax.ppermute(send, "wave", [(i, i ^ 1) for i in range(ring)])
-    keep = pl.pallas_call(
-        keep_kernel,
+    cores = [(i, i ^ 1) for i in range(ring)]
+    other_upper = lax.ppermute(upper, "wave", cores)
+    lower = pl.pallas_call(
+        lower_kernel,
         out_shape=part,
         in_specs=[VMEM] * 6,
         out_specs=VMEM,
         compiler_params=pltpu.CompilerParams(vmem_limit_bytes=LIMIT),
         cost_estimate=pl.CostEstimate(flops=5_000_000_000, bytes_accessed=3_000_000, transcendentals=0),
-        name="interpolate_keep",
+        name="interpolate_lower",
     )(main, edge, *weights)
+    other_lower = lax.ppermute(lower, "wave", cores)
+    scratch = [pltpu.VMEM((ROWS * 256, 128), F32), pltpu.VMEM((PEERS * 16, 128), F32)]
     message = pl.pallas_call(
-        fourier_kernel,
-        out_shape=jax.ShapeDtypeStruct((DEVICES * 16, 128), BF16),
+        upper_fourier_kernel,
+        out_shape=jax.ShapeDtypeStruct((PEERS * 16, 128), BF16),
         in_specs=[VMEM] * 4,
         out_specs=VMEM,
-        scratch_shapes=[
-            pltpu.VMEM((ROWS * 512, 128), F32),
-            pltpu.VMEM((DEVICES * 16, 128), F32),
-        ],
-        compiler_params=pltpu.CompilerParams(vmem_limit_bytes=LIMIT),
-        name="fourier",
-    )(keep, other, inner, outer)
+        scratch_shapes=scratch,
+        compiler_params=pltpu.CompilerParams(vmem_limit_bytes=LIMIT),
+        cost_estimate=pl.CostEstimate(flops=5_000_000_000, bytes_accessed=3_000_000, transcendentals=0),
+        name="fourier_upper",
+    )(upper, other_upper, inner, outer)
+    message = pl.pallas_call(
+        lower_fourier_kernel,
+        out_shape=jax.ShapeDtypeStruct((PEERS * 32, 128), BF16),
+        in_specs=[VMEM] * 5,
+        out_specs=VMEM,
+        scratch_shapes=scratch,
+        compiler_params=pltpu.CompilerParams(vmem_limit_bytes=LIMIT),
+        name="fourier_lower",
+    )(lower, other_lower, inner, outer, message)
     message = lax.all_to_all(
-        message.reshape(DEVICES, 16, 128), ("lat", "wave"), split_axis=0, concat_axis=0, tiled=True
+        message.reshape(PEERS, 32, 128),
+        ("lat", "wave"),
+        split_axis=0,
+        concat_axis=0,
+        tiled=True,
+        axis_index_groups=[[2 * peer + core for peer in range(PEERS)] for core in range(2)],
     )
     degrees = legendre.shape[2]
     return pl.pallas_call(

time: 45.7 us -> 45.6 us (level); the launches traced: 45.4 us -> 44.7 us
  blocking collectives: 24.3 us -> 23.5 us
    all_to_all x1, blocking collectives: 24.3 us -> 23.5 us  [local(): lax.all_to_all(message.reshape(PEERS, 32, 128), ('lat', 'wave'), split_ax...]
    pallas_call x4 -> x5, Pallas kernels: 7.45 us -> 7.18 us  [the longest x1 3.42 us: local(): pl.pallas_call(table_kernel, out_shape=(jax.ShapeDtypeStruct((BAND, 256,...]
    ppermute x1 -> x2, starting transfers between devices: 2.34 us -> 2.42 us  [the longest x1 2.33 us: local(): other_upper = lax.ppermute(upper, 'wave', cores)]
  transfers between devices with their start and end apart: 5 -> 6, of which waited for: 1 -> 1; matrix products, arithmetic and copies ran while one was open for 4% -> 4% of each run, Pallas kernels for 10% -> 12%
where the time goes in v6:
time: 45.6 us; the launch traced here: 44.7 us
  blocking collectives  23.5 us (52%)
  Pallas kernels  9.18 us (20%)
  starting transfers between devices  7.81 us (17%)
  other arithmetic  3.4 us (7%)
  waiting for transfers between devices  0.46 us (1%)
    all_to_all x1, blocking collectives, local(): lax.all_to_all(message.reshape(PEERS, 32, 128), ('lat', 'wave'), split_ax...  23.5 us
    pallas_call x1, Pallas kernels, local(): pl.pallas_call(table_kernel, out_shape=(jax.ShapeDtypeStruct((BAND, 256,...  3.42 us
    ppermute x2, starting transfers between devices, swapped(): return lax.ppermute(own, 'lat', pairs + [(j, i) for i, j in pairs])  2.87 us
    ppermute x1, starting transfers between devices, local(): other_upper = lax.ppermute(upper, 'wave', cores)  2.33 us
    pallas_call x1, Pallas kernels, local(): pl.pallas_call(legendre_kernel, out_shape=jax.ShapeDtypeStruct((SLOTS, 2...  1.91 us
    ppermute x1, starting transfers between devices, local(): lax.ppermute(stencil[:, :, WIDE - 128:], 'wave', [(i, (i + 1) % ring) for...  1.55 us
    another operation x2, other arithmetic, local(): jnp.stack([depart_row.astype(F32), depart_col.astype(F32), frac_row, frac...  1.51 us
    pallas_call x1, Pallas kernels, local(): pl.pallas_call(upper_kernel, out_shape=(part, jax.ShapeDtypeStruct((COUNT...  1.09 us
  transfers between devices with their start and end apart: 6, of which 1 were waited for; matrix products, arithmetic and copies ran while one was open for 4% of the time, Pallas kernels for 12%

profile of v6, /device:TPU:1, one launch (start us, length us, event | category | flops | bytes accessed | tf_op | source)
XLA Modules:
  0.0 44.7 jit_solution(14582739192100556282)
XLA Ops:
  0.0 0.8 %pad_add_fusion = s32[1288]{0:T(1024)S(1)} fusion(s32[1280]{0:T(1024)} %param.10, s32[8]{0:T(128)} %param.9), kind=kLoop, calls=%fused_computation.5 | loop fusion | flops 1288 | bytes 10304 | tf_op jit(solution)/shard_map/concatenate | solution.py:367
  0.8 0.1 iota_compare_fusion
  0.9 1.0 %select_bitcast_fusion = bf16[8,24,640]{2,0,1:T(8,128)(2,1)S(1)} fusion(bf16[24,8,640]{2,1,0:T(8,128)(2,1)} %param.8, pred[8,640]{1,0:T(8,128)(4,1)S(1)} %iota_compare_fusion), kind=kLoop, calls=%fused_computation | loop fusion | flops 122880 | bytes 496640 | tf_op jit(solution)/shard_map/transpose | solution.py:372
  1.9 2.2 %collective-permute-start.1 = (bf16[192,640]{1,0:T(8,128)(2,1)S(1)}, bf16[192,640]{1,0:T(8,128)(2,1)S(1)}, u32[]{:S(2)}, u32[]{:S(2)}) collective-permute-start(bf16[192,640]{1,0:T(8,128)(2,1)S(1)} %bitcast.12), channel_id=1, source_target_pairs={{0,8},{16,24},{32,40},{48,56},{64,72},{80,88},{96,104},{112,120},{... | collective-permute-start | bytes 737288 | tf_op jit(solution)/shard_map/ppermute | solution.py:376
  4.1 0.7 %collective-permute-start = (bf16[192,640]{1,0:T(8,128)(2,1)S(1)}, bf16[192,640]{1,0:T(8,128)(2,1)S(1)}, u32[]{:S(2)}, u32[]{:S(2)}) collective-permute-start(bf16[192,640]{1,0:T(8,128)(2,1)S(1)} %bitcast.13), channel_id=1, source_target_pairs={{8,16},{24,32},{40,48},{56,64},{72,80},{88,96},{104,112},{16,8},{3... | collective-permute-start | bytes 737288 | tf_op jit(solution)/shard_map/ppermute | solution.py:376
  4.7 0.8 %convert_bitcast_fusion = (f32[1,8,640]{2,1,0:T(8,128)S(1)}, f32[1,8,640]{2,1,0:T(8,128)S(1)}) fusion(s32[8,640]{1,0:T(8,128)} %param.12, s32[8,640]{1,0:T(8,128)} %param.11), kind=kLoop, calls=%fused_computation.2 | loop fusion | flops 10240 | bytes 81920 | tf_op jit(solution)/shard_map/stack | solution.py:382
  5.5 0.8 %pad_maximum_fusion.stencil = f32[4,8,640]{2,1,0:T(8,128)S(1)} fusion(f32[1,8,640]{2,1,0:T(8,128)} %bitcast.16, f32[1,8,640]{2,1,0:T(8,128)} %bitcast.17, f32[1,8,640]{2,1,0:T(8,128)S(1)} %get-tuple-element.37, f32[1,8,640]{2,1,0:T(8,128)S(1)} %get-tuple-element.38), kind=kLoop, calls=%fused_computation.1 | loop fusion | flops 61440 | bytes 163840 | tf_op jit(solution)/shard_map/stack | solution.py:382
  6.3 1.0 %collective-permute-start.3 = (f32[4,8,128]{2,1,0:T(8,128)S(1)}, f32[4,8,128]{2,1,0:T(8,128)S(1)}, u32[]{:S(2)}, u32[]{:S(2)}) collective-permute-start(f32[4,8,128]{2,1,0:T(8,128)S(1)} %get-tuple-element.33), channel_id=1, source_target_pairs={{1,0},{2,1},{3,2},{4,3},{5,4},{6,5},{7,6},{0,7},{9,8},{10,9},{11,1... | collective-permute-start | bytes 49160 | tf_op jit(solution)/shard_map/ppermute | solution.py:388
  7.2 1.5 %collective-permute-start.2 = (f32[4,8,128]{2,1,0:T(8,128)S(1)}, f32[4,8,128]{2,1,0:T(8,128)S(1)}, u32[]{:S(2)}, u32[]{:S(2)}) collective-permute-start(f32[4,8,128]{2,1,0:T(8,128)S(1)} %get-tuple-element.34), channel_id=1, source_target_pairs={{0,1},{1,2},{2,3},{3,4},{4,5},{5,6},{6,7},{7,0},{8,9},{9,10},{10,1... | collective-permute-start | bytes 49160 | tf_op jit(solution)/shard_map/ppermute | solution.py:385
  8.8 0.1 slice_convert_fusion
  8.8 0.1 convert_element_type.20
  9.0 0.1 copy.11
  9.0 0.1 broadcast_in_dim.12.lengths
  9.1 3.4 %tables.1 = (bf16[8,256,1280]{2,1,0:T(8,128)(2,1)S(1)}, f32[8,8,1280]{2,1,0:T(8,128)S(1)}, bf16[4,5,256,256]{3,2,1,0:T(8,128)(2,1)S(1)}, f32[4,5,24,256]{3,2,1,0:T(8,128)S(1)}, f32[10,128]{1,0:T(8,128)S(1)}) custom-call(f32[8,128]{1,0:T(8,128)S(1)} %broadcast_in_dim.12.lengths, f32[20,64]{1,0:T(8,128)S(1)} %bitcast.15, f32[4,8,640]{2,1,0:T(8,128)S(1)} %pad_maximum_fusion.stencil), custom_call_target="tpu_custom_call" | custom-call | flops 5000000000 | bytes 3000000 | tf_op jit(solution)/shard_map/tables/pallas_call | solution.py:392
  12.5 0.1 wrap_tables.1
  12.7 1.1 %interpolate_upper.1 = (bf16[4,144,128]{2,1,0:T(8,128)(2,1)S(1)}, bf16[576,640]{1,0:T(8,128)(2,1)S(1)}, bf16[576,768]{1,0:T(8,128)(2,1)S(1)}) custom-call(bf16[192,640]{1,0:T(8,128)(2,1)S(1)} %bitcast.14, bf16[192,640]{1,0:T(8,128)(2,1)S(1)} %collective-permute-done.first, bf16[192,640]{1,0:T(8,128)(2,1)S(1)} %collective-permute-done.1.second, ...), custom_call_target="tpu_custom_call" | custom-call | tf_op jit(solution)/shard_map/interpolate_upper/pallas_call | solution.py:423
  13.8 2.3 %collective-permute-start.5 = (bf16[4,144,128]{2,1,0:T(8,128)(2,1)S(1)}, bf16[4,144,128]{2,1,0:T(8,128)(2,1)S(1)}, u32[]{:S(2)}, u32[]{:S(2)}) collective-permute-start(bf16[4,144,128]{2,1,0:T(8,128)(2,1)S(1)} %get-tuple-element.32.mine), channel_id=1, source_target_pairs={{0,1},{1,0},{2,3},{3,2},{4,5},{5,4},{6,7},{7,6},{8,9},{9,8},{10,11... | collective-permute-start | bytes 442376 | tf_op jit(solution)/shard_map/ppermute | solution.py:436
  16.1 0.9 %interpolate_lower.1.mine = bf16[4,144,128]{2,1,0:T(8,128)(2,1)S(1)} custom-call(bf16[576,640]{1,0:T(8,128)(2,1)S(1)} %get-tuple-element.28.main, bf16[576,768]{1,0:T(8,128)(2,1)S(1)} %get-tuple-element.29.edge, bf16[4,5,256,256]{3,2,1,0:T(8,128)(2,1)S(1)} %get-tuple-element.24.columns, f32[4,5,24,256]{3,2,1,0:T(8,128)S(1)} %get-tuple-element.25.rows_of, ...), custom_call_target="tpu_custom_call" | custom-call | flops 5000000000 | bytes 3000000 | tf_op jit(solution)/shard_map/interpolate_lower/pallas_call | solution.py:437
  17.0 0.1 collective-permute-start.4
  17.1 0.9 %fourier_upper.1.upper = bf16[1024,128]{1,0:T(8,128)(2,1)S(1)} custom-call(bf16[4,144,128]{2,1,0:T(8,128)(2,1)S(1)} %get-tuple-element.32.mine, bf16[4,144,128]{2,1,0:T(8,128)(2,1)S(1)} %collective-permute-done.5.other, bf16[8,256,1280]{2,1,0:T(8,128)(2,1)S(1)} %get-tuple-element.30.inner, f32[8,8,1280]{2,1,0:T(8,128)S(1)} %get-tuple-element.31.outer), custom_call_target="tpu_custom_call" | custom-call | flops 5000000000 | bytes 3000000 | tf_op jit(solution)/shard_map/fourier_upper/pallas_call | solution.py:448
  18.0 0.4 collective-permute-done.4.other
  18.4 0.9 %fourier_lower.1 = bf16[2048,128]{1,0:T(8,128)(2,1)S(1)} custom-call(bf16[4,144,128]{2,1,0:T(8,128)(2,1)S(1)} %interpolate_lower.1.mine, bf16[4,144,128]{2,1,0:T(8,128)(2,1)S(1)} %collective-permute-done.4.other, bf16[8,256,1280]{2,1,0:T(8,128)(2,1)S(1)} %get-tuple-element.30.inner, f32[8,8,1280]{2,1,0:T(8,128)S(1)} %get-tuple-element.31.outer, ...), custom_call_target="tpu_custom_call" | custom-call | tf_op jit(solution)/shard_map/fourier_lower/pallas_call | solution.py:458
  19.3 23.5 %all_to_all.5.message = bf16[64,32,128]{2,1,0:T(8,128)(2,1)S(1)} all-to-all(bf16[64,32,128]{2,1,0:T(8,128)(2,1)S(1)} %bitcast.11), channel_id=1, replica_groups={{0,2,4,6,8,10,12,14,16,18,20,22,24,26,28,30,32,34,36,38,40,42,44,46,48,..., dimensions={0} | all-to-all | bytes 1048576 | tf_op jit(solution)/shard_map/all_to_all | solution.py:467
  42.8 1.9 %legendre.1 = f32[10,48,1280]{2,1,0:T(8,128)} custom-call(f32[10,128]{1,0:T(8,128)S(1)} %get-tuple-element.22.waves, bf16[64,32,128]{2,1,0:T(8,128)(2,1)S(1)} %all_to_all.5.message, bf16[10,128,1280]{2,1,0:T(8,128)(2,1)S(1)} %copy-done), custom_call_target="tpu_custom_call" | custom-call | tf_op jit(solution)/shard_map/legendre/pallas_call | solution.py:476
  (10 shorter events, 0.1 us)
Async XLA Ops:
  1.9 10.8 %collective-permute-start.1 = (bf16[192,640]{1,0:T(8,128)(2,1)S(1)}, bf16[192,640]{1,0:T(8,128)(2,1)S(1)}, u32[]{:S(2)}, u32[]{:S(2)}) collective-permute-start(bf16[192,640]{1,0:T(8,128)(2,1)S(1)} %bitcast.12), channel_id=1, source_target_pairs={{0,8},{16,24},{32,40},{48,56},{64,72},{80,88},{96,104},{112,120},{... | collective-permute-start | bytes 737288 | tf_op jit(solution)/shard_map/ppermute | solution.py:376
  4.1 8.6 %collective-permute-start = (bf16[192,640]{1,0:T(8,128)(2,1)S(1)}, bf16[192,640]{1,0:T(8,128)(2,1)S(1)}, u32[]{:S(2)}, u32[]{:S(2)}) collective-permute-start(bf16[192,640]{1,0:T(8,128)(2,1)S(1)} %bitcast.13), channel_id=1, source_target_pairs={{8,16},{24,32},{40,48},{56,64},{72,80},{88,96},{104,112},{16,8},{3... | collective-permute-start | bytes 737288 | tf_op jit(solution)/shard_map/ppermute | solution.py:376
  6.3 6.3 %collective-permute-start.3 = (f32[4,8,128]{2,1,0:T(8,128)S(1)}, f32[4,8,128]{2,1,0:T(8,128)S(1)}, u32[]{:S(2)}, u32[]{:S(2)}) collective-permute-start(f32[4,8,128]{2,1,0:T(8,128)S(1)} %get-tuple-element.33), channel_id=1, source_target_pairs={{1,0},{2,1},{3,2},{4,3},{5,4},{6,5},{7,6},{0,7},{9,8},{10,9},{11,1... | collective-permute-start | bytes 49160 | tf_op jit(solution)/shard_map/ppermute | solution.py:388
  7.2 5.3 %collective-permute-start.2 = (f32[4,8,128]{2,1,0:T(8,128)S(1)}, f32[4,8,128]{2,1,0:T(8,128)S(1)}, u32[]{:S(2)}, u32[]{:S(2)}) collective-permute-start(f32[4,8,128]{2,1,0:T(8,128)S(1)} %get-tuple-element.34), channel_id=1, source_target_pairs={{0,1},{1,2},{2,3},{3,4},{4,5},{5,6},{6,7},{7,0},{8,9},{9,10},{10,1... | collective-permute-start | bytes 49160 | tf_op jit(solution)/shard_map/ppermute | solution.py:385
  13.8 3.3 %collective-permute-start.5 = (bf16[4,144,128]{2,1,0:T(8,128)(2,1)S(1)}, bf16[4,144,128]{2,1,0:T(8,128)(2,1)S(1)}, u32[]{:S(2)}, u32[]{:S(2)}) collective-permute-start(bf16[4,144,128]{2,1,0:T(8,128)(2,1)S(1)} %get-tuple-element.32.mine), channel_id=1, source_target_pairs={{0,1},{1,0},{2,3},{3,2},{4,5},{5,4},{6,7},{7,6},{8,9},{9,8},{10,11... | collective-permute-start | bytes 442376 | tf_op jit(solution)/shard_map/ppermute | solution.py:436
  17.0 1.5 %collective-permute-start.4 = (bf16[4,144,128]{2,1,0:T(8,128)(2,1)S(1)}, bf16[4,144,128]{2,1,0:T(8,128)(2,1)S(1)}, u32[]{:S(2)}, u32[]{:S(2)}) collective-permute-start(bf16[4,144,128]{2,1,0:T(8,128)(2,1)S(1)} %interpolate_lower.1.mine), channel_id=1, source_target_pairs={{0,1},{1,0},{2,3},{3,2},{4,5},{5,4},{6,7},{7,6},{8,9},{9,8},{10,11... | collective-permute-start | bytes 442376 | tf_op jit(solution)/shard_map/ppermute | solution.py:446
  18.0 24.8 %copy-start = (bf16[10,128,1280]{2,1,0:T(8,128)(2,1)S(1)}, bf16[10,128,1280]{2,1,0:T(8,128)(2,1)}, u32[]{:S(2)}) copy-start(bf16[10,128,1280]{2,1,0:T(8,128)(2,1)} %table.1) | copy-start | bytes 9830404

commit v7 on v6

--- a/solution.py
+++ b/solution.py
@@ -69,7 +69,7 @@
 
 
 def upper_kernel(
-    own, first, second, columns, rows_of, wrap_columns, wrap_rows, out, main, edge
+    own, second, first, columns, rows_of, wrap_columns, wrap_rows, out, main, edge
 ):
     size = BAND * SLICES
     odd = lax.axis_index("lat") % 2
@@ -379,7 +379,10 @@
     under = swapped(0)
 
     own, depart_row = lax.optimization_barrier((own, depart_row))
-    stencil = jnp.stack([depart_row.astype(F32), depart_col.astype(F32), frac_row, frac_col])
+    item = lax.broadcasted_iota(jnp.int32, (4, BAND, WIDE), 0)
+    departs = jnp.where(item == 0, depart_row[None], depart_col[None]).astype(F32)
+    fractions = jnp.where(item == 2, frac_row[None], frac_col[None])
+    stencil = jnp.where(item < 2, departs, fractions)
     stencil, scalars = lax.optimization_barrier((stencil, scalars))
     ordered = scalars[BAND:].reshape(PEERS, 2 * SLOTS).T.astype(F32)
     from_left = lax.ppermute(
@@ -431,7 +434,7 @@
         out_specs=(VMEM,) * 3,
         compiler_params=pltpu.CompilerParams(vmem_limit_bytes=LIMIT),
         name="interpolate_upper",
-    )(own, over, under, *weights)
+    )(own, under, over, *weights)
     cores = [(i, i ^ 1) for i in range(ring)]
     other_upper = lax.ppermute(upper, "wave", cores)
     lower = pl.pallas_call(

time: 45.6 us -> 45.1 us (0.989)
  blocking collectives: 23.5 us -> 21 us
  starting transfers between devices: 7.81 us -> 10.3 us
  other arithmetic: 3.4 us -> 2.77 us
    ppermute x2, starting transfers between devices: 2.87 us -> 5.41 us  [swapped(): return lax.ppermute(own, 'lat', pairs + [(j, i) for i, j in pairs])]
    all_to_all x1, blocking collectives: 23.5 us -> 21 us  [local(): lax.all_to_all(message.reshape(PEERS, 32, 128), ('lat', 'wave'), split_ax...]
    another operation x2 -> x0, other arithmetic: 1.51 us -> none  [local(): jnp.stack([depart_row.astype(F32), depart_col.astype(F32), frac_row, frac...]
    select_n x0 -> x1, other arithmetic: none -> 0.86 us  [local(): stencil = jnp.where(item < 2, departs, fractions)]
  transfers between devices with their start and end apart: 6 -> 6, of which waited for: 1 -> 1; matrix products, arithmetic and copies ran while one was open for 4% -> 3% of each run, Pallas kernels for 12% -> 12%
where the time goes in v7:
time: 45.1 us; the launch traced here: 44.2 us
  blocking collectives  21 us (47%)
  starting transfers between devices  10.3 us (23%)
  Pallas kernels  9.19 us (20%)
  other arithmetic  2.77 us (6%)
    all_to_all x1, blocking collectives, local(): lax.all_to_all(message.reshape(PEERS, 32, 128), ('lat', 'wave'), split_ax...  21 us
    ppermute x2, starting transfers between devices, swapped(): return lax.ppermute(own, 'lat', pairs + [(j, i) for i, j in pairs])  5.41 us
    pallas_call x1, Pallas kernels, local(): pl.pallas_call(table_kernel, out_shape=(jax.ShapeDtypeStruct((BAND, 256,...  3.42 us
    ppermute x1, starting transfers between devices, local(): other_upper = lax.ppermute(upper, 'wave', cores)  2.05 us
    pallas_call x1, Pallas kernels, local(): pl.pallas_call(legendre_kernel, out_shape=jax.ShapeDtypeStruct((SLOTS, 2...  1.92 us
    ppermute x1, starting transfers between devices, local(): lax.ppermute(stencil[:, :, WIDE - 128:], 'wave', [(i, (i + 1) % ring) for...  1.55 us
    ppermute x1, starting transfers between devices, local(): lax.ppermute(stencil[:, :, :128], 'wave', [((i + 1) % ring, i) for i in r...  1.25 us
    pallas_call x1, Pallas kernels, local(): pl.pallas_call(upper_kernel, out_shape=(part, jax.ShapeDtypeStruct((COUNT...  1.09 us
  transfers between devices with their start and end apart: 6, of which 1 were waited for; matrix products, arithmetic and copies ran while one was open for 3% of the time, Pallas kernels for 12%

profile of v7, /device:TPU:1, one launch (start us, length us, event | category | flops | bytes accessed | tf_op | source)
XLA Modules:
  0.0 44.2 jit_solution(6343431864020345760)
XLA Ops:
  0.0 0.8 %pad_add_fusion = s32[1288]{0:T(1024)S(1)} fusion(s32[1280]{0:T(1024)} %param.10, s32[8]{0:T(128)} %param.9), kind=kLoop, calls=%fused_computation.3 | loop fusion | flops 1288 | bytes 10304 | tf_op jit(solution)/shard_map/concatenate | solution.py:367
  0.8 0.1 iota_compare_fusion
  0.9 1.0 %select_bitcast_fusion = bf16[8,24,640]{2,0,1:T(8,128)(2,1)S(1)} fusion(bf16[24,8,640]{2,1,0:T(8,128)(2,1)} %param.8, pred[8,640]{1,0:T(8,128)(4,1)S(1)} %iota_compare_fusion), kind=kLoop, calls=%fused_computation | loop fusion | flops 122880 | bytes 496640 | tf_op jit(solution)/shard_map/transpose | solution.py:372
  1.9 0.7 %collective-permute-start.1 = (bf16[192,640]{1,0:T(8,128)(2,1)S(1)}, bf16[192,640]{1,0:T(8,128)(2,1)S(1)}, u32[]{:S(2)}, u32[]{:S(2)}) collective-permute-start(bf16[192,640]{1,0:T(8,128)(2,1)S(1)} %bitcast.6), channel_id=1, source_target_pairs={{8,16},{24,32},{40,48},{56,64},{72,80},{88,96},{104,112},{16,8},{3... | collective-permute-start | bytes 737288 | tf_op jit(solution)/shard_map/ppermute | solution.py:376
  2.6 4.7 %collective-permute-start = (bf16[192,640]{1,0:T(8,128)(2,1)S(1)}, bf16[192,640]{1,0:T(8,128)(2,1)S(1)}, u32[]{:S(2)}, u32[]{:S(2)}) collective-permute-start(bf16[192,640]{1,0:T(8,128)(2,1)S(1)} %bitcast.7), channel_id=1, source_target_pairs={{0,8},{16,24},{32,40},{48,56},{64,72},{80,88},{96,104},{112,120},{... | collective-permute-start | bytes 737288 | tf_op jit(solution)/shard_map/ppermute | solution.py:376
  7.3 0.9 %select_select_fusion.stencil = f32[4,8,640]{2,1,0:T(8,128)S(1)} fusion(f32[8,640]{1,0:T(8,128)} %param.14, f32[8,640]{1,0:T(8,128)} %param.13, s32[8,640]{1,0:T(8,128)} %param.12, s32[8,640]{1,0:T(8,128)} %param.11, pred[4]{0:T(512)(128)(4,1)S(1)} %get-tuple-element.37, pred[4]{0:T(512)(128)(4,1)S(1)} %get-tuple-element.38, ...), kind=kLoop, calls=%fused_computation.1 | loop fusion | flops 81920 | bytes 163852 | tf_op jit(solution)/shard_map/jit(_where)/select_n | solution.py:385
  8.2 1.2 %collective-permute-start.3 = (f32[4,8,128]{2,1,0:T(8,128)S(1)}, f32[4,8,128]{2,1,0:T(8,128)S(1)}, u32[]{:S(2)}, u32[]{:S(2)}) collective-permute-start(f32[4,8,128]{2,1,0:T(8,128)S(1)} %get-tuple-element.33), channel_id=1, source_target_pairs={{1,0},{2,1},{3,2},{4,3},{5,4},{6,5},{7,6},{0,7},{9,8},{10,9},{11,1... | collective-permute-start | bytes 49160 | tf_op jit(solution)/shard_map/ppermute | solution.py:391
  9.4 1.5 %collective-permute-start.2 = (f32[4,8,128]{2,1,0:T(8,128)S(1)}, f32[4,8,128]{2,1,0:T(8,128)S(1)}, u32[]{:S(2)}, u32[]{:S(2)}) collective-permute-start(f32[4,8,128]{2,1,0:T(8,128)S(1)} %get-tuple-element.34), channel_id=1, source_target_pairs={{0,1},{1,2},{2,3},{3,4},{4,5},{5,6},{6,7},{7,0},{8,9},{9,10},{10,1... | collective-permute-start | bytes 49160 | tf_op jit(solution)/shard_map/ppermute | solution.py:388
  11.0 0.1 slice_convert_fusion
  11.1 0.1 convert_element_type.16
  11.2 0.1 copy.11
  11.2 0.1 broadcast_in_dim.56.lengths
  11.3 3.4 %tables.1 = (bf16[8,256,1280]{2,1,0:T(8,128)(2,1)S(1)}, f32[8,8,1280]{2,1,0:T(8,128)S(1)}, bf16[4,5,256,256]{3,2,1,0:T(8,128)(2,1)S(1)}, f32[4,5,24,256]{3,2,1,0:T(8,128)S(1)}, f32[10,128]{1,0:T(8,128)S(1)}) custom-call(f32[8,128]{1,0:T(8,128)S(1)} %broadcast_in_dim.56.lengths, f32[20,64]{1,0:T(8,128)S(1)} %bitcast.9, f32[4,8,640]{2,1,0:T(8,128)S(1)} %select_select_fusion.stencil), custom_call_target="tpu_custom_call" | custom-call | flops 5000000000 | bytes 3000000 | tf_op jit(solution)/shard_map/tables/pallas_call | solution.py:395
  14.8 0.1 wrap_tables.1
  14.9 1.1 %interpolate_upper.1 = (bf16[4,144,128]{2,1,0:T(8,128)(2,1)S(1)}, bf16[576,640]{1,0:T(8,128)(2,1)S(1)}, bf16[576,768]{1,0:T(8,128)(2,1)S(1)}) custom-call(bf16[192,640]{1,0:T(8,128)(2,1)S(1)} %bitcast.8, bf16[192,640]{1,0:T(8,128)(2,1)S(1)} %collective-permute-done.second, bf16[192,640]{1,0:T(8,128)(2,1)S(1)} %collective-permute-done.1.first, ...), custom_call_target="tpu_custom_call" | custom-call | tf_op jit(solution)/shard_map/interpolate_upper/pallas_call | solution.py:426
  16.0 2.0 %collective-permute-start.5 = (bf16[4,144,128]{2,1,0:T(8,128)(2,1)S(1)}, bf16[4,144,128]{2,1,0:T(8,128)(2,1)S(1)}, u32[]{:S(2)}, u32[]{:S(2)}) collective-permute-start(bf16[4,144,128]{2,1,0:T(8,128)(2,1)S(1)} %get-tuple-element.32.mine), channel_id=1, source_target_pairs={{0,1},{1,0},{2,3},{3,2},{4,5},{5,4},{6,7},{7,6},{8,9},{9,8},{10,11... | collective-permute-start | bytes 442376 | tf_op jit(solution)/shard_map/ppermute | solution.py:439
  18.0 0.9 %interpolate_lower.1.mine = bf16[4,144,128]{2,1,0:T(8,128)(2,1)S(1)} custom-call(bf16[576,640]{1,0:T(8,128)(2,1)S(1)} %get-tuple-element.28.main, bf16[576,768]{1,0:T(8,128)(2,1)S(1)} %get-tuple-element.29.edge, bf16[4,5,256,256]{3,2,1,0:T(8,128)(2,1)S(1)} %get-tuple-element.24.columns, f32[4,5,24,256]{3,2,1,0:T(8,128)S(1)} %get-tuple-element.25.rows_of, ...), custom_call_target="tpu_custom_call" | custom-call | flops 5000000000 | bytes 3000000 | tf_op jit(solution)/shard_map/interpolate_lower/pallas_call | solution.py:440
  18.9 0.1 collective-permute-start.4
  19.0 0.0 collective-permute-done.5.other
  19.0 0.9 %fourier_upper.1.upper = bf16[1024,128]{1,0:T(8,128)(2,1)S(1)} custom-call(bf16[4,144,128]{2,1,0:T(8,128)(2,1)S(1)} %get-tuple-element.32.mine, bf16[4,144,128]{2,1,0:T(8,128)(2,1)S(1)} %collective-permute-done.5.other, bf16[8,256,1280]{2,1,0:T(8,128)(2,1)S(1)} %get-tuple-element.30.inner, f32[8,8,1280]{2,1,0:T(8,128)S(1)} %get-tuple-element.31.outer), custom_call_target="tpu_custom_call" | custom-call | flops 5000000000 | bytes 3000000 | tf_op jit(solution)/shard_map/fourier_upper/pallas_call | solution.py:451
  19.9 0.4 collective-permute-done.4.other
  20.4 0.9 %fourier_lower.1 = bf16[2048,128]{1,0:T(8,128)(2,1)S(1)} custom-call(bf16[4,144,128]{2,1,0:T(8,128)(2,1)S(1)} %interpolate_lower.1.mine, bf16[4,144,128]{2,1,0:T(8,128)(2,1)S(1)} %collective-permute-done.4.other, bf16[8,256,1280]{2,1,0:T(8,128)(2,1)S(1)} %get-tuple-element.30.inner, f32[8,8,1280]{2,1,0:T(8,128)S(1)} %get-tuple-element.31.outer, ...), custom_call_target="tpu_custom_call" | custom-call | tf_op jit(solution)/shard_map/fourier_lower/pallas_call | solution.py:461
  21.3 21.0 %all_to_all.5.message = bf16[64,32,128]{2,1,0:T(8,128)(2,1)S(1)} all-to-all(bf16[64,32,128]{2,1,0:T(8,128)(2,1)S(1)} %bitcast.5), channel_id=1, replica_groups={{0,2,4,6,8,10,12,14,16,18,20,22,24,26,28,30,32,34,36,38,40,42,44,46,48,..., dimensions={0} | all-to-all | bytes 1048576 | tf_op jit(solution)/shard_map/all_to_all | solution.py:470
  42.3 1.9 %legendre.1 = f32[10,48,1280]{2,1,0:T(8,128)} custom-call(f32[10,128]{1,0:T(8,128)S(1)} %get-tuple-element.22.waves, bf16[64,32,128]{2,1,0:T(8,128)(2,1)S(1)} %all_to_all.5.message, bf16[10,128,1280]{2,1,0:T(8,128)(2,1)S(1)} %copy-done), custom_call_target="tpu_custom_call" | custom-call | tf_op jit(solution)/shard_map/legendre/pallas_call | solution.py:479
  (11 shorter events, 0.1 us)
Async XLA Ops:
  1.9 13.0 %collective-permute-start.1 = (bf16[192,640]{1,0:T(8,128)(2,1)S(1)}, bf16[192,640]{1,0:T(8,128)(2,1)S(1)}, u32[]{:S(2)}, u32[]{:S(2)}) collective-permute-start(bf16[192,640]{1,0:T(8,128)(2,1)S(1)} %bitcast.6), channel_id=1, source_target_pairs={{8,16},{24,32},{40,48},{56,64},{72,80},{88,96},{104,112},{16,8},{3... | collective-permute-start | bytes 737288 | tf_op jit(solution)/shard_map/ppermute | solution.py:376
  2.6 12.3 %collective-permute-start = (bf16[192,640]{1,0:T(8,128)(2,1)S(1)}, bf16[192,640]{1,0:T(8,128)(2,1)S(1)}, u32[]{:S(2)}, u32[]{:S(2)}) collective-permute-start(bf16[192,640]{1,0:T(8,128)(2,1)S(1)} %bitcast.7), channel_id=1, source_target_pairs={{0,8},{16,24},{32,40},{48,56},{64,72},{80,88},{96,104},{112,120},{... | collective-permute-start | bytes 737288 | tf_op jit(solution)/shard_map/ppermute | solution.py:376
  8.2 6.6 %collective-permute-start.3 = (f32[4,8,128]{2,1,0:T(8,128)S(1)}, f32[4,8,128]{2,1,0:T(8,128)S(1)}, u32[]{:S(2)}, u32[]{:S(2)}) collective-permute-start(f32[4,8,128]{2,1,0:T(8,128)S(1)} %get-tuple-element.33), channel_id=1, source_target_pairs={{1,0},{2,1},{3,2},{4,3},{5,4},{6,5},{7,6},{0,7},{9,8},{10,9},{11,1... | collective-permute-start | bytes 49160 | tf_op jit(solution)/shard_map/ppermute | solution.py:391
  9.4 5.3 %collective-permute-start.2 = (f32[4,8,128]{2,1,0:T(8,128)S(1)}, f32[4,8,128]{2,1,0:T(8,128)S(1)}, u32[]{:S(2)}, u32[]{:S(2)}) collective-permute-start(f32[4,8,128]{2,1,0:T(8,128)S(1)} %get-tuple-element.34), channel_id=1, source_target_pairs={{0,1},{1,2},{2,3},{3,4},{4,5},{5,6},{6,7},{7,0},{8,9},{9,10},{10,1... | collective-permute-start | bytes 49160 | tf_op jit(solution)/shard_map/ppermute | solution.py:388
  16.0 3.1 %collective-permute-start.5 = (bf16[4,144,128]{2,1,0:T(8,128)(2,1)S(1)}, bf16[4,144,128]{2,1,0:T(8,128)(2,1)S(1)}, u32[]{:S(2)}, u32[]{:S(2)}) collective-permute-start(bf16[4,144,128]{2,1,0:T(8,128)(2,1)S(1)} %get-tuple-element.32.mine), channel_id=1, source_target_pairs={{0,1},{1,0},{2,3},{3,2},{4,5},{5,4},{6,7},{7,6},{8,9},{9,8},{10,11... | collective-permute-start | bytes 442376 | tf_op jit(solution)/shard_map/ppermute | solution.py:439
  18.9 1.5 %collective-permute-start.4 = (bf16[4,144,128]{2,1,0:T(8,128)(2,1)S(1)}, bf16[4,144,128]{2,1,0:T(8,128)(2,1)S(1)}, u32[]{:S(2)}, u32[]{:S(2)}) collective-permute-start(bf16[4,144,128]{2,1,0:T(8,128)(2,1)S(1)} %interpolate_lower.1.mine), channel_id=1, source_target_pairs={{0,1},{1,0},{2,3},{3,2},{4,5},{5,4},{6,7},{7,6},{8,9},{9,8},{10,11... | collective-permute-start | bytes 442376 | tf_op jit(solution)/shard_map/ppermute | solution.py:449
  19.9 22.4 %copy-start = (bf16[10,128,1280]{2,1,0:T(8,128)(2,1)S(1)}, bf16[10,128,1280]{2,1,0:T(8,128)(2,1)}, u32[]{:S(2)}) copy-start(bf16[10,128,1280]{2,1,0:T(8,128)(2,1)} %table.1) | copy-start | bytes 9830404

commit v8 on v7

--- a/solution.py
+++ b/solution.py
@@ -199,6 +199,7 @@
         shift = jnp.where(step == at, value, shift)
     shift = shift.astype(F32)
     fine = step.astype(F32)
+    coarse = 16.0 * fine
 
     def one(row, carry):
         length = length_rows[row]
@@ -211,24 +212,22 @@
             outer[row, :, lanes] = moved[0] * norm
             outer[row, :, lanes_two] = moved[1] * norm
             other = [part[7:8] for part in moved]
-            small = turn(fine * wave, length, inverse)
-            low = turn(8.0 * fine * wave, length, inverse)
-            half = rotated([part[7:8] for part in low], [part[1:2] for part in low])
+            near = turn(fine * wave, length, inverse)
+            eight = rotated([part[7:8] for part in near], [part[1:2] for part in near])
+            small = [
+                jnp.concatenate(parts, axis=0).astype(BF16)
+                for parts in zip(near, rotated(eight, near))
+            ]
+            low = turn(coarse * wave, length, inverse)
             for tile in range(2):
                 if tile:
                     low = rotated(low, other)
-                high = rotated(low, half)
-                for coarse in range(0, 16, 2):
-                    source = low if coarse < 8 else high
-                    at = coarse % 8
-                    pairs = [
-                        rotated([part[k : k + 1] for part in source], small) for k in (at, at + 1)
+                for k in range(8):
+                    start = [
+                        jnp.broadcast_to(part[k : k + 1], (16, 128)).astype(BF16) for part in low
                     ]
-                    rows = slice(128 * tile + 8 * coarse, 128 * tile + 8 * coarse + 16)
-                    for side, to in enumerate((lanes, lanes_two)):
-                        inner[row, rows, to] = jnp.concatenate(
-                            [pair[side] for pair in pairs], axis=0
-                        ).astype(BF16)
+                    rows = slice(128 * tile + 16 * k, 128 * tile + 16 * k + 16)
+                    inner[row, rows, lanes], inner[row, rows, lanes_two] = rotated(start, small)
         return carry
 
     lax.fori_loop(0, BAND, one, 0)
@@ -339,24 +338,24 @@
         for z in range(1, 4):
             total = total + message[4 * band + z].astype(F32)
         flat[32 * band : 32 * band + 32, :] = total
-    for row in range(BAND):
-        for part in range(4):
+    copies = []
+    for part in range(4):
+        for row in range(BAND):
             sorted_rows[pl.ds(128 * part + row, 16, stride=8), :] = flat[
                 pl.ds(4 * row + part, 16, stride=32), :
             ]
-    for part in range(4):
         rows = slice(128 * part, 128 * part + 128)
         left[rows, :] = sorted_rows[rows, :].T.astype(BF16)
-    copies = []
-    for slot in range(SLOTS):
-        first = 256 * (slot % 2) + 48 * (slot // 2)
-        product = jnp.dot(left[first : first + 48, :], table[slot], preferred_element_type=F32)
-        wave = jnp.concatenate([waves[slot : slot + 1, :]] * (product.shape[1] // 128), axis=1)
-        degree = lax.broadcasted_iota(jnp.int32, product.shape, 1).astype(F32)
-        result[slot] = jnp.where(degree >= wave, product, 0.0)
-        copy = pltpu.make_async_copy(result.at[slot], out.at[slot], done.at[slot])
-        copy.start()
-        copies.append(copy)
+        for group in ((2, 3, 4) if part % 2 else (0, 1)):
+            slot = 2 * group + part // 2
+            first = 256 * (part // 2) + 48 * group
+            product = jnp.dot(left[first : first + 48, :], table[slot], preferred_element_type=F32)
+            wave = jnp.concatenate([waves[slot : slot + 1, :]] * (product.shape[1] // 128), axis=1)
+            degree = lax.broadcasted_iota(jnp.int32, product.shape, 1).astype(F32)
+            result[slot] = jnp.where(degree >= wave, product, 0.0)
+            copy = pltpu.make_async_copy(result.at[slot], out.at[slot], done.at[slot])
+            copy.start()
+            copies.append(copy)
     for copy in copies:
         copy.wait()
 

time: 45.1 us -> 45 us (level)
  transfers between devices with their start and end apart: 6 -> 6, of which waited for: 1 -> 1; matrix products, arithmetic and copies ran while one was open for 3% -> 3% of each run, Pallas kernels for 12% -> 11%
where the time goes in v8:
time: 45 us; the launch traced here: 44.2 us
  blocking collectives  21 us (47%)
  starting transfers between devices  10.7 us (24%)
  Pallas kernels  8.76 us (19%)
  other arithmetic  2.77 us (6%)
  waiting for transfers between devices  0.45 us (1%)
    all_to_all x1, blocking collectives, local(): lax.all_to_all(message.reshape(PEERS, 32, 128), ('lat', 'wave'), split_ax...  21 us
    ppermute x2, starting transfers between devices, swapped(): return lax.ppermute(own, 'lat', pairs + [(j, i) for i, j in pairs])  5.41 us
    pallas_call x1, Pallas kernels, local(): pl.pallas_call(table_kernel, out_shape=(jax.ShapeDtypeStruct((BAND, 256,...  3.03 us
    ppermute x1, starting transfers between devices, local(): other_upper = lax.ppermute(upper, 'wave', cores)  2.43 us
    pallas_call x1, Pallas kernels, local(): pl.pallas_call(legendre_kernel, out_shape=jax.ShapeDtypeStruct((SLOTS, 2...  1.87 us
    ppermute x1, starting transfers between devices, local(): lax.ppermute(stencil[:, :, WIDE - 128:], 'wave', [(i, (i + 1) % ring) for...  1.55 us
    ppermute x1, starting transfers between devices, local(): lax.ppermute(stencil[:, :, :128], 'wave', [((i + 1) % ring, i) for i in r...  1.25 us
    pallas_call x1, Pallas kernels, local(): pl.pallas_call(upper_kernel, out_shape=(part, jax.ShapeDtypeStruct((COUNT...  1.09 us
  transfers between devices with their start and end apart: 6, of which 1 were waited for; matrix products, arithmetic and copies ran while one was open for 3% of the time, Pallas kernels for 11%

profile of v8, /device:TPU:1, one launch (start us, length us, event | category | flops | bytes accessed | tf_op | source)
XLA Modules:
  0.0 44.2 jit_solution(12768039629717301712)
XLA Ops:
  0.0 0.8 %pad_add_fusion = s32[1288]{0:T(1024)S(1)} fusion(s32[1280]{0:T(1024)} %param.10, s32[8]{0:T(128)} %param.9), kind=kLoop, calls=%fused_computation.3 | loop fusion | flops 1288 | bytes 10304 | tf_op jit(solution)/shard_map/concatenate | solution.py:366
  0.8 0.1 iota_compare_fusion
  0.9 1.0 %select_bitcast_fusion = bf16[8,24,640]{2,0,1:T(8,128)(2,1)S(1)} fusion(bf16[24,8,640]{2,1,0:T(8,128)(2,1)} %param.8, pred[8,640]{1,0:T(8,128)(4,1)S(1)} %iota_compare_fusion), kind=kLoop, calls=%fused_computation | loop fusion | flops 122880 | bytes 496640 | tf_op jit(solution)/shard_map/transpose | solution.py:371
  1.9 0.7 %collective-permute-start.1 = (bf16[192,640]{1,0:T(8,128)(2,1)S(1)}, bf16[192,640]{1,0:T(8,128)(2,1)S(1)}, u32[]{:S(2)}, u32[]{:S(2)}) collective-permute-start(bf16[192,640]{1,0:T(8,128)(2,1)S(1)} %bitcast.6), channel_id=1, source_target_pairs={{8,16},{24,32},{40,48},{56,64},{72,80},{88,96},{104,112},{16,8},{3... | collective-permute-start | bytes 737288 | tf_op jit(solution)/shard_map/ppermute | solution.py:375
  2.6 4.7 %collective-permute-start = (bf16[192,640]{1,0:T(8,128)(2,1)S(1)}, bf16[192,640]{1,0:T(8,128)(2,1)S(1)}, u32[]{:S(2)}, u32[]{:S(2)}) collective-permute-start(bf16[192,640]{1,0:T(8,128)(2,1)S(1)} %bitcast.7), channel_id=1, source_target_pairs={{0,8},{16,24},{32,40},{48,56},{64,72},{80,88},{96,104},{112,120},{... | collective-permute-start | bytes 737288 | tf_op jit(solution)/shard_map/ppermute | solution.py:375
  7.3 0.9 %select_select_fusion.stencil = f32[4,8,640]{2,1,0:T(8,128)S(1)} fusion(f32[8,640]{1,0:T(8,128)} %param.14, f32[8,640]{1,0:T(8,128)} %param.13, s32[8,640]{1,0:T(8,128)} %param.12, s32[8,640]{1,0:T(8,128)} %param.11, pred[4]{0:T(512)(128)(4,1)S(1)} %get-tuple-element.37, pred[4]{0:T(512)(128)(4,1)S(1)} %get-tuple-element.38, ...), kind=kLoop, calls=%fused_computation.1 | loop fusion | flops 81920 | bytes 163852 | tf_op jit(solution)/shard_map/jit(_where)/select_n | solution.py:384
  8.2 1.2 %collective-permute-start.3 = (f32[4,8,128]{2,1,0:T(8,128)S(1)}, f32[4,8,128]{2,1,0:T(8,128)S(1)}, u32[]{:S(2)}, u32[]{:S(2)}) collective-permute-start(f32[4,8,128]{2,1,0:T(8,128)S(1)} %get-tuple-element.33), channel_id=1, source_target_pairs={{1,0},{2,1},{3,2},{4,3},{5,4},{6,5},{7,6},{0,7},{9,8},{10,9},{11,1... | collective-permute-start | bytes 49160 | tf_op jit(solution)/shard_map/ppermute | solution.py:390
  9.4 1.5 %collective-permute-start.2 = (f32[4,8,128]{2,1,0:T(8,128)S(1)}, f32[4,8,128]{2,1,0:T(8,128)S(1)}, u32[]{:S(2)}, u32[]{:S(2)}) collective-permute-start(f32[4,8,128]{2,1,0:T(8,128)S(1)} %get-tuple-element.34), channel_id=1, source_target_pairs={{0,1},{1,2},{2,3},{3,4},{4,5},{5,6},{6,7},{7,0},{8,9},{9,10},{10,1... | collective-permute-start | bytes 49160 | tf_op jit(solution)/shard_map/ppermute | solution.py:387
  11.0 0.1 slice_convert_fusion
  11.1 0.1 convert_element_type.16
  11.2 0.1 copy.11
  11.2 0.1 broadcast_in_dim.56.lengths
  11.3 3.0 %tables.1 = (bf16[8,256,1280]{2,1,0:T(8,128)(2,1)S(1)}, f32[8,8,1280]{2,1,0:T(8,128)S(1)}, bf16[4,5,256,256]{3,2,1,0:T(8,128)(2,1)S(1)}, f32[4,5,24,256]{3,2,1,0:T(8,128)S(1)}, f32[10,128]{1,0:T(8,128)S(1)}) custom-call(f32[8,128]{1,0:T(8,128)S(1)} %broadcast_in_dim.56.lengths, f32[20,64]{1,0:T(8,128)S(1)} %bitcast.9, f32[4,8,640]{2,1,0:T(8,128)S(1)} %select_select_fusion.stencil), custom_call_target="tpu_custom_call" | custom-call | flops 5000000000 | bytes 3000000 | tf_op jit(solution)/shard_map/tables/pallas_call | solution.py:394
  14.4 0.1 wrap_tables.1
  14.5 1.1 %interpolate_upper.1 = (bf16[4,144,128]{2,1,0:T(8,128)(2,1)S(1)}, bf16[576,640]{1,0:T(8,128)(2,1)S(1)}, bf16[576,768]{1,0:T(8,128)(2,1)S(1)}) custom-call(bf16[192,640]{1,0:T(8,128)(2,1)S(1)} %bitcast.8, bf16[192,640]{1,0:T(8,128)(2,1)S(1)} %collective-permute-done.second, bf16[192,640]{1,0:T(8,128)(2,1)S(1)} %collective-permute-done.1.first, ...), custom_call_target="tpu_custom_call" | custom-call | tf_op jit(solution)/shard_map/interpolate_upper/pallas_call | solution.py:425
  15.6 2.4 %collective-permute-start.5 = (bf16[4,144,128]{2,1,0:T(8,128)(2,1)S(1)}, bf16[4,144,128]{2,1,0:T(8,128)(2,1)S(1)}, u32[]{:S(2)}, u32[]{:S(2)}) collective-permute-start(bf16[4,144,128]{2,1,0:T(8,128)(2,1)S(1)} %get-tuple-element.32.mine), channel_id=1, source_target_pairs={{0,1},{1,0},{2,3},{3,2},{4,5},{5,4},{6,7},{7,6},{8,9},{9,8},{10,11... | collective-permute-start | bytes 442376 | tf_op jit(solution)/shard_map/ppermute | solution.py:438
  18.0 0.9 %interpolate_lower.1.mine = bf16[4,144,128]{2,1,0:T(8,128)(2,1)S(1)} custom-call(bf16[576,640]{1,0:T(8,128)(2,1)S(1)} %get-tuple-element.28.main, bf16[576,768]{1,0:T(8,128)(2,1)S(1)} %get-tuple-element.29.edge, bf16[4,5,256,256]{3,2,1,0:T(8,128)(2,1)S(1)} %get-tuple-element.24.columns, f32[4,5,24,256]{3,2,1,0:T(8,128)S(1)} %get-tuple-element.25.rows_of, ...), custom_call_target="tpu_custom_call" | custom-call | flops 5000000000 | bytes 3000000 | tf_op jit(solution)/shard_map/interpolate_lower/pallas_call | solution.py:439
  18.9 0.1 collective-permute-start.4
  19.0 0.0 collective-permute-done.5.other
  19.0 0.9 %fourier_upper.1.upper = bf16[1024,128]{1,0:T(8,128)(2,1)S(1)} custom-call(bf16[4,144,128]{2,1,0:T(8,128)(2,1)S(1)} %get-tuple-element.32.mine, bf16[4,144,128]{2,1,0:T(8,128)(2,1)S(1)} %collective-permute-done.5.other, bf16[8,256,1280]{2,1,0:T(8,128)(2,1)S(1)} %get-tuple-element.30.inner, f32[8,8,1280]{2,1,0:T(8,128)S(1)} %get-tuple-element.31.outer), custom_call_target="tpu_custom_call" | custom-call | flops 5000000000 | bytes 3000000 | tf_op jit(solution)/shard_map/fourier_upper/pallas_call | solution.py:450
  19.9 0.4 collective-permute-done.4.other
  20.4 0.9 %fourier_lower.1 = bf16[2048,128]{1,0:T(8,128)(2,1)S(1)} custom-call(bf16[4,144,128]{2,1,0:T(8,128)(2,1)S(1)} %interpolate_lower.1.mine, bf16[4,144,128]{2,1,0:T(8,128)(2,1)S(1)} %collective-permute-done.4.other, bf16[8,256,1280]{2,1,0:T(8,128)(2,1)S(1)} %get-tuple-element.30.inner, f32[8,8,1280]{2,1,0:T(8,128)S(1)} %get-tuple-element.31.outer, ...), custom_call_target="tpu_custom_call" | custom-call | tf_op jit(solution)/shard_map/fourier_lower/pallas_call | solution.py:460
  21.3 21.0 %all_to_all.5.message = bf16[64,32,128]{2,1,0:T(8,128)(2,1)S(1)} all-to-all(bf16[64,32,128]{2,1,0:T(8,128)(2,1)S(1)} %bitcast.5), channel_id=1, replica_groups={{0,2,4,6,8,10,12,14,16,18,20,22,24,26,28,30,32,34,36,38,40,42,44,46,48,..., dimensions={0} | all-to-all | bytes 1048576 | tf_op jit(solution)/shard_map/all_to_all | solution.py:469
  42.3 1.9 %legendre.1 = f32[10,48,1280]{2,1,0:T(8,128)} custom-call(f32[10,128]{1,0:T(8,128)S(1)} %get-tuple-element.22.waves, bf16[64,32,128]{2,1,0:T(8,128)(2,1)S(1)} %all_to_all.5.message, bf16[10,128,1280]{2,1,0:T(8,128)(2,1)S(1)} %copy-done), custom_call_target="tpu_custom_call" | custom-call | tf_op jit(solution)/shard_map/legendre/pallas_call | solution.py:478
  (11 shorter events, 0.1 us)
Async XLA Ops:
  1.9 12.6 %collective-permute-start.1 = (bf16[192,640]{1,0:T(8,128)(2,1)S(1)}, bf16[192,640]{1,0:T(8,128)(2,1)S(1)}, u32[]{:S(2)}, u32[]{:S(2)}) collective-permute-start(bf16[192,640]{1,0:T(8,128)(2,1)S(1)} %bitcast.6), channel_id=1, source_target_pairs={{8,16},{24,32},{40,48},{56,64},{72,80},{88,96},{104,112},{16,8},{3... | collective-permute-start | bytes 737288 | tf_op jit(solution)/shard_map/ppermute | solution.py:375
  2.6 11.9 %collective-permute-start = (bf16[192,640]{1,0:T(8,128)(2,1)S(1)}, bf16[192,640]{1,0:T(8,128)(2,1)S(1)}, u32[]{:S(2)}, u32[]{:S(2)}) collective-permute-start(bf16[192,640]{1,0:T(8,128)(2,1)S(1)} %bitcast.7), channel_id=1, source_target_pairs={{0,8},{16,24},{32,40},{48,56},{64,72},{80,88},{96,104},{112,120},{... | collective-permute-start | bytes 737288 | tf_op jit(solution)/shard_map/ppermute | solution.py:375
  8.2 6.2 %collective-permute-start.3 = (f32[4,8,128]{2,1,0:T(8,128)S(1)}, f32[4,8,128]{2,1,0:T(8,128)S(1)}, u32[]{:S(2)}, u32[]{:S(2)}) collective-permute-start(f32[4,8,128]{2,1,0:T(8,128)S(1)} %get-tuple-element.33), channel_id=1, source_target_pairs={{1,0},{2,1},{3,2},{4,3},{5,4},{6,5},{7,6},{0,7},{9,8},{10,9},{11,1... | collective-permute-start | bytes 49160 | tf_op jit(solution)/shard_map/ppermute | solution.py:390
  9.4 4.9 %collective-permute-start.2 = (f32[4,8,128]{2,1,0:T(8,128)S(1)}, f32[4,8,128]{2,1,0:T(8,128)S(1)}, u32[]{:S(2)}, u32[]{:S(2)}) collective-permute-start(f32[4,8,128]{2,1,0:T(8,128)S(1)} %get-tuple-element.34), channel_id=1, source_target_pairs={{0,1},{1,2},{2,3},{3,4},{4,5},{5,6},{6,7},{7,0},{8,9},{9,10},{10,1... | collective-permute-start | bytes 49160 | tf_op jit(solution)/shard_map/ppermute | solution.py:387
  15.6 3.4 %collective-permute-start.5 = (bf16[4,144,128]{2,1,0:T(8,128)(2,1)S(1)}, bf16[4,144,128]{2,1,0:T(8,128)(2,1)S(1)}, u32[]{:S(2)}, u32[]{:S(2)}) collective-permute-start(bf16[4,144,128]{2,1,0:T(8,128)(2,1)S(1)} %get-tuple-element.32.mine), channel_id=1, source_target_pairs={{0,1},{1,0},{2,3},{3,2},{4,5},{5,4},{6,7},{7,6},{8,9},{9,8},{10,11... | collective-permute-start | bytes 442376 | tf_op jit(solution)/shard_map/ppermute | solution.py:438
  18.9 1.5 %collective-permute-start.4 = (bf16[4,144,128]{2,1,0:T(8,128)(2,1)S(1)}, bf16[4,144,128]{2,1,0:T(8,128)(2,1)S(1)}, u32[]{:S(2)}, u32[]{:S(2)}) collective-permute-start(bf16[4,144,128]{2,1,0:T(8,128)(2,1)S(1)} %interpolate_lower.1.mine), channel_id=1, source_target_pairs={{0,1},{1,0},{2,3},{3,2},{4,5},{5,4},{6,7},{7,6},{8,9},{9,8},{10,11... | collective-permute-start | bytes 442376 | tf_op jit(solution)/shard_map/ppermute | solution.py:448
  19.9 22.4 %copy-start = (bf16[10,128,1280]{2,1,0:T(8,128)(2,1)S(1)}, bf16[10,128,1280]{2,1,0:T(8,128)(2,1)}, u32[]{:S(2)}) copy-start(bf16[10,128,1280]{2,1,0:T(8,128)(2,1)} %table.1) | copy-start | bytes 9830404

commit v9 on v8

--- a/solution.py
+++ b/solution.py
@@ -2,6 +2,7 @@
 
 import jax
 import jax.numpy as jnp
+import numpy as np
 from jax import lax
 from jax.experimental import pallas as pl
 from jax.experimental.pallas import tpu as pltpu
@@ -18,6 +19,8 @@
 BLOCKS = 5
 SLOTS = 10
 PEERS = 64
+ORDER = [int(peer) for peer in np.random.RandomState(0).permutation(PEERS)]
+STANDS = [ORDER.index(peer) for peer in range(PEERS)]
 GROUPS = 5
 ROWS = 4
 STACK = 144
@@ -179,6 +182,15 @@
     lane = lax.broadcasted_iota(jnp.int32, (SLOTS, PEERS), 1)
     mine = jnp.sum(jnp.where(lane == peer, slots, 0.0), axis=1, keepdims=True)
     own_waves[...] = jnp.broadcast_to(mine, (SLOTS, 128))
+    column = lax.broadcasted_iota(jnp.int32, (1, PEERS), 1)
+    order = jnp.zeros((1, PEERS), jnp.int32)
+    for at, peer in enumerate(ORDER):
+        order = jnp.where(column == at, peer, order)
+    chosen = (lax.broadcasted_iota(jnp.int32, (PEERS, PEERS), 0) == order).astype(F32).astype(BF16)
+    high = jnp.floor(slots * 0.125)
+    slots = 8.0 * jnp.dot(high.astype(BF16), chosen, preferred_element_type=F32) + jnp.dot(
+        (slots - 8.0 * high).astype(BF16), chosen, preferred_element_type=F32
+    )
     groups = [
         jnp.concatenate([slots[k : k + 1], slots[k + 1 : k + 2]], axis=1)
         for k in range(0, SLOTS, 2)
@@ -334,9 +346,9 @@
 
 def legendre_kernel(waves, message, table, out, flat, sorted_rows, left, result, done):
     for band in range(16):
-        total = message[4 * band].astype(F32)
+        total = message[STANDS[4 * band]].astype(F32)
         for z in range(1, 4):
-            total = total + message[4 * band + z].astype(F32)
+            total = total + message[STANDS[4 * band + z]].astype(F32)
         flat[32 * band : 32 * band + 32, :] = total
     copies = []
     for part in range(4):
@@ -472,7 +484,7 @@
         split_axis=0,
         concat_axis=0,
         tiled=True,
-        axis_index_groups=[[2 * peer + core for peer in range(PEERS)] for core in range(2)],
+        axis_index_groups=[[2 * peer + core for peer in ORDER] for core in range(2)],
     )
     degrees = legendre.shape[2]
     return pl.pallas_call(

time: 45 us -> 43 us (0.956)
  blocking collectives: 21 us -> 19.4 us
    all_to_all x1, blocking collectives: 21 us -> 19.4 us  [local(): lax.all_to_all(message.reshape(PEERS, 32, 128), ('lat', 'wave'), split_ax...]
  transfers between devices with their start and end apart: 6 -> 6, of which waited for: 1 -> 1; matrix products, arithmetic and copies ran while one was open for 3% -> 3% of each run, Pallas kernels for 11% -> 12%
where the time goes in v9:
time: 43 us; the launch traced here: 42.6 us
  blocking collectives  19.4 us (45%)
  starting transfers between devices  10.6 us (25%)
  Pallas kernels  8.92 us (21%)
  other arithmetic  2.77 us (6%)
  waiting for transfers between devices  0.45 us (1%)
    all_to_all x1, blocking collectives, local(): lax.all_to_all(message.reshape(PEERS, 32, 128), ('lat', 'wave'), split_ax...  19.4 us
    ppermute x2, starting transfers between devices, swapped(): return lax.ppermute(own, 'lat', pairs + [(j, i) for i, j in pairs])  5.41 us
    pallas_call x1, Pallas kernels, local(): pl.pallas_call(table_kernel, out_shape=(jax.ShapeDtypeStruct((BAND, 256,...  3.19 us
    ppermute x1, starting transfers between devices, local(): other_upper = lax.ppermute(upper, 'wave', cores)  2.27 us
    pallas_call x1, Pallas kernels, local(): pl.pallas_call(legendre_kernel, out_shape=jax.ShapeDtypeStruct((SLOTS, 2...  1.87 us
    ppermute x1, starting transfers between devices, local(): lax.ppermute(stencil[:, :, WIDE - 128:], 'wave', [(i, (i + 1) % ring) for...  1.55 us
    ppermute x1, starting transfers between devices, local(): lax.ppermute(stencil[:, :, :128], 'wave', [((i + 1) % ring, i) for i in r...  1.25 us
    pallas_call x1, Pallas kernels, local(): pl.pallas_call(upper_kernel, out_shape=(part, jax.ShapeDtypeStruct((COUNT...  1.09 us
  transfers between devices with their start and end apart: 6, of which 1 were waited for; matrix products, arithmetic and copies ran while one was open for 3% of the time, Pallas kernels for 12%

profile of v9, /device:TPU:1, one launch (start us, length us, event | category | flops | bytes accessed | tf_op | source)
XLA Modules:
  0.0 42.6 jit_solution(4570240735122013636)
XLA Ops:
  0.0 0.8 %pad_add_fusion = s32[1288]{0:T(1024)S(1)} fusion(s32[1280]{0:T(1024)} %param.10, s32[8]{0:T(128)} %param.9), kind=kLoop, calls=%fused_computation.3 | loop fusion | flops 1288 | bytes 10304 | tf_op jit(solution)/shard_map/concatenate | solution.py:378
  0.8 0.1 iota_compare_fusion
  0.9 1.0 %select_bitcast_fusion = bf16[8,24,640]{2,0,1:T(8,128)(2,1)S(1)} fusion(bf16[24,8,640]{2,1,0:T(8,128)(2,1)} %param.8, pred[8,640]{1,0:T(8,128)(4,1)S(1)} %iota_compare_fusion), kind=kLoop, calls=%fused_computation | loop fusion | flops 122880 | bytes 496640 | tf_op jit(solution)/shard_map/transpose | solution.py:383
  1.9 0.7 %collective-permute-start.1 = (bf16[192,640]{1,0:T(8,128)(2,1)S(1)}, bf16[192,640]{1,0:T(8,128)(2,1)S(1)}, u32[]{:S(2)}, u32[]{:S(2)}) collective-permute-start(bf16[192,640]{1,0:T(8,128)(2,1)S(1)} %bitcast.6), channel_id=1, source_target_pairs={{8,16},{24,32},{40,48},{56,64},{72,80},{88,96},{104,112},{16,8},{3... | collective-permute-start | bytes 737288 | tf_op jit(solution)/shard_map/ppermute | solution.py:387
  2.6 4.7 %collective-permute-start = (bf16[192,640]{1,0:T(8,128)(2,1)S(1)}, bf16[192,640]{1,0:T(8,128)(2,1)S(1)}, u32[]{:S(2)}, u32[]{:S(2)}) collective-permute-start(bf16[192,640]{1,0:T(8,128)(2,1)S(1)} %bitcast.7), channel_id=1, source_target_pairs={{0,8},{16,24},{32,40},{48,56},{64,72},{80,88},{96,104},{112,120},{... | collective-permute-start | bytes 737288 | tf_op jit(solution)/shard_map/ppermute | solution.py:387
  7.3 0.9 %select_select_fusion.stencil = f32[4,8,640]{2,1,0:T(8,128)S(1)} fusion(f32[8,640]{1,0:T(8,128)} %param.14, f32[8,640]{1,0:T(8,128)} %param.13, s32[8,640]{1,0:T(8,128)} %param.12, s32[8,640]{1,0:T(8,128)} %param.11, pred[4]{0:T(512)(128)(4,1)S(1)} %get-tuple-element.37, pred[4]{0:T(512)(128)(4,1)S(1)} %get-tuple-element.38, ...), kind=kLoop, calls=%fused_computation.1 | loop fusion | flops 81920 | bytes 163852 | tf_op jit(solution)/shard_map/jit(_where)/select_n | solution.py:396
  8.2 1.2 %collective-permute-start.3 = (f32[4,8,128]{2,1,0:T(8,128)S(1)}, f32[4,8,128]{2,1,0:T(8,128)S(1)}, u32[]{:S(2)}, u32[]{:S(2)}) collective-permute-start(f32[4,8,128]{2,1,0:T(8,128)S(1)} %get-tuple-element.33), channel_id=1, source_target_pairs={{1,0},{2,1},{3,2},{4,3},{5,4},{6,5},{7,6},{0,7},{9,8},{10,9},{11,1... | collective-permute-start | bytes 49160 | tf_op jit(solution)/shard_map/ppermute | solution.py:402
  9.4 1.5 %collective-permute-start.2 = (f32[4,8,128]{2,1,0:T(8,128)S(1)}, f32[4,8,128]{2,1,0:T(8,128)S(1)}, u32[]{:S(2)}, u32[]{:S(2)}) collective-permute-start(f32[4,8,128]{2,1,0:T(8,128)S(1)} %get-tuple-element.34), channel_id=1, source_target_pairs={{0,1},{1,2},{2,3},{3,4},{4,5},{5,6},{6,7},{7,0},{8,9},{9,10},{10,1... | collective-permute-start | bytes 49160 | tf_op jit(solution)/shard_map/ppermute | solution.py:399
  11.0 0.1 slice_convert_fusion
  11.1 0.1 convert_element_type.16
  11.2 0.1 copy.11
  11.2 0.1 broadcast_in_dim.56.lengths
  11.3 3.2 %tables.1 = (bf16[8,256,1280]{2,1,0:T(8,128)(2,1)S(1)}, f32[8,8,1280]{2,1,0:T(8,128)S(1)}, bf16[4,5,256,256]{3,2,1,0:T(8,128)(2,1)S(1)}, f32[4,5,24,256]{3,2,1,0:T(8,128)S(1)}, f32[10,128]{1,0:T(8,128)S(1)}) custom-call(f32[8,128]{1,0:T(8,128)S(1)} %broadcast_in_dim.56.lengths, f32[20,64]{1,0:T(8,128)S(1)} %bitcast.9, f32[4,8,640]{2,1,0:T(8,128)S(1)} %select_select_fusion.stencil), custom_call_target="tpu_custom_call" | custom-call | flops 5000000000 | bytes 3000000 | tf_op jit(solution)/shard_map/tables/pallas_call | solution.py:406
  14.5 0.1 wrap_tables.1
  14.6 1.1 %interpolate_upper.1 = (bf16[4,144,128]{2,1,0:T(8,128)(2,1)S(1)}, bf16[576,640]{1,0:T(8,128)(2,1)S(1)}, bf16[576,768]{1,0:T(8,128)(2,1)S(1)}) custom-call(bf16[192,640]{1,0:T(8,128)(2,1)S(1)} %bitcast.8, bf16[192,640]{1,0:T(8,128)(2,1)S(1)} %collective-permute-done.second, bf16[192,640]{1,0:T(8,128)(2,1)S(1)} %collective-permute-done.1.first, ...), custom_call_target="tpu_custom_call" | custom-call | tf_op jit(solution)/shard_map/interpolate_upper/pallas_call | solution.py:437
  15.7 2.3 %collective-permute-start.5 = (bf16[4,144,128]{2,1,0:T(8,128)(2,1)S(1)}, bf16[4,144,128]{2,1,0:T(8,128)(2,1)S(1)}, u32[]{:S(2)}, u32[]{:S(2)}) collective-permute-start(bf16[4,144,128]{2,1,0:T(8,128)(2,1)S(1)} %get-tuple-element.32.mine), channel_id=1, source_target_pairs={{0,1},{1,0},{2,3},{3,2},{4,5},{5,4},{6,7},{7,6},{8,9},{9,8},{10,11... | collective-permute-start | bytes 442376 | tf_op jit(solution)/shard_map/ppermute | solution.py:450
  18.0 0.9 %interpolate_lower.1.mine = bf16[4,144,128]{2,1,0:T(8,128)(2,1)S(1)} custom-call(bf16[576,640]{1,0:T(8,128)(2,1)S(1)} %get-tuple-element.28.main, bf16[576,768]{1,0:T(8,128)(2,1)S(1)} %get-tuple-element.29.edge, bf16[4,5,256,256]{3,2,1,0:T(8,128)(2,1)S(1)} %get-tuple-element.24.columns, f32[4,5,24,256]{3,2,1,0:T(8,128)S(1)} %get-tuple-element.25.rows_of, ...), custom_call_target="tpu_custom_call" | custom-call | flops 5000000000 | bytes 3000000 | tf_op jit(solution)/shard_map/interpolate_lower/pallas_call | solution.py:451
  18.9 0.1 collective-permute-start.4
  19.0 0.0 collective-permute-done.5.other
  19.0 0.9 %fourier_upper.1.upper = bf16[1024,128]{1,0:T(8,128)(2,1)S(1)} custom-call(bf16[4,144,128]{2,1,0:T(8,128)(2,1)S(1)} %get-tuple-element.32.mine, bf16[4,144,128]{2,1,0:T(8,128)(2,1)S(1)} %collective-permute-done.5.other, bf16[8,256,1280]{2,1,0:T(8,128)(2,1)S(1)} %get-tuple-element.30.inner, f32[8,8,1280]{2,1,0:T(8,128)S(1)} %get-tuple-element.31.outer), custom_call_target="tpu_custom_call" | custom-call | flops 5000000000 | bytes 3000000 | tf_op jit(solution)/shard_map/fourier_upper/pallas_call | solution.py:462
  19.9 0.4 collective-permute-done.4.other
  20.4 0.9 %fourier_lower.1 = bf16[2048,128]{1,0:T(8,128)(2,1)S(1)} custom-call(bf16[4,144,128]{2,1,0:T(8,128)(2,1)S(1)} %interpolate_lower.1.mine, bf16[4,144,128]{2,1,0:T(8,128)(2,1)S(1)} %collective-permute-done.4.other, bf16[8,256,1280]{2,1,0:T(8,128)(2,1)S(1)} %get-tuple-element.30.inner, f32[8,8,1280]{2,1,0:T(8,128)S(1)} %get-tuple-element.31.outer, ...), custom_call_target="tpu_custom_call" | custom-call | tf_op jit(solution)/shard_map/fourier_lower/pallas_call | solution.py:472
  21.3 19.4 %all_to_all.5.message = bf16[64,32,128]{2,1,0:T(8,128)(2,1)S(1)} all-to-all(bf16[64,32,128]{2,1,0:T(8,128)(2,1)S(1)} %bitcast.5), channel_id=1, replica_groups={{90,58,86,122,68,66,62,80,52,124,44,4,22,56,108,8,20,70,104,92,60,14,28..., dimensions={0} | all-to-all | bytes 1048576 | tf_op jit(solution)/shard_map/all_to_all | solution.py:481
  40.7 1.9 %legendre.1 = f32[10,48,1280]{2,1,0:T(8,128)} custom-call(f32[10,128]{1,0:T(8,128)S(1)} %get-tuple-element.22.waves, bf16[64,32,128]{2,1,0:T(8,128)(2,1)S(1)} %all_to_all.5.message, bf16[10,128,1280]{2,1,0:T(8,128)(2,1)S(1)} %copy-done), custom_call_target="tpu_custom_call" | custom-call | tf_op jit(solution)/shard_map/legendre/pallas_call | solution.py:490
  (11 shorter events, 0.1 us)
Async XLA Ops:
  1.9 12.8 %collective-permute-start.1 = (bf16[192,640]{1,0:T(8,128)(2,1)S(1)}, bf16[192,640]{1,0:T(8,128)(2,1)S(1)}, u32[]{:S(2)}, u32[]{:S(2)}) collective-permute-start(bf16[192,640]{1,0:T(8,128)(2,1)S(1)} %bitcast.6), channel_id=1, source_target_pairs={{8,16},{24,32},{40,48},{56,64},{72,80},{88,96},{104,112},{16,8},{3... | collective-permute-start | bytes 737288 | tf_op jit(solution)/shard_map/ppermute | solution.py:387
  2.6 12.1 %collective-permute-start = (bf16[192,640]{1,0:T(8,128)(2,1)S(1)}, bf16[192,640]{1,0:T(8,128)(2,1)S(1)}, u32[]{:S(2)}, u32[]{:S(2)}) collective-permute-start(bf16[192,640]{1,0:T(8,128)(2,1)S(1)} %bitcast.7), channel_id=1, source_target_pairs={{0,8},{16,24},{32,40},{48,56},{64,72},{80,88},{96,104},{112,120},{... | collective-permute-start | bytes 737288 | tf_op jit(solution)/shard_map/ppermute | solution.py:387
  8.2 6.3 %collective-permute-start.3 = (f32[4,8,128]{2,1,0:T(8,128)S(1)}, f32[4,8,128]{2,1,0:T(8,128)S(1)}, u32[]{:S(2)}, u32[]{:S(2)}) collective-permute-start(f32[4,8,128]{2,1,0:T(8,128)S(1)} %get-tuple-element.33), channel_id=1, source_target_pairs={{1,0},{2,1},{3,2},{4,3},{5,4},{6,5},{7,6},{0,7},{9,8},{10,9},{11,1... | collective-permute-start | bytes 49160 | tf_op jit(solution)/shard_map/ppermute | solution.py:402
  9.4 5.1 %collective-permute-start.2 = (f32[4,8,128]{2,1,0:T(8,128)S(1)}, f32[4,8,128]{2,1,0:T(8,128)S(1)}, u32[]{:S(2)}, u32[]{:S(2)}) collective-permute-start(f32[4,8,128]{2,1,0:T(8,128)S(1)} %get-tuple-element.34), channel_id=1, source_target_pairs={{0,1},{1,2},{2,3},{3,4},{4,5},{5,6},{6,7},{7,0},{8,9},{9,10},{10,1... | collective-permute-start | bytes 49160 | tf_op jit(solution)/shard_map/ppermute | solution.py:399
  15.7 3.3 %collective-permute-start.5 = (bf16[4,144,128]{2,1,0:T(8,128)(2,1)S(1)}, bf16[4,144,128]{2,1,0:T(8,128)(2,1)S(1)}, u32[]{:S(2)}, u32[]{:S(2)}) collective-permute-start(bf16[4,144,128]{2,1,0:T(8,128)(2,1)S(1)} %get-tuple-element.32.mine), channel_id=1, source_target_pairs={{0,1},{1,0},{2,3},{3,2},{4,5},{5,4},{6,7},{7,6},{8,9},{9,8},{10,11... | collective-permute-start | bytes 442376 | tf_op jit(solution)/shard_map/ppermute | solution.py:450
  18.9 1.5 %collective-permute-start.4 = (bf16[4,144,128]{2,1,0:T(8,128)(2,1)S(1)}, bf16[4,144,128]{2,1,0:T(8,128)(2,1)S(1)}, u32[]{:S(2)}, u32[]{:S(2)}) collective-permute-start(bf16[4,144,128]{2,1,0:T(8,128)(2,1)S(1)} %interpolate_lower.1.mine), channel_id=1, source_target_pairs={{0,1},{1,0},{2,3},{3,2},{4,5},{5,4},{6,7},{7,6},{8,9},{9,8},{10,11... | collective-permute-start | bytes 442376 | tf_op jit(solution)/shard_map/ppermute | solution.py:460
  19.9 20.8 %copy-start = (bf16[10,128,1280]{2,1,0:T(8,128)(2,1)S(1)}, bf16[10,128,1280]{2,1,0:T(8,128)(2,1)}, u32[]{:S(2)}) copy-start(bf16[10,128,1280]{2,1,0:T(8,128)(2,1)} %table.1) | copy-start | bytes 9830404

commit v10 on v9

--- a/solution.py
+++ b/solution.py
@@ -19,7 +19,7 @@
 BLOCKS = 5
 SLOTS = 10
 PEERS = 64
-ORDER = [int(peer) for peer in np.random.RandomState(0).permutation(PEERS)]
+ORDER = [int(peer) for peer in np.random.RandomState(6).permutation(PEERS)]
 STANDS = [ORDER.index(peer) for peer in range(PEERS)]
 GROUPS = 5
 ROWS = 4
@@ -257,7 +257,8 @@
             rows_of[pair, block] = row_table(points, pair, block)
         return carry
 
-    lax.fori_loop(0, BAND // 2, one_pair, 0)
+    for pair in range(BAND // 2):
+        one_pair(pair, 0)
 
 
 def wrap_kernel(lengths, from_left, from_right, wrap_columns, wrap_rows, points):

time: 43 us -> 42.9 us (level)
    all_to_all x1, blocking collectives: 19.4 us -> 19 us  [local(): lax.all_to_all(message.reshape(PEERS, 32, 128), ('lat', 'wave'), split_ax...]
where the time goes in v10:
time: 42.9 us; the launch traced here: 42.1 us
  blocking collectives  19 us (44%)
  starting transfers between devices  10.6 us (25%)
  Pallas kernels  8.89 us (21%)
  other arithmetic  2.77 us (6%)
  waiting for transfers between devices  0.45 us (1%)
    all_to_all x1, blocking collectives, local(): lax.all_to_all(message.reshape(PEERS, 32, 128), ('lat', 'wave'), split_ax...  19 us
    ppermute x2, starting transfers between devices, swapped(): return lax.ppermute(own, 'lat', pairs + [(j, i) for i, j in pairs])  5.41 us
    pallas_call x1, Pallas kernels, local(): pl.pallas_call(table_kernel, out_shape=(jax.ShapeDtypeStruct((BAND, 256,...  3.17 us
    ppermute x1, starting transfers between devices, local(): other_upper = lax.ppermute(upper, 'wave', cores)  2.3 us
    pallas_call x1, Pallas kernels, local(): pl.pallas_call(legendre_kernel, out_shape=jax.ShapeDtypeStruct((SLOTS, 2...  1.87 us
    ppermute x1, starting transfers between devices, local(): lax.ppermute(stencil[:, :, WIDE - 128:], 'wave', [(i, (i + 1) % ring) for...  1.55 us
    ppermute x1, starting transfers between devices, local(): lax.ppermute(stencil[:, :, :128], 'wave', [((i + 1) % ring, i) for i in r...  1.25 us
    pallas_call x1, Pallas kernels, local(): pl.pallas_call(upper_kernel, out_shape=(part, jax.ShapeDtypeStruct((COUNT...  1.09 us
  transfers between devices with their start and end apart: 6, of which 1 were waited for; matrix products, arithmetic and copies ran while one was open for 3% of the time, Pallas kernels for 12%

profile of v10, /device:TPU:1, one launch (start us, length us, event | category | flops | bytes accessed | tf_op | source)
XLA Modules:
  0.0 42.1 jit_solution(14788884063426091707)
XLA Ops:
  0.0 0.8 %pad_add_fusion = s32[1288]{0:T(1024)S(1)} fusion(s32[1280]{0:T(1024)} %param.10, s32[8]{0:T(128)} %param.9), kind=kLoop, calls=%fused_computation.3 | loop fusion | flops 1288 | bytes 10304 | tf_op jit(solution)/shard_map/concatenate | solution.py:379
  0.8 0.1 iota_compare_fusion
  0.9 1.0 %select_bitcast_fusion = bf16[8,24,640]{2,0,1:T(8,128)(2,1)S(1)} fusion(bf16[24,8,640]{2,1,0:T(8,128)(2,1)} %param.8, pred[8,640]{1,0:T(8,128)(4,1)S(1)} %iota_compare_fusion), kind=kLoop, calls=%fused_computation | loop fusion | flops 122880 | bytes 496640 | tf_op jit(solution)/shard_map/transpose | solution.py:384
  1.9 0.7 %collective-permute-start.1 = (bf16[192,640]{1,0:T(8,128)(2,1)S(1)}, bf16[192,640]{1,0:T(8,128)(2,1)S(1)}, u32[]{:S(2)}, u32[]{:S(2)}) collective-permute-start(bf16[192,640]{1,0:T(8,128)(2,1)S(1)} %bitcast.6), channel_id=1, source_target_pairs={{8,16},{24,32},{40,48},{56,64},{72,80},{88,96},{104,112},{16,8},{3... | collective-permute-start | bytes 737288 | tf_op jit(solution)/shard_map/ppermute | solution.py:388
  2.6 4.7 %collective-permute-start = (bf16[192,640]{1,0:T(8,128)(2,1)S(1)}, bf16[192,640]{1,0:T(8,128)(2,1)S(1)}, u32[]{:S(2)}, u32[]{:S(2)}) collective-permute-start(bf16[192,640]{1,0:T(8,128)(2,1)S(1)} %bitcast.7), channel_id=1, source_target_pairs={{0,8},{16,24},{32,40},{48,56},{64,72},{80,88},{96,104},{112,120},{... | collective-permute-start | bytes 737288 | tf_op jit(solution)/shard_map/ppermute | solution.py:388
  7.3 0.9 %select_select_fusion.stencil = f32[4,8,640]{2,1,0:T(8,128)S(1)} fusion(f32[8,640]{1,0:T(8,128)} %param.14, f32[8,640]{1,0:T(8,128)} %param.13, s32[8,640]{1,0:T(8,128)} %param.12, s32[8,640]{1,0:T(8,128)} %param.11, pred[4]{0:T(512)(128)(4,1)S(1)} %get-tuple-element.37, pred[4]{0:T(512)(128)(4,1)S(1)} %get-tuple-element.38, ...), kind=kLoop, calls=%fused_computation.1 | loop fusion | flops 81920 | bytes 163852 | tf_op jit(solution)/shard_map/jit(_where)/select_n | solution.py:397
  8.2 1.2 %collective-permute-start.3 = (f32[4,8,128]{2,1,0:T(8,128)S(1)}, f32[4,8,128]{2,1,0:T(8,128)S(1)}, u32[]{:S(2)}, u32[]{:S(2)}) collective-permute-start(f32[4,8,128]{2,1,0:T(8,128)S(1)} %get-tuple-element.33), channel_id=1, source_target_pairs={{1,0},{2,1},{3,2},{4,3},{5,4},{6,5},{7,6},{0,7},{9,8},{10,9},{11,1... | collective-permute-start | bytes 49160 | tf_op jit(solution)/shard_map/ppermute | solution.py:403
  9.4 1.5 %collective-permute-start.2 = (f32[4,8,128]{2,1,0:T(8,128)S(1)}, f32[4,8,128]{2,1,0:T(8,128)S(1)}, u32[]{:S(2)}, u32[]{:S(2)}) collective-permute-start(f32[4,8,128]{2,1,0:T(8,128)S(1)} %get-tuple-element.34), channel_id=1, source_target_pairs={{0,1},{1,2},{2,3},{3,4},{4,5},{5,6},{6,7},{7,0},{8,9},{9,10},{10,1... | collective-permute-start | bytes 49160 | tf_op jit(solution)/shard_map/ppermute | solution.py:400
  11.0 0.1 slice_convert_fusion
  11.1 0.1 convert_element_type.16
  11.2 0.1 copy.11
  11.2 0.1 broadcast_in_dim.56.lengths
  11.3 3.2 %tables.1 = (bf16[8,256,1280]{2,1,0:T(8,128)(2,1)S(1)}, f32[8,8,1280]{2,1,0:T(8,128)S(1)}, bf16[4,5,256,256]{3,2,1,0:T(8,128)(2,1)S(1)}, f32[4,5,24,256]{3,2,1,0:T(8,128)S(1)}, f32[10,128]{1,0:T(8,128)S(1)}) custom-call(f32[8,128]{1,0:T(8,128)S(1)} %broadcast_in_dim.56.lengths, f32[20,64]{1,0:T(8,128)S(1)} %bitcast.9, f32[4,8,640]{2,1,0:T(8,128)S(1)} %select_select_fusion.stencil), custom_call_target="tpu_custom_call" | custom-call | flops 5000000000 | bytes 3000000 | tf_op jit(solution)/shard_map/tables/pallas_call | solution.py:407
  14.5 0.1 wrap_tables.1
  14.6 1.1 %interpolate_upper.1 = (bf16[4,144,128]{2,1,0:T(8,128)(2,1)S(1)}, bf16[576,640]{1,0:T(8,128)(2,1)S(1)}, bf16[576,768]{1,0:T(8,128)(2,1)S(1)}) custom-call(bf16[192,640]{1,0:T(8,128)(2,1)S(1)} %bitcast.8, bf16[192,640]{1,0:T(8,128)(2,1)S(1)} %collective-permute-done.second, bf16[192,640]{1,0:T(8,128)(2,1)S(1)} %collective-permute-done.1.first, ...), custom_call_target="tpu_custom_call" | custom-call | tf_op jit(solution)/shard_map/interpolate_upper/pallas_call | solution.py:438
  15.7 2.3 %collective-permute-start.5 = (bf16[4,144,128]{2,1,0:T(8,128)(2,1)S(1)}, bf16[4,144,128]{2,1,0:T(8,128)(2,1)S(1)}, u32[]{:S(2)}, u32[]{:S(2)}) collective-permute-start(bf16[4,144,128]{2,1,0:T(8,128)(2,1)S(1)} %get-tuple-element.32.mine), channel_id=1, source_target_pairs={{0,1},{1,0},{2,3},{3,2},{4,5},{5,4},{6,7},{7,6},{8,9},{9,8},{10,11... | collective-permute-start | bytes 442376 | tf_op jit(solution)/shard_map/ppermute | solution.py:451
  18.0 0.9 %interpolate_lower.1.mine = bf16[4,144,128]{2,1,0:T(8,128)(2,1)S(1)} custom-call(bf16[576,640]{1,0:T(8,128)(2,1)S(1)} %get-tuple-element.28.main, bf16[576,768]{1,0:T(8,128)(2,1)S(1)} %get-tuple-element.29.edge, bf16[4,5,256,256]{3,2,1,0:T(8,128)(2,1)S(1)} %get-tuple-element.24.columns, f32[4,5,24,256]{3,2,1,0:T(8,128)S(1)} %get-tuple-element.25.rows_of, ...), custom_call_target="tpu_custom_call" | custom-call | flops 5000000000 | bytes 3000000 | tf_op jit(solution)/shard_map/interpolate_lower/pallas_call | solution.py:452
  18.9 0.1 collective-permute-start.4
  19.0 0.0 collective-permute-done.5.other
  19.0 0.9 %fourier_upper.1.upper = bf16[1024,128]{1,0:T(8,128)(2,1)S(1)} custom-call(bf16[4,144,128]{2,1,0:T(8,128)(2,1)S(1)} %get-tuple-element.32.mine, bf16[4,144,128]{2,1,0:T(8,128)(2,1)S(1)} %collective-permute-done.5.other, bf16[8,256,1280]{2,1,0:T(8,128)(2,1)S(1)} %get-tuple-element.30.inner, f32[8,8,1280]{2,1,0:T(8,128)S(1)} %get-tuple-element.31.outer), custom_call_target="tpu_custom_call" | custom-call | flops 5000000000 | bytes 3000000 | tf_op jit(solution)/shard_map/fourier_upper/pallas_call | solution.py:463
  19.9 0.4 collective-permute-done.4.other
  20.4 0.9 %fourier_lower.1 = bf16[2048,128]{1,0:T(8,128)(2,1)S(1)} custom-call(bf16[4,144,128]{2,1,0:T(8,128)(2,1)S(1)} %interpolate_lower.1.mine, bf16[4,144,128]{2,1,0:T(8,128)(2,1)S(1)} %collective-permute-done.4.other, bf16[8,256,1280]{2,1,0:T(8,128)(2,1)S(1)} %get-tuple-element.30.inner, f32[8,8,1280]{2,1,0:T(8,128)S(1)} %get-tuple-element.31.outer, ...), custom_call_target="tpu_custom_call" | custom-call | tf_op jit(solution)/shard_map/fourier_lower/pallas_call | solution.py:473
  21.3 19.0 %all_to_all.5.message = bf16[64,32,128]{2,1,0:T(8,128)(2,1)S(1)} all-to-all(bf16[64,32,128]{2,1,0:T(8,128)(2,1)S(1)} %bitcast.5), channel_id=1, replica_groups={{122,14,0,124,78,48,80,64,106,68,6,82,102,126,12,42,86,28,76,98,60,38,4..., dimensions={0} | all-to-all | bytes 1048576 | tf_op jit(solution)/shard_map/all_to_all | solution.py:482
  40.2 1.9 %legendre.1 = f32[10,48,1280]{2,1,0:T(8,128)} custom-call(f32[10,128]{1,0:T(8,128)S(1)} %get-tuple-element.22.waves, bf16[64,32,128]{2,1,0:T(8,128)(2,1)S(1)} %all_to_all.5.message, bf16[10,128,1280]{2,1,0:T(8,128)(2,1)S(1)} %copy-done), custom_call_target="tpu_custom_call" | custom-call | tf_op jit(solution)/shard_map/legendre/pallas_call | solution.py:491
  (11 shorter events, 0.1 us)
Async XLA Ops:
  1.9 12.7 %collective-permute-start.1 = (bf16[192,640]{1,0:T(8,128)(2,1)S(1)}, bf16[192,640]{1,0:T(8,128)(2,1)S(1)}, u32[]{:S(2)}, u32[]{:S(2)}) collective-permute-start(bf16[192,640]{1,0:T(8,128)(2,1)S(1)} %bitcast.6), channel_id=1, source_target_pairs={{8,16},{24,32},{40,48},{56,64},{72,80},{88,96},{104,112},{16,8},{3... | collective-permute-start | bytes 737288 | tf_op jit(solution)/shard_map/ppermute | solution.py:388
  2.6 12.1 %collective-permute-start = (bf16[192,640]{1,0:T(8,128)(2,1)S(1)}, bf16[192,640]{1,0:T(8,128)(2,1)S(1)}, u32[]{:S(2)}, u32[]{:S(2)}) collective-permute-start(bf16[192,640]{1,0:T(8,128)(2,1)S(1)} %bitcast.7), channel_id=1, source_target_pairs={{0,8},{16,24},{32,40},{48,56},{64,72},{80,88},{96,104},{112,120},{... | collective-permute-start | bytes 737288 | tf_op jit(solution)/shard_map/ppermute | solution.py:388
  8.2 6.3 %collective-permute-start.3 = (f32[4,8,128]{2,1,0:T(8,128)S(1)}, f32[4,8,128]{2,1,0:T(8,128)S(1)}, u32[]{:S(2)}, u32[]{:S(2)}) collective-permute-start(f32[4,8,128]{2,1,0:T(8,128)S(1)} %get-tuple-element.33), channel_id=1, source_target_pairs={{1,0},{2,1},{3,2},{4,3},{5,4},{6,5},{7,6},{0,7},{9,8},{10,9},{11,1... | collective-permute-start | bytes 49160 | tf_op jit(solution)/shard_map/ppermute | solution.py:403
  9.4 5.1 %collective-permute-start.2 = (f32[4,8,128]{2,1,0:T(8,128)S(1)}, f32[4,8,128]{2,1,0:T(8,128)S(1)}, u32[]{:S(2)}, u32[]{:S(2)}) collective-permute-start(f32[4,8,128]{2,1,0:T(8,128)S(1)} %get-tuple-element.34), channel_id=1, source_target_pairs={{0,1},{1,2},{2,3},{3,4},{4,5},{5,6},{6,7},{7,0},{8,9},{9,10},{10,1... | collective-permute-start | bytes 49160 | tf_op jit(solution)/shard_map/ppermute | solution.py:400
  15.7 3.3 %collective-permute-start.5 = (bf16[4,144,128]{2,1,0:T(8,128)(2,1)S(1)}, bf16[4,144,128]{2,1,0:T(8,128)(2,1)S(1)}, u32[]{:S(2)}, u32[]{:S(2)}) collective-permute-start(bf16[4,144,128]{2,1,0:T(8,128)(2,1)S(1)} %get-tuple-element.32.mine), channel_id=1, source_target_pairs={{0,1},{1,0},{2,3},{3,2},{4,5},{5,4},{6,7},{7,6},{8,9},{9,8},{10,11... | collective-permute-start | bytes 442376 | tf_op jit(solution)/shard_map/ppermute | solution.py:451
  18.9 1.5 %collective-permute-start.4 = (bf16[4,144,128]{2,1,0:T(8,128)(2,1)S(1)}, bf16[4,144,128]{2,1,0:T(8,128)(2,1)S(1)}, u32[]{:S(2)}, u32[]{:S(2)}) collective-permute-start(bf16[4,144,128]{2,1,0:T(8,128)(2,1)S(1)} %interpolate_lower.1.mine), channel_id=1, source_target_pairs={{0,1},{1,0},{2,3},{3,2},{4,5},{5,4},{6,7},{7,6},{8,9},{9,8},{10,11... | collective-permute-start | bytes 442376 | tf_op jit(solution)/shard_map/ppermute | solution.py:461
  19.9 20.3 %copy-start = (bf16[10,128,1280]{2,1,0:T(8,128)(2,1)S(1)}, bf16[10,128,1280]{2,1,0:T(8,128)(2,1)}, u32[]{:S(2)}) copy-start(bf16[10,128,1280]{2,1,0:T(8,128)(2,1)} %table.1) | copy-start | bytes 9830404
